TPU v7x, 32 devices: a whole 2x2x4 slice. The times are simulated.
32 devices in a mesh: member: 2 (over y), band: 4 (over z), fld: 2 (over x), sub: 2 (over core).
Axes of the slice: x: 2, y: 2, z: 4, core: 2. Of those that a mesh axis runs over, the one named last changes fastest.
Arguments:
- spectra: bfloat16 [8, 16, 3, 2, 1280], P(('member', 'band'), ('fld', 'sub')), parts along dimension 0, may hold values from -2 to 2
- legendre: bfloat16 [4, 1280, 1280], P('band'), may hold values from -0.15625 to 0.15625
- assignment: int32 [4], replicated, may hold values from 0 to 3, each once
- circle_longitudes: int32 [1280], replicated, may hold values from 12 to 5136, as said below
- coriolis: float32 [2, 1280], replicated, may hold values from -1.5 to 1.5
- weights: float32 [2, 1280], replicated, may hold values from 13 to 138
- thickness: float32 [16], P(('fld', 'sub')), may hold values from 0.5 to 5
Outputs:
- tendencies: bfloat16 [8, 16, 3, 2, 1280], P(('member', 'band'), ('fld', 'sub')), parts along dimension 0
There are 2 independent parts, one for each index of `member`. A program takes and returns all parts, laid end to end along the dimension named above; an argument that names none is the same for every part. Nothing has to cross between parts.
Inputs may be any that keep to these rules, and one draw needn't show every extreme that they name: Each value once: slot s holds the wavenumber 320 * assignment[s]. `circle_longitudes`: row h of each hemisphere (h counted from the pole) holds between 12 + 4 h and 20 + 4 h points, a multiple of four, the same in both hemispheres; row 1279 holds 5136.
All inputs are finite; a program needn't handle non-finite values.
Results may differ from a plain program's by a relative error of at most 0.0059.
Values may be sent and summed in bfloat16 or wider, within the bound.
No kernel may reach another device: no remote copies, remote signals or barrier semaphores. Data moves between devices by JAX's collectives and lax.ppermute only.
A program may use at most 128 MiB of HBM per device.

v0:
```python
import jax
import jax.numpy as jnp
from jax import lax
from jax.sharding import PartitionSpec as P

TWO_PI = 6.283185307179586


def carried_in(value, axis, join, neutral):
    count, mine = (lax.axis_size(axis), lax.axis_index(axis))
    pieces = lax.all_gather(value, axis)
    pieces = pieces[::-1]
    mine = count - 1 - mine
    subtotal = jnp.full_like(value, 0) + jnp.asarray(neutral, value.dtype)

    def hop(position, subtotal):
        longer = join(subtotal, pieces[position])
        return jnp.where(position < mine, longer, subtotal)

    return lax.fori_loop(0, count - 1, hop, subtotal)


def wave_masks(wavenumbers, coeff_count):
    row_index = jnp.arange(coeff_count, dtype=jnp.int32)
    inside = row_index[None, :] < (coeff_count - wavenumbers)[:, None]
    part_index = jnp.arange(2, dtype=jnp.int32)
    real_ok = (part_index[None, :] == 0) | (wavenumbers[:, None] > 0)
    return inside[:, None, :] & real_ok[:, :, None]


def trig_tables(wavenumbers, counts, row_bound):
    positions = jnp.arange(row_bound, dtype=jnp.int32)
    phase_index = wavenumbers[None, :, None] * positions[None, None, :] % counts[:, None, None]
    angles = TWO_PI * phase_index.astype(jnp.float32) / counts[:, None, None].astype(jnp.float32)
    inside_row = positions[None, None, :] < counts[:, None, None]
    cosine = jnp.where(inside_row, jnp.cos(angles), 0.0)
    sine_part = jnp.where(inside_row, jnp.sin(angles), 0.0)
    return jnp.stack([cosine, sine_part], axis=1).astype(jnp.bfloat16)


def inverse_factor(wavenumbers, counts):
    resolved = 2 * wavenumbers[None, :] < counts[:, None]
    gain_value = jnp.where(resolved, jnp.where(wavenumbers[None, :] == 0, 1.0, 2.0), 0.0)
    sign_pair = jnp.array([1.0, -1.0], dtype=jnp.float32)
    return gain_value[:, None, :] * sign_pair[None, :, None]


def direct_scale(wavenumbers, counts, quadrature):
    resolved = 2 * wavenumbers[None, :] < counts[:, None]
    unit_multiplier = jnp.where(resolved, 1.0, 0.0) / counts[:, None].astype(jnp.float32)
    sign_pair = jnp.array([1.0, -1.0], dtype=jnp.float32)
    return (
        quadrature[:, :, None, None]
        * sign_pair[None, None, :, None]
        * unit_multiplier[:, None, None, :]
    )


def tendency_terms(physical_samples, planetary):
    vorticity = physical_samples[:, :, :, 0]
    spreading_rate_grid = physical_samples[:, :, :, 1]
    thermal_state = physical_samples[:, :, :, 2]
    absolute = vorticity + planetary[:, :, None, None]
    return jnp.stack(
        [
            -absolute * spreading_rate_grid,
            absolute * vorticity,
            0.5 * (vorticity * vorticity + spreading_rate_grid * spreading_rate_grid),
            -thermal_state * spreading_rate_grid,
        ],
        axis=3,
    ).astype(jnp.bfloat16)


def add_terms(earlier_sum, later_sum):
    return earlier_sum + later_sum


def on_device(spectra, legendre, assignment, circle_longitudes, coriolis, weights, thickness):
    waves_dev = spectra.shape[0]
    layers_per_chip = spectra.shape[1]
    coeff_count = spectra.shape[4]
    lat_half = legendre.shape[2]
    band_count = lax.axis_size("band")
    band_place = lax.axis_index("band")
    wave_total = waves_dev * band_count
    stride_size = coeff_count // wave_total
    all_waves = stride_size * assignment
    own_waves = lax.dynamic_slice_in_dim(all_waves, band_place * waves_dev, waves_dev)
    keeper = wave_masks(own_waves, coeff_count)
    masked = jnp.where(keeper[:, None, None, :, :], spectra, jnp.zeros_like(spectra))
    parity = jnp.where(jnp.arange(coeff_count) % 2 == 0, 1.0, -1.0).astype(jnp.float32)
    flipped = masked * parity.astype(jnp.bfloat16)[None, None, None, None, :]
    stacked = jnp.stack([masked, flipped], axis=1)
    both_sides = jnp.einsum(
        "ktp,kelfrt->kelfrp", legendre, stacked, preferred_element_type=jnp.float32
    )
    north_part = both_sides[:, 0]
    austral_portion = both_sides[:, 1]
    fourier = jnp.stack([north_part, austral_portion], axis=1).astype(jnp.bfloat16)
    slot_count = lat_half // band_count
    outgoing = fourier.reshape(waves_dev, 2, layers_per_chip, 3, 2, slot_count, band_count)
    arrived = lax.all_to_all(outgoing, "band", split_axis=6, concat_axis=0, tiled=True)
    gridded = arrived.reshape(wave_total, 2, layers_per_chip, 3, 2, slot_count)
    own_counts = lax.dynamic_slice_in_dim(
        circle_longitudes.reshape(slot_count, band_count), band_place, 1, axis=1
    )[:, 0]
    own_planet = jnp.transpose(
        lax.dynamic_slice_in_dim(
            coriolis.reshape(2, slot_count, band_count), band_place, 1, axis=2
        )[:, :, 0]
    )
    own_quad = jnp.transpose(
        lax.dynamic_slice_in_dim(weights.reshape(2, slot_count, band_count), band_place, 1, axis=2)[
            :, :, 0
        ]
    )
    block_count = max(
        (divisor for divisor in range(1, min(8, slot_count) + 1) if slot_count % divisor == 0)
    )
    tile_extent = slot_count // block_count
    pieces = []
    for block_index in range(block_count):
        first_slot = block_index * tile_extent
        last_slot = first_slot + tile_extent - 1
        row_bound = 20 + 4 * (band_count * last_slot + band_count - 1)
        row_bound = -(-row_bound // 128) * 128
        counts = own_counts[first_slot : first_slot + tile_extent]
        tables = trig_tables(all_waves, counts, row_bound)
        gain_lookup = jnp.transpose(inverse_factor(all_waves, counts), (2, 1, 0)).astype(
            jnp.bfloat16
        )
        coeff_block = (
            gridded[..., first_slot : first_slot + tile_extent]
            * gain_lookup[:, None, None, None, :, :]
        )
        physical_samples = jnp.einsum(
            "kelfrj,jrkx->jelfx", coeff_block, tables, preferred_element_type=jnp.float32
        )
        tendency = tendency_terms(
            physical_samples, own_planet[first_slot : first_slot + tile_extent]
        )
        summed = jnp.einsum(
            "jelqx,jrkx->kelqrj", tendency, tables, preferred_element_type=jnp.float32
        )
        factor = jnp.transpose(
            direct_scale(all_waves, counts, own_quad[first_slot : first_slot + tile_extent]),
            (3, 1, 2, 0),
        )
        pieces.append((summed * factor[:, :, None, None, :, :]).astype(jnp.bfloat16))
    returned = jnp.concatenate(pieces, axis=5)
    outward = returned.reshape(wave_total, 2, layers_per_chip, 4, 2, slot_count, 1)
    landed = lax.all_to_all(outward, "band", split_axis=0, concat_axis=6, tiled=True)
    spectral_back = landed.reshape(waves_dev, 2, layers_per_chip, 4, 2, lat_half)
    projected = jnp.einsum(
        "ktp,kelqrp->kelqrt", legendre, spectral_back, preferred_element_type=jnp.float32
    )
    combined = projected[:, 0] + parity * projected[:, 1]
    weighted = masked[:, :, 2].astype(jnp.float32) * thickness[None, :, None, None]
    column_local = jnp.cumsum(weighted[:, ::-1], axis=1)[:, ::-1]
    below_sum = carried_in(
        jnp.sum(weighted, axis=1),
        ("fld", "sub"),
        add_terms,
        jnp.zeros((waves_dev, 2, coeff_count), jnp.float32),
    )
    column = column_local + below_sum[:, None]
    degree = own_waves[:, None] + jnp.arange(coeff_count, dtype=jnp.int32)[None, :]
    truncation_value = coeff_count - 1
    laplace = (degree * (degree + 1)).astype(jnp.float32) / float(
        truncation_value * (truncation_value + 1)
    )
    divergence_tend = combined[:, :, 1] + laplace[:, None, None, :] * (column + combined[:, :, 2])
    result = jnp.stack([combined[:, :, 0], divergence_tend, combined[:, :, 3]], axis=2)
    result = jnp.where(keeper[:, None, None, :, :], result, 0.0)
    return result.astype(jnp.bfloat16)


def solution(mesh):
    in_specs = (
        P(("member", "band"), ("fld", "sub"), None, None, None),
        P("band", None, None),
        P(),
        P(),
        P(),
        P(),
        P(("fld", "sub")),
    )
    out_specs = P(("member", "band"), ("fld", "sub"), None, None, None)
    return jax.shard_map(
        on_device, mesh=mesh, in_specs=in_specs, out_specs=out_specs, check_vma=False
    )
```

profile of v0, /device:TPU:0, one launch (start us, length us, event | category | flops | bytes accessed | tf_op | source)
XLA Modules:
  0.0 1077.8 jit_solution(9537342005354708111)
XLA Ops:
  5.4 9.5 reshape.1922
  14.9 4.4 copy.107
  19.3 6.3 all-to-all-start
  83.7 5.7 all-gather.1
  103.1 15.8 %select_convert_fusion.15 = (bf16[40,1,4,768]{3,2,1,0:T(4,128)(2,1)}, bf16[40,1,4,768]{3,2,1,0:T(4,128)(2,1)}) fusion(f32[40]{0:T(128)} %get-tuple-element.262, pred[40]{0:T(512)(128)(4,1)} %get-tuple-element.271, s32[40]{0:T(128)} %get-tuple-element.263, s32[4,768]{1,0:T(4,128)} %iota_multiply_fusion.7, pred[40,768]{1,0:T(8,128)(4,1)} %iota_compare_fusion.7), kind=kLoop, calls=%fused_computation.240 | loop fusion | flops 1720320 | bytes 534888 | tf_op jit(solution)/shard_map/convert.47
  118.9 26.6 %select_convert_fusion.13 = (bf16[40,1,4,1408]{3,2,1,0:T(4,128)(2,1)}, bf16[40,1,4,1408]{3,2,1,0:T(4,128)(2,1)}) fusion(f32[40]{0:T(128)} %get-tuple-element.251, pred[40]{0:T(512)(128)(4,1)} %get-tuple-element.270, s32[40]{0:T(128)} %get-tuple-element.250, s32[4,1408]{1,0:T(4,128)} %iota_multiply_fusion.6, pred[40,1408]{1,0:T(8,128)(4,1)} %iota_compare_fusion.6), kind=kLoop, calls=%fused_computation.226 | loop fusion | flops 3153920 | bytes 980328 | tf_op jit(solution)/shard_map/convert.41
  145.5 37.4 %select_convert_fusion.11 = (bf16[40,1,4,2048]{3,2,1,0:T(4,128)(2,1)}, bf16[40,1,4,2048]{3,2,1,0:T(4,128)(2,1)}) fusion(f32[40]{0:T(128)} %get-tuple-element.260, pred[40]{0:T(512)(128)(4,1)} %get-tuple-element.269, s32[40]{0:T(128)} %get-tuple-element.261, s32[4,2048]{1,0:T(4,128)} %iota_multiply_fusion.5, pred[40,2048]{1,0:T(8,128)(4,1)} %iota_compare_fusion.5), kind=kLoop, calls=%fused_computation.205 | loop fusion | flops 4587520 | bytes 1425768 | tf_op jit(solution)/shard_map/convert.35
  182.9 48.4 %select_convert_fusion.9 = (bf16[40,1,4,2688]{3,2,1,0:T(4,128)(2,1)}, bf16[40,1,4,2688]{3,2,1,0:T(4,128)(2,1)}) fusion(f32[40]{0:T(128)} %get-tuple-element.247, pred[40]{0:T(512)(128)(4,1)} %get-tuple-element.268, s32[40]{0:T(128)} %get-tuple-element.246, s32[4,2688]{1,0:T(4,128)S(1)} %copy-done.35, pred[40,2688]{1,0:T(8,128)(4,1)S(1)} %iota_compare_fusion.4), kind=kLoop, calls=%fused_computation.177 | loop fusion | flops 6021120 | bytes 1871208 | tf_op jit(solution)/shard_map/convert.29
  231.4 58.9 %select_convert_fusion.7 = (bf16[40,1,4,3328]{3,2,1,0:T(4,128)(2,1)}, bf16[40,1,4,3328]{3,2,1,0:T(4,128)(2,1)}) fusion(f32[40]{0:T(128)} %get-tuple-element.258, pred[40]{0:T(512)(128)(4,1)} %get-tuple-element.267, s32[40]{0:T(128)} %get-tuple-element.259, s32[4,3328]{1,0:T(4,128)S(1)} %copy-done.29, pred[40,3328]{1,0:T(8,128)(4,1)S(1)} %copy-done.19), kind=kLoop, calls=%fused_computation.152 | loop fusion | flops 7454720 | bytes 2316648 | tf_op jit(solution)/shard_map/convert.23
  290.4 68.9 %select_convert_fusion.5 = (bf16[40,1,4,3968]{3,2,1,0:T(4,128)(2,1)}, bf16[40,1,4,3968]{3,2,1,0:T(4,128)(2,1)}) fusion(f32[40]{0:T(128)S(1)} %copy-done.74, pred[40]{0:T(512)(128)(4,1)S(1)} %copy-done.75, s32[40]{0:T(128)S(1)} %copy-done.73, s32[4,3968]{1,0:T(4,128)S(1)} %copy-done.28, pred[40,3968]{1,0:T(8,128)(4,1)S(1)} %copy-done.18), kind=kLoop, calls=%fused_computation.138 | loop fusion | flops 8888320 | bytes 2762088 | tf_op jit(solution)/shard_map/convert.17
  359.4 79.9 %select_convert_fusion.3 = (bf16[40,1,4,4608]{3,2,1,0:T(4,128)(2,1)}, bf16[40,1,4,4608]{3,2,1,0:T(4,128)(2,1)}) fusion(f32[40]{0:T(128)S(1)} %copy-done.70, pred[40]{0:T(512)(128)(4,1)S(1)} %copy-done.72, s32[40]{0:T(128)S(1)} %copy-done.71, s32[4,4608]{1,0:T(4,128)S(1)} %copy-done.23, pred[40,4608]{1,0:T(8,128)(4,1)S(1)} %copy-done.17), kind=kLoop, calls=%fused_computation.117 | loop fusion | flops 10321920 | bytes 3207528 | tf_op jit(solution)/shard_map/convert.11
  439.3 91.1 %select_convert_fusion.1 = (bf16[40,1,4,5248]{3,2,1,0:T(4,128)(2,1)}, bf16[40,1,4,5248]{3,2,1,0:T(4,128)(2,1)}) fusion(f32[40]{0:T(128)S(1)} %copy-done.77, pred[40]{0:T(512)(128)(4,1)S(1)} %copy-done.78, s32[40]{0:T(128)S(1)} %copy-done.76, s32[4,5248]{1,0:T(4,128)S(1)} %copy-done.21, pred[40,5248]{1,0:T(8,128)(4,1)S(1)} %copy-done.16), kind=kLoop, calls=%fused_computation.103 | loop fusion | flops 11755520 | bytes 3652968 | tf_op jit(solution)/shard_map/convert.5
  540.7 10.2 fusion.156
  554.8 3.4 convolution_bitcast_fusion.6
  560.5 2.8 maximum_bitcast_fusion.6
  563.3 19.4 %fusion.153 = bf16[4,2,4,4,2,40]{3,0,2,1,4,5:T(4,128)(2,1)} fusion(bf16[40,2,4,4,1408,1]{4,2,3,1,0,5:T(4,128)(2,1)S(1)} %maximum_bitcast_fusion.6, f32[4,2,2,40]{0,1,2,3:T(2,128)S(1)} %copy-done.48, bf16[40,1,4,1408]{3,2,1,0:T(4,128)(2,1)S(1)} %copy-done.13, bf16[40,1,4,1408]{3,2,1,0:T(4,128)(2,1)S(1)} %copy-done.12), kind=kOutput, calls=%fused_computation.195 | convolution fusion | flops 30658560 | bytes 4528640 | tf_op jit(solution)/shard_map/jelqx,jrkx->kelqrj/dot_general | solution.py:143
  586.5 4.3 convolution_bitcast_fusion.5
  590.8 3.3 fusion.58
  594.1 4.1 maximum_bitcast_fusion.5
  598.3 25.7 %fusion.150 = bf16[4,2,4,4,2,40]{3,0,2,1,4,5:T(4,128)(2,1)} fusion(bf16[40,2,4,4,2048,1]{4,2,3,1,0,5:T(4,128)(2,1)S(1)} %maximum_bitcast_fusion.5, f32[4,2,2,40]{0,1,2,3:T(2,128)S(1)} %copy-done.47, bf16[40,1,4,2048]{3,2,1,0:T(4,128)(2,1)S(1)} %copy-done.11, bf16[40,1,4,2048]{3,2,1,0:T(4,128)(2,1)S(1)} %copy-done.10), kind=kOutput, calls=%fused_computation.194 | convolution fusion | flops 44584960 | bytes 6576640 | tf_op jit(solution)/shard_map/jelqx,jrkx->kelqrj/dot_general | solution.py:143
  627.9 5.4 convolution_bitcast_fusion.4
  633.3 3.4 fusion.35
  636.7 5.3 maximum_bitcast_fusion.4
  642.1 36.8 %fusion.145 = bf16[4,2,4,4,2,40]{3,0,2,1,4,5:T(4,128)(2,1)} fusion(bf16[40,2,4,4,2688,1]{4,2,3,1,0,5:T(4,128)(2,1)S(1)} %maximum_bitcast_fusion.4, f32[4,2,2,40]{0,1,2,3:T(2,128)S(1)} %copy-done.46, bf16[40,1,4,2688]{3,2,1,0:T(4,128)(2,1)} %get-tuple-element.173, bf16[40,1,4,2688]{3,2,1,0:T(4,128)(2,1)S(1)} %copy-done.9), kind=kOutput, calls=%fused_computation.193 | convolution fusion | flops 58511360 | bytes 8624640 | tf_op jit(solution)/shard_map/jelqx,jrkx->kelqrj/dot_general | solution.py:143
  682.8 10.8 %convolution_bitcast_fusion.3 = f32[40,2,4,3,3328]{4,2,3,1,0:T(4,128)} fusion(bf16[4,2,4,3,2,40]{0,2,4,3,1,5:T(4,128)(2,1)} %copy.133, bf16[40,1,4,3328]{3,2,1,0:T(4,128)(2,1)} %get-tuple-element.169, bf16[40,1,4,3328]{3,2,1,0:T(4,128)(2,1)} %get-tuple-element.168), kind=kOutput, calls=%fused_computation.18 | convolution fusion | flops 55377920 | bytes 14924800 | tf_op jit(solution)/shard_map/kelfrj,jrkx->jelfx/dot_general | solution.py:137
  693.6 6.9 fusion.28
  700.5 6.9 maximum_bitcast_fusion.3
  707.5 41.9 %fusion.140 = bf16[4,2,4,4,2,40]{3,0,2,1,4,5:T(4,128)(2,1)} fusion(bf16[40,2,4,4,3328,1]{4,2,3,1,0,5:T(4,128)(2,1)S(1)} %maximum_bitcast_fusion.3, f32[4,2,2,40]{0,1,2,3:T(2,128)S(1)} %copy-done.45, bf16[40,1,4,3328]{3,2,1,0:T(4,128)(2,1)S(1)} %copy-done.8, bf16[40,1,4,3328]{3,2,1,0:T(4,128)(2,1)S(1)} %copy-done.7), kind=kOutput, calls=%fused_computation.192 | convolution fusion | flops 72437760 | bytes 10672640 | tf_op jit(solution)/shard_map/jelqx,jrkx->kelqrj/dot_general | solution.py:143
  753.3 12.6 %convolution_bitcast_fusion.2 = f32[40,2,4,3,3968]{4,2,3,1,0:T(4,128)} fusion(bf16[4,2,4,3,2,40]{0,2,4,3,1,5:T(4,128)(2,1)} %copy.139, bf16[40,1,4,3968]{3,2,1,0:T(4,128)(2,1)} %get-tuple-element.167, bf16[40,1,4,3968]{3,2,1,0:T(4,128)(2,1)} %get-tuple-element.166), kind=kOutput, calls=%fused_computation.17 | convolution fusion | flops 66027520 | bytes 17792000 | tf_op jit(solution)/shard_map/kelfrj,jrkx->jelfx/dot_general | solution.py:137
  765.9 8.2 fusion.23
  774.1 8.5 maximum_bitcast_fusion.2
  782.6 51.5 %fusion.159 = bf16[4,2,4,4,2,40]{3,0,2,1,4,5:T(4,128)(2,1)} fusion(bf16[40,2,4,4,3968,1]{4,2,3,1,0,5:T(4,128)(2,1)S(1)} %maximum_bitcast_fusion.2, bf16[40,1,4,3968]{3,2,1,0:T(4,128)(2,1)S(1)} %copy-done.6, bf16[40,1,4,3968]{3,2,1,0:T(4,128)(2,1)S(1)} %copy-done.5, f32[4,2,2,40]{0,1,2,3:T(2,128)S(1)} %copy-done.44), kind=kOutput, calls=%fused_computation.197 | convolution fusion | flops 86364160 | bytes 12720640 | tf_op jit(solution)/shard_map/jelqx,jrkx->kelqrj/dot_general | solution.py:143
  834.1 2.6 copy.143
  838.0 11.3 %convolution_bitcast_fusion.1 = f32[40,2,4,3,4608]{4,2,3,1,0:T(4,128)} fusion(bf16[4,2,4,3,2,40]{0,2,4,3,1,5:T(4,128)(2,1)} %copy.145, bf16[40,1,4,4608]{3,2,1,0:T(4,128)(2,1)} %get-tuple-element.165, bf16[40,1,4,4608]{3,2,1,0:T(4,128)(2,1)} %get-tuple-element.164), kind=kOutput, calls=%fused_computation.8 | convolution fusion | flops 76677120 | bytes 20659200 | tf_op jit(solution)/shard_map/kelfrj,jrkx->jelfx/dot_general | solution.py:137
  849.3 9.7 fusion.16
  859.1 10.0 maximum_bitcast_fusion.1
  869.1 60.9 %fusion.135 = bf16[4,2,4,4,2,40]{3,0,2,1,4,5:T(4,128)(2,1)} fusion(bf16[40,2,4,4,4608,1]{4,2,3,1,0,5:T(4,128)(2,1)} %maximum_bitcast_fusion.1, bf16[40,1,4,4608]{3,2,1,0:T(4,128)(2,1)S(1)} %copy-done.4, bf16[40,1,4,4608]{3,2,1,0:T(4,128)(2,1)S(1)} %copy-done.3, f32[4,2,2,40]{0,1,2,3:T(2,128)S(1)} %copy-done.43), kind=kOutput, calls=%fused_computation.189 | convolution fusion | flops 100290560 | bytes 14768640 | tf_op jit(solution)/shard_map/jelqx,jrkx->kelqrj/dot_general | solution.py:143
  930.0 2.6 copy.149
  933.9 12.9 %convolution_bitcast_fusion = f32[40,2,4,3,5248]{4,2,3,1,0:T(4,128)} fusion(bf16[4,2,4,3,2,40]{0,2,4,3,1,5:T(4,128)(2,1)} %copy.151, bf16[40,1,4,5248]{3,2,1,0:T(4,128)(2,1)} %get-tuple-element.163, bf16[40,1,4,5248]{3,2,1,0:T(4,128)(2,1)} %get-tuple-element.162), kind=kOutput, calls=%fused_computation.4 | convolution fusion | flops 87326720 | bytes 23526400 | tf_op jit(solution)/shard_map/kelfrj,jrkx->jelfx/dot_general | solution.py:137
  946.8 9.8 fusion.11
  956.6 13.3 %maximum_bitcast_fusion = bf16[40,2,4,4,5248,1]{4,2,3,1,0,5:T(4,128)(2,1)} fusion(bf16[40,2,4,1,5248]{4,2,3,1,0:T(4,128)(2,1)S(1)} %get-tuple-element.133, bf16[40,2,4,1,5248]{4,2,3,1,0:T(4,128)(2,1)S(1)} %get-tuple-element.132, bf16[40,2,4,1,5248]{4,2,3,1,0:T(4,128)(2,1)S(1)} %get-tuple-element.131, bf16[40,2,4,1,5248]{4,2,3,1,0:T(4,128)(2,1)S(1)} %get-tuple-element.130), kind=kLoop, calls=%fused_computation.1 | loop fusion | flops 20152320 | bytes 26869760 | tf_op jit(solution)/shard_map/stack | solution.py:64
  969.9 70.2 %fusion.130 = bf16[4,2,4,4,2,40]{3,0,2,1,4,5:T(4,128)(2,1)} fusion(bf16[40,2,4,4,5248,1]{4,2,3,1,0,5:T(4,128)(2,1)} %maximum_bitcast_fusion, bf16[40,1,4,5248]{3,2,1,0:T(4,128)(2,1)S(1)} %copy-done.2, bf16[40,1,4,5248]{3,2,1,0:T(4,128)(2,1)S(1)} %copy-done.1, f32[4,2,2,40]{0,1,2,3:T(2,128)S(1)} %copy-done.42), kind=kOutput, calls=%fused_computation.188 | convolution fusion | flops 114216960 | bytes 16816640 | tf_op jit(solution)/shard_map/jelqx,jrkx->kelqrj/dot_general | solution.py:143
  1040.2 2.6 copy.155
  1045.0 5.1 all-to-all-start.1
  1052.3 3.5 rev.9
  1056.6 3.6 rev.10
  1060.7 3.7 copy.215
  1064.5 11.1 %reshape.1924 = bf16[2,4,4,2,1280]{4,1,3,2,0:T(4,128)(2,1)S(1)} reshape(bf16[1,2,4,4,2,320,4,1]{6,5,2,4,3,1,7,0:T(8,128)(2,1)} %copy.215) | data formatting | bytes 327680 | tf_op jit(solution)/shard_map/reshape.91
  (273 shorter events, 120.2 us)
Async XLA Ops:
  14.9 14.5 %copy-start.79 = (s32[4]{0:T(128)S(1)}, s32[4]{0:T(128)}, u32[]{:S(2)}) copy-start(s32[4]{0:T(128)} %param.27) | copy-start | bytes 52
  19.3 511.9 %all-to-all-start = ((bf16[1,2,4,3,2,320,4]{5,2,4,3,1,0,6:T(4,128)(2,1)}), bf16[1,2,4,3,2,320,4]{5,2,4,3,1,0,6:T(4,128)(2,1)S(1)}, u32[]{:S(2)}, u32[]{:S(2)}) async-start(bf16[1,2,4,3,2,320,4]{5,2,4,3,1,0,6:T(4,128)(2,1)} %copy.107), calls=%async_computation | async-start | bytes 294912 | tf_op jit(solution)/shard_map/all_to_all | solution.py:103
  29.4 15.5 %copy-start.52 = (s32[40]{0:T(128)}, s32[40]{0:T(128)S(1)}, u32[]{:S(2)}) copy-start(s32[40]{0:T(128)S(1)} %get-tuple-element.112) | copy-start | bytes 484
  29.4 15.5 %copy-start.53 = (s32[40]{0:T(128)}, s32[40]{0:T(128)S(1)}, u32[]{:S(2)}) copy-start(s32[40]{0:T(128)S(1)} %get-tuple-element.113) | copy-start | bytes 484
  29.5 15.5 %copy-start.54 = (s32[40]{0:T(128)}, s32[40]{0:T(128)S(1)}, u32[]{:S(2)}) copy-start(s32[40]{0:T(128)S(1)} %get-tuple-element.114) | copy-start | bytes 484
  29.5 15.5 %copy-start.55 = (s32[40]{0:T(128)}, s32[40]{0:T(128)S(1)}, u32[]{:S(2)}) copy-start(s32[40]{0:T(128)S(1)} %get-tuple-element.115) | copy-start | bytes 484
  29.5 15.5 %copy-start.56 = (s32[40]{0:T(128)}, s32[40]{0:T(128)S(1)}, u32[]{:S(2)}) copy-start(s32[40]{0:T(128)S(1)} %get-tuple-element.116) | copy-start | bytes 484
  103.1 79.8 %copy-start.35 = (s32[4,2688]{1,0:T(4,128)S(1)}, s32[4,2688]{1,0:T(4,128)}, u32[]{:S(2)}) copy-start(s32[4,2688]{1,0:T(4,128)} %iota_multiply_fusion.4) | copy-start | bytes 129028
  103.1 128.3 %copy-start.19 = (pred[40,3328]{1,0:T(8,128)(4,1)S(1)}, pred[40,3328]{1,0:T(8,128)(4,1)}, u32[]{:S(2)}) copy-start(pred[40,3328]{1,0:T(8,128)(4,1)} %iota_compare_fusion.3) | copy-start | bytes 399364
  103.1 128.3 %copy-start.29 = (s32[4,3328]{1,0:T(4,128)S(1)}, s32[4,3328]{1,0:T(4,128)}, u32[]{:S(2)}) copy-start(s32[4,3328]{1,0:T(4,128)} %iota_multiply_fusion.3) | copy-start | bytes 159748
  145.4 144.8 %copy-start.18 = (pred[40,3968]{1,0:T(8,128)(4,1)S(1)}, pred[40,3968]{1,0:T(8,128)(4,1)}, u32[]{:S(2)}) copy-start(pred[40,3968]{1,0:T(8,128)(4,1)} %iota_compare_fusion.2) | copy-start | bytes 476164
  145.4 144.9 %copy-start.28 = (s32[4,3968]{1,0:T(4,128)S(1)}, s32[4,3968]{1,0:T(4,128)}, u32[]{:S(2)}) copy-start(s32[4,3968]{1,0:T(4,128)} %iota_multiply_fusion.2) | copy-start | bytes 190468
  145.4 144.9 %copy-start.73 = (s32[40]{0:T(128)S(1)}, s32[40]{0:T(128)}, u32[]{:S(2)}) copy-start(s32[40]{0:T(128)} %get-tuple-element.242) | copy-start | bytes 484
  145.5 144.9 %copy-start.74 = (f32[40]{0:T(128)S(1)}, f32[40]{0:T(128)}, u32[]{:S(2)}) copy-start(f32[40]{0:T(128)} %get-tuple-element.243) | copy-start | bytes 484
  145.5 144.9 %copy-start.75 = (pred[40]{0:T(512)(128)(4,1)S(1)}, pred[40]{0:T(512)(128)(4,1)}, u32[]{:S(2)}) copy-start(pred[40]{0:T(512)(128)(4,1)} %get-tuple-element.266) | copy-start | bytes 124
  231.3 128.0 %copy-start.17 = (pred[40,4608]{1,0:T(8,128)(4,1)S(1)}, pred[40,4608]{1,0:T(8,128)(4,1)}, u32[]{:S(2)}) copy-start(pred[40,4608]{1,0:T(8,128)(4,1)} %iota_compare_fusion.1) | copy-start | bytes 552964
  231.3 128.0 %copy-start.23 = (s32[4,4608]{1,0:T(4,128)S(1)}, s32[4,4608]{1,0:T(4,128)}, u32[]{:S(2)}) copy-start(s32[4,4608]{1,0:T(4,128)} %iota_multiply_fusion.1) | copy-start | bytes 221188
  231.3 128.0 %copy-start.70 = (f32[40]{0:T(128)S(1)}, f32[40]{0:T(128)}, u32[]{:S(2)}) copy-start(f32[40]{0:T(128)} %get-tuple-element.256) | copy-start | bytes 484
  231.3 128.0 %copy-start.71 = (s32[40]{0:T(128)S(1)}, s32[40]{0:T(128)}, u32[]{:S(2)}) copy-start(s32[40]{0:T(128)} %get-tuple-element.257) | copy-start | bytes 484
  231.3 128.0 %copy-start.72 = (pred[40]{0:T(512)(128)(4,1)S(1)}, pred[40]{0:T(512)(128)(4,1)}, u32[]{:S(2)}) copy-start(pred[40]{0:T(512)(128)(4,1)} %get-tuple-element.265) | copy-start | bytes 124
  290.3 149.0 %copy-start.16 = (pred[40,5248]{1,0:T(8,128)(4,1)S(1)}, pred[40,5248]{1,0:T(8,128)(4,1)}, u32[]{:S(2)}) copy-start(pred[40,5248]{1,0:T(8,128)(4,1)} %iota_compare_fusion) | copy-start | bytes 629764
  290.3 149.0 %copy-start.21 = (s32[4,5248]{1,0:T(4,128)S(1)}, s32[4,5248]{1,0:T(4,128)}, u32[]{:S(2)}) copy-start(s32[4,5248]{1,0:T(4,128)} %iota_multiply_fusion) | copy-start | bytes 251908
  290.3 149.0 %copy-start.76 = (s32[40]{0:T(128)S(1)}, s32[40]{0:T(128)}, u32[]{:S(2)}) copy-start(s32[40]{0:T(128)} %get-tuple-element.230) | copy-start | bytes 484
  290.4 149.0 %copy-start.77 = (f32[40]{0:T(128)S(1)}, f32[40]{0:T(128)}, u32[]{:S(2)}) copy-start(f32[40]{0:T(128)} %get-tuple-element.231) | copy-start | bytes 484
  290.4 149.0 %copy-start.78 = (pred[40]{0:T(512)(128)(4,1)S(1)}, pred[40]{0:T(512)(128)(4,1)}, u32[]{:S(2)}) copy-start(pred[40]{0:T(512)(128)(4,1)} %get-tuple-element.264) | copy-start | bytes 124
  359.3 171.1 %copy-start.60 = (f32[4,40]{1,0:T(4,128)S(1)}, f32[4,40]{1,0:T(4,128)}, u32[]{:S(2)}) copy-start(f32[4,40]{1,0:T(4,128)} %copy.150) | copy-start | bytes 1924
  359.3 171.1 %copy-start.61 = (f32[4,40]{1,0:T(4,128)S(1)}, f32[4,40]{1,0:T(4,128)}, u32[]{:S(2)}) copy-start(f32[4,40]{1,0:T(4,128)} %copy.114) | copy-start | bytes 1924
  359.3 171.1 %copy-start.62 = (f32[4,40]{1,0:T(4,128)S(1)}, f32[4,40]{1,0:T(4,128)}, u32[]{:S(2)}) copy-start(f32[4,40]{1,0:T(4,128)} %copy.120) | copy-start | bytes 1924
  359.3 171.1 %copy-start.63 = (f32[4,40]{1,0:T(4,128)S(1)}, f32[4,40]{1,0:T(4,128)}, u32[]{:S(2)}) copy-start(f32[4,40]{1,0:T(4,128)} %copy.126) | copy-start | bytes 1924
  359.3 171.1 %copy-start.64 = (f32[4,40]{1,0:T(4,128)S(1)}, f32[4,40]{1,0:T(4,128)}, u32[]{:S(2)}) copy-start(f32[4,40]{1,0:T(4,128)} %copy.132) | copy-start | bytes 1924
  359.3 171.1 %copy-start.65 = (f32[4,40]{1,0:T(4,128)S(1)}, f32[4,40]{1,0:T(4,128)}, u32[]{:S(2)}) copy-start(f32[4,40]{1,0:T(4,128)} %copy.138) | copy-start | bytes 1924
  359.4 171.1 %copy-start.66 = (f32[4,40]{1,0:T(4,128)S(1)}, f32[4,40]{1,0:T(4,128)}, u32[]{:S(2)}) copy-start(f32[4,40]{1,0:T(4,128)} %copy.144) | copy-start | bytes 1924
  359.4 171.1 %copy-start.67 = (f32[4,40]{1,0:T(4,128)S(1)}, f32[4,40]{1,0:T(4,128)}, u32[]{:S(2)}) copy-start(f32[4,40]{1,0:T(4,128)} %copy.108) | copy-start | bytes 1924
  359.4 171.1 %copy-start.69 = (f32[2]{0:T(128)S(1)}, f32[2]{0:T(128)}, u32[]{:S(2)}) copy-start(f32[2]{0:T(128)} %constant.153.clone) | copy-start | bytes 28
  563.3 22.0 %copy-start.33 = (bf16[4,2,4,3,2,40]{5,2,4,3,1,0:T(4,128)(2,1)S(1)}, bf16[4,2,4,3,2,40]{5,2,4,3,1,0:T(4,128)(2,1)}, u32[]{:S(2)}) copy-start(bf16[4,2,4,3,2,40]{5,2,4,3,1,0:T(4,128)(2,1)} %get-tuple-element.179) | copy-start | bytes 46084
  598.3 28.3 %copy-start.32 = (bf16[4,2,4,3,2,40]{5,2,4,3,1,0:T(4,128)(2,1)S(1)}, bf16[4,2,4,3,2,40]{5,2,4,3,1,0:T(4,128)(2,1)}, u32[]{:S(2)}) copy-start(bf16[4,2,4,3,2,40]{5,2,4,3,1,0:T(4,128)(2,1)} %get-tuple-element.178) | copy-start | bytes 46084
  642.1 39.5 %copy-start.31 = (bf16[4,2,4,3,2,40]{5,2,4,3,1,0:T(4,128)(2,1)S(1)}, bf16[4,2,4,3,2,40]{5,2,4,3,1,0:T(4,128)(2,1)}, u32[]{:S(2)}) copy-start(bf16[4,2,4,3,2,40]{5,2,4,3,1,0:T(4,128)(2,1)} %get-tuple-element.177) | copy-start | bytes 46084
  869.1 63.5 %copy-start.30 = (bf16[4,2,4,3,2,40]{5,2,4,3,1,0:T(4,128)(2,1)S(1)}, bf16[4,2,4,3,2,40]{5,2,4,3,1,0:T(4,128)(2,1)}, u32[]{:S(2)}) copy-start(bf16[4,2,4,3,2,40]{5,2,4,3,1,0:T(4,128)(2,1)} %get-tuple-element.174) | copy-start | bytes 46084
  933.9 12.9 %copy-start.36 = (f32[40,2]{1,0:T(8,128)S(1)}, f32[40,2]{1,0:T(8,128)}, u32[]{:S(2)}) copy-start(f32[40,2]{1,0:T(8,128)} %copy.152) | copy-start | bytes 964
  956.6 13.3 %copy-start.1 = (bf16[40,1,4,5248]{3,2,1,0:T(4,128)(2,1)S(1)}, bf16[40,1,4,5248]{3,2,1,0:T(4,128)(2,1)}, u32[]{:S(2)}) copy-start(bf16[40,1,4,5248]{3,2,1,0:T(4,128)(2,1)} %get-tuple-element.162) | copy-start | bytes 5038084
  956.6 13.3 %copy-start.2 = (bf16[40,1,4,5248]{3,2,1,0:T(4,128)(2,1)S(1)}, bf16[40,1,4,5248]{3,2,1,0:T(4,128)(2,1)}, u32[]{:S(2)}) copy-start(bf16[40,1,4,5248]{3,2,1,0:T(4,128)(2,1)} %get-tuple-element.163) | copy-start | bytes 5038084
  956.6 13.3 %copy-start.42 = (f32[4,2,2,40]{0,1,2,3:T(2,128)S(1)}, f32[4,2,2,40]{0,1,2,3:T(2,128)}, u32[]{:S(2)}) copy-start(f32[4,2,2,40]{0,1,2,3:T(2,128)} %broadcast_multiply_fusion) | copy-start | bytes 7684
  969.9 72.9 %copy-start.24 = (bf16[4,2,4,4,2,40]{5,3,4,2,1,0:T(4,128)(2,1)S(1)}, bf16[4,2,4,4,2,40]{5,3,4,2,1,0:T(4,128)(2,1)}, u32[]{:S(2)}) copy-start(bf16[4,2,4,4,2,40]{5,3,4,2,1,0:T(4,128)(2,1)} %copy.113) | copy-start | bytes 61444
  969.9 72.9 %copy-start.25 = (bf16[4,2,4,4,2,40]{5,3,4,2,1,0:T(4,128)(2,1)S(1)}, bf16[4,2,4,4,2,40]{5,3,4,2,1,0:T(4,128)(2,1)}, u32[]{:S(2)}) copy-start(bf16[4,2,4,4,2,40]{5,3,4,2,1,0:T(4,128)(2,1)} %copy.119) | copy-start | bytes 61444
  969.9 72.9 %copy-start.26 = (bf16[4,2,4,4,2,40]{5,3,4,2,1,0:T(4,128)(2,1)S(1)}, bf16[4,2,4,4,2,40]{5,3,4,2,1,0:T(4,128)(2,1)}, u32[]{:S(2)}) copy-start(bf16[4,2,4,4,2,40]{5,3,4,2,1,0:T(4,128)(2,1)} %copy.125) | copy-start | bytes 61444
  969.9 72.9 %copy-start.27 = (bf16[4,2,4,4,2,40]{5,3,4,2,1,0:T(4,128)(2,1)S(1)}, bf16[4,2,4,4,2,40]{5,3,4,2,1,0:T(4,128)(2,1)}, u32[]{:S(2)}) copy-start(bf16[4,2,4,4,2,40]{5,3,4,2,1,0:T(4,128)(2,1)} %copy.131) | copy-start | bytes 61444
  969.9 80.2 %copy-start.20 = (f32[1,2,1280]{2,1,0:T(2,128)S(1)}, f32[1,2,1280]{2,1,0:T(2,128)}, u32[]{:S(2)}) copy-start(f32[1,2,1280]{2,1,0:T(2,128)} %custom-call) | copy-start | bytes 30724
  1045.0 15.7 %all-to-all-start.1 = ((bf16[4,2,4,4,2,320,1]{5,3,6,4,2,1,0:T(4,128)(2,1)}), bf16[4,2,4,4,2,320,1]{5,3,6,4,2,1,0:T(4,128)(2,1)S(1)}, u32[]{:S(2)}, u32[]{:S(2)}) async-start(bf16[4,2,4,4,2,320,1]{5,3,6,4,2,1,0:T(4,128)(2,1)} %bitcast.79), calls=%async_computation.1 | async-start | bytes 393216 | tf_op jit(solution)/shard_map/all_to_all | solution.py:153
  (34 other events, 202.3 us)
where the time goes:
time: 1090 us; the launch traced here: 1080 us
  other arithmetic  568 us (52%)
  matrix products  382 us (35%)
  local copies, waits for them, and re-layouts  109 us (10%)
  starting transfers between devices  11.4 us (1%)
    another operation x16, other arithmetic  472 us
    dot_general x8, matrix products, on_device(): jnp.einsum('jelqx,jrkx->kelqrj', tendency, tables, preferred_element_type...  317 us
    dot_general x8, matrix products, on_device(): jnp.einsum('kelfrj,jrkx->jelfx', coeff_block, tables, preferred_element_t...  63.2 us
    another operation x8, other arithmetic, tendency_terms(): jnp.stack([-absolute * spreading_rate_grid, absolute * vorticity, 0.5 * (...  52.4 us
  transfers between devices with their start and end apart: 2, of which 0 were waited for; matrix products, arithmetic and copies ran while one was open for 47% of the time, Pallas kernels for 0%

commit v1 on v0

v1 whole, which is shorter than its diff:
```python
import functools
import math

import jax
import jax.numpy as jnp
import numpy as np
from jax import lax
from jax.experimental import pallas as pl
from jax.experimental.pallas import tpu as pltpu
from jax.sharding import PartitionSpec as P


FIELDS = 3
TERMS = 4
LANES = 128


def round_up(value, multiple):
    return -(-value // multiple) * multiple


def inverse_kernel(chunk, info_ref, thick_ref, spectra_ref, table_ref, fourier_ref, column_ref, total_ref,
                   rows_scr, table_scr, acc_scr, sems):
    levels, coeffs = spectra_ref.shape[1], spectra_ref.shape[4]
    chunks = coeffs // chunk
    copies = [
        pltpu.make_async_copy(table_ref.at[0, pl.ds(i * chunk, chunk)], table_scr.at[i], sems.at[i])
        for i in range(chunks)
    ]
    for copy in copies:
        copy.start()
    wave = info_ref[0]
    rows = levels * FIELDS * 2
    for level in range(levels):
        for field in range(FIELDS):
            at = (level * FIELDS + field) * 2
            rows_scr[at:at + 2, :] = spectra_ref[0, level, field].astype(jnp.float32)
    coeff = lax.broadcasted_iota(jnp.int32, (rows, coeffs), 1)
    part = lax.broadcasted_iota(jnp.int32, (rows, coeffs), 0) % 2
    keep = (coeff < coeffs - wave) & ((part == 0) | (wave > 0))
    masked = jnp.where(keep, rows_scr[...], 0.0).astype(jnp.bfloat16)
    out_rows = 2 * rows
    place = lax.broadcasted_iota(jnp.int32, (out_rows, rows), 0)
    source = lax.broadcasted_iota(jnp.int32, (out_rows, rows), 1)
    chosen = (place // (2 * levels) == source % (2 * FIELDS)) & (place % levels == source // (2 * FIELDS))
    move = jnp.where(chosen, 1.0, 0.0).astype(jnp.bfloat16)
    spread = jnp.dot(move, masked, preferred_element_type=jnp.float32)
    odd = lax.broadcasted_iota(jnp.int32, (out_rows, coeffs), 1) % 2 == 1
    south = lax.broadcasted_iota(jnp.int32, (out_rows, coeffs), 0) // levels % 2 == 1
    signed = jnp.where(odd & south, -spread, spread).astype(jnp.bfloat16)
    for i in range(chunks):
        copies[i].wait()
        product = jnp.dot(signed[:, i * chunk:(i + 1) * chunk], table_scr[i], preferred_element_type=jnp.float32)
        if i == 0:
            acc_scr[...] = product
        elif i < chunks - 1:
            acc_scr[...] += product
        else:
            fourier_ref[...] = (acc_scr[...] + product).astype(jnp.bfloat16)
    level_at = lax.broadcasted_iota(jnp.int32, (2 * levels, coeffs), 0) % levels
    for r in range(2):
        at = (2 * 2 + r) * 2 * levels
        column = jnp.zeros((2 * levels, coeffs), jnp.float32)
        for level in range(levels):
            weighted = spread[at + level:at + level + 1] * thick_ref[level]
            column += jnp.where(level_at <= level, weighted, 0.0)
        column_ref[r * 2 * levels:(r + 1) * 2 * levels, :] = column
        total_ref[r:r + 1, :] = column[0:1]


def direct_kernel(waves, half, stacked, chunk, info_ref, *refs):
    slots = 1 if stacked else waves
    fourier_refs, refs = refs[:slots], refs[slots:]
    below_refs, refs = refs[:3], refs[3:]
    (synth_ref, analysis_ref, planet_ref, quad_ref, column_ref, table_ref, out_ref,
     table_scr, back_scr, sems) = refs
    levels = out_ref.shape[1]
    coeffs, lats = table_ref.shape[1], table_ref.shape[2]
    pair = 2 * levels
    chunks = coeffs // chunk
    copies = [
        pltpu.make_async_copy(table_ref.at[0, pl.ds(i * chunk, chunk)], table_scr.at[i], sems.at[i])
        for i in range(chunks)
    ]
    for copy in copies:
        copy.start()
    wave = info_ref[0]

    def lat_block(block, carry):
        lanes = pl.ds(pl.multiple_of(block * LANES, LANES), LANES)
        coefs = []
        for k in range(waves):
            fields = []
            for field in range(FIELDS):
                at = field * 2 * pair
                if stacked:
                    both = fourier_refs[0][k, at:at + 2 * pair, lanes]
                else:
                    both = fourier_refs[k][at:at + 2 * pair, lanes]
                both = both.astype(jnp.float32)
                fields.append((both[:pair], both[pair:]))
            coefs.append(fields)
        planet = planet_ref[:, lanes]
        zero = jnp.zeros((pair, LANES), jnp.float32)

        def angle(j, sums):
            even = [zero] * FIELDS
            odd = [zero] * FIELDS
            for k in range(waves):
                harmonic = info_ref[1 + k]
                cosine = synth_ref[harmonic, j, 0:1, lanes]
                sine = synth_ref[harmonic, j, 1:2, lanes]
                for field in range(FIELDS):
                    real, imag = coefs[k][field]
                    even[field] = even[field] + real * cosine
                    odd[field] = odd[field] + imag * sine
            (z_e, d_e, t_e), (z_o, d_o, t_o) = even, odd
            a_e = z_e + planet
            cosine = analysis_ref[j, 0:1, lanes]
            sine = analysis_ref[j, 1:2, lanes]
            kinds = (
                (-(a_e * d_e + z_o * d_o), -(a_e * d_o + z_o * d_e)),
                (a_e * z_e + z_o * z_o, (a_e + z_e) * z_o),
                (0.5 * (z_e * z_e + z_o * z_o + d_e * d_e + d_o * d_o), z_e * z_o + d_e * d_o),
                (-(t_e * d_e + t_o * d_o), -(t_e * d_o + t_o * d_e)),
            )
            out = []
            for q, (in_even, in_odd) in enumerate(kinds):
                out.append(sums[2 * q] + in_even * cosine)
                out.append(sums[2 * q + 1] + in_odd * sine)
            return out

        sums = [zero] * (2 * TERMS)
        if half <= 8:
            for j in range(half):
                sums = angle(j, sums)
        else:
            sums = lax.fori_loop(0, half, angle, sums)
        quad = quad_ref[:, lanes]
        for q in range(TERMS):
            both = jnp.concatenate([sums[2 * q] * quad, sums[2 * q + 1] * quad], axis=0)
            back_scr[q * 2 * pair:(q + 1) * 2 * pair, lanes] = both.astype(jnp.bfloat16)
        return carry

    lax.fori_loop(0, lats // LANES, lat_block, 0)

    back = back_scr[...]
    groups = 2 * FIELDS
    place = lax.broadcasted_iota(jnp.int32, (levels * groups, groups * pair), 0)
    source = lax.broadcasted_iota(jnp.int32, (levels * groups, groups * pair), 1)
    chosen = (place % groups == source // pair) & (place // groups == source % pair)
    move = jnp.where(chosen, 1.0, 0.0).astype(jnp.bfloat16)
    truncation = coeffs - 1
    for i in range(chunks):
        copies[i].wait()
        span = slice(i * chunk, (i + 1) * chunk)
        product = lax.dot_general(back, table_scr[i], (((1,), (1,)), ((), ())), preferred_element_type=jnp.float32)
        coeff = lax.broadcasted_iota(jnp.int32, (pair, chunk), 1) + i * chunk
        lower = lax.broadcasted_iota(jnp.int32, (pair, chunk), 0) < levels
        flip = coeff % 2 == 1
        degree = wave + coeff
        laplace = (degree * (degree + 1)).astype(jnp.float32) / float(truncation * (truncation + 1))
        inside = coeff < coeffs - wave

        def both_rows(q, r):
            at = (2 * q + r) * pair
            rows = product[at:at + pair]
            south = pltpu.roll(rows, levels, 0)
            return rows + jnp.where(flip, -south, south)

        results = []
        for field in range(FIELDS):
            for r in range(2):
                if field == 0:
                    value = both_rows(0, r)
                elif field == 1:
                    column = column_ref[r * pair:(r + 1) * pair, span]
                    for below in below_refs:
                        column = column + below[r:r + 1, span]
                    value = both_rows(1, r) + laplace * (column + both_rows(2, r))
                else:
                    value = both_rows(3, r)
                keep = inside & lower
                if r == 1:
                    keep = keep & (wave > 0)
                results.append(jnp.where(keep, value, 0.0))
        stacked_rows = jnp.concatenate(results, axis=0).astype(jnp.bfloat16)
        ordered = jnp.dot(move, stacked_rows, preferred_element_type=jnp.float32)
        for level in range(levels):
            for field in range(FIELDS):
                at = (level * FIELDS + field) * 2
                out_ref[0, level, field, :, span] = ordered[at:at + 2].astype(jnp.bfloat16)


def angle_tables(waves, spacing, counts, harmonic):
    most = 3 * (waves - 1) + 1
    half = most // 2 + 1
    tries = jnp.arange(1, most, dtype=jnp.int32)[:, None]
    fits = spacing * tries % counts[None, :] == 0
    angles = jnp.min(jnp.where(fits, tries, most), axis=0)
    which = (jnp.arange(1, most + 1, dtype=jnp.int32)[:, None] == angles[None, :]).astype(jnp.float32)
    n = np.arange(1, most + 1)[None, None, :]
    a = np.arange(waves)[:, None, None]
    j = np.arange(half)[None, :, None]
    turn = 2.0 * np.pi * (a * j % n) / n
    live = 2 * j <= n
    alone = (j == 0) | (2 * j == n)
    basis = np.stack([np.cos(turn), -np.sin(turn)], axis=2)
    share = np.where(live, np.where(alone, 1.0, 2.0), 0.0) / n
    table = np.concatenate([basis.reshape(-1, most), np.broadcast_to(share, (1, half, most)).reshape(-1, most)])
    looked = jnp.dot(jnp.asarray(table, jnp.float32), which, precision=lax.Precision.HIGHEST)
    trig = looked[:waves * half * 2].reshape(waves, half, 2, -1)
    share = looked[waves * half * 2:]
    order = jnp.arange(waves, dtype=jnp.int32)
    seen = 2 * spacing * order[:, None] < counts[None, :]
    gain = jnp.where(seen, jnp.where(order[:, None] == 0, 1.0, 2.0), 0.0)
    synthesis = trig * gain[:, None, None, :]
    own = lax.dynamic_index_in_dim(trig, harmonic, 0, False)
    own_seen = 2 * spacing * harmonic < counts
    analysis = own * jnp.where(own_seen, share, 0.0)[:, None, :]
    return half, synthesis, analysis


def on_device(spectra, legendre, assignment, circle_longitudes, coriolis, weights, thickness):
    levels, coeffs = spectra.shape[1], spectra.shape[4]
    lats = legendre.shape[2]
    waves = lax.axis_size("band")
    me = lax.axis_index("band")
    spacing = coeffs // waves
    few = waves <= 8
    if few:
        order = (me - jnp.arange(waves, dtype=jnp.int32)) % waves
    else:
        order = jnp.arange(waves, dtype=jnp.int32)
    own_harmonic = lax.dynamic_index_in_dim(assignment, me, 0, False)
    info = jnp.concatenate([(spacing * own_harmonic)[None], assignment[order]])
    pair = 2 * levels
    rows = levels * FIELDS * 2
    chunk = 256 if coeffs % 256 == 0 else LANES
    chunks = coeffs // chunk
    smem = pl.BlockSpec(memory_space=pltpu.SMEM)
    vmem = pl.BlockSpec(memory_space=pltpu.VMEM)
    hbm = pl.BlockSpec(memory_space=pl.ANY)

    fourier, column, total = pl.pallas_call(
        functools.partial(inverse_kernel, chunk),
        out_shape=(
            jax.ShapeDtypeStruct((2 * rows, lats), jnp.bfloat16),
            jax.ShapeDtypeStruct((2 * pair, coeffs), jnp.float32),
            jax.ShapeDtypeStruct((2, coeffs), jnp.float32),
        ),
        in_specs=[smem, smem, vmem, hbm],
        out_specs=(vmem, vmem, vmem),
        scratch_shapes=[
            pltpu.VMEM((rows, coeffs), jnp.float32),
            pltpu.VMEM((chunks, chunk, lats), jnp.bfloat16),
            pltpu.VMEM((2 * rows, lats), jnp.float32),
            pltpu.SemaphoreType.DMA((chunks,)),
        ],
        compiler_params=pltpu.CompilerParams(vmem_limit_bytes=24 << 20),
        name="inverse",
    )(info, thickness, spectra, legendre)

    deep = ("fld", "sub")
    places = lax.axis_size(deep)
    belows = [
        lax.ppermute(total, deep, [(i, i - k) for i in range(k, places)]) for k in range(1, places)
    ]
    if len(belows) > 3:
        belows = [belows[0], belows[1], functools.reduce(jnp.add, belows[2:])]
    while len(belows) < 3:
        belows.append(jnp.zeros_like(total))
    if few:
        fouriers = [fourier] + [
            lax.ppermute(fourier, "band", [(i, (i + k) % waves) for i in range(waves)]) for k in range(1, waves)
        ]
    else:
        fouriers = [lax.all_gather(fourier, "band")]
    half, synthesis, analysis = angle_tables(waves, spacing, circle_longitudes, own_harmonic)
    planet = jnp.repeat(coriolis, levels, axis=0)
    quad = jnp.repeat(weights, levels, axis=0)

    (tendencies,) = pl.pallas_call(
        functools.partial(direct_kernel, waves, half, not few, chunk),
        out_shape=(jax.ShapeDtypeStruct(spectra.shape, jnp.bfloat16),),
        in_specs=[smem] + [vmem] * (len(fouriers) + 3 + 5) + [hbm],
        out_specs=(vmem,),
        scratch_shapes=[
            pltpu.VMEM((chunks, chunk, lats), jnp.bfloat16),
            pltpu.VMEM((TERMS * 2 * pair, lats), jnp.bfloat16),
            pltpu.SemaphoreType.DMA((chunks,)),
        ],
        compiler_params=pltpu.CompilerParams(vmem_limit_bytes=(24 if few else 56) << 20),
        name="direct",
    )(info, *fouriers, *belows, synthesis, analysis, planet, quad, column, legendre)
    return tendencies


def solution(mesh):
    in_specs = (
        P(("member", "band"), ("fld", "sub"), None, None, None),
        P("band", None, None),
        P(),
        P(),
        P(),
        P(),
        P(("fld", "sub")),
    )
    out_specs = P(("member", "band"), ("fld", "sub"), None, None, None)
    return jax.shard_map(
        on_device, mesh=mesh, in_specs=in_specs, out_specs=out_specs, check_vma=False
    )
```

time: 1090 us -> 50.4 us (0.05)
  the two profiles are of different devices: /device:TPU:0 before, /device:TPU:3 now
where the time goes in v1:
time: 50.4 us; the launch traced here: 49.4 us
  local copies, waits for them, and re-layouts  16.9 us (34%)
  starting transfers between devices  12.1 us (24%)
  Pallas kernels  9.87 us (20%)
  other arithmetic  6.83 us (14%)
  between operations  3.42 us (7%)
    unnamed x24, local copies, waits for them, and re-layouts  8.02 us
    ppermute x3, starting transfers between devices, on_device(): lax.ppermute(total, deep, [(i, i - k) for i in range(k, places)])  7.45 us
    pallas_call x1, Pallas kernels, on_device(): pl.pallas_call(functools.partial(direct_kernel, waves, half, not few, chu...  6.53 us
    ppermute x3, starting transfers between devices, on_device(): lax.ppermute(fourier, 'band', [(i, (i + k) % waves) for i in range(waves)])  4.67 us
    pallas_call x1, Pallas kernels, on_device(): pl.pallas_call(functools.partial(inverse_kernel, chunk), out_shape=(jax.S...  3.34 us
    mul x1, other arithmetic, angle_tables(): analysis = own * jnp.where(own_seen, share, 0.0)[:, None, :]  1.49 us
    reshape x1, local copies, waits for them, and re-layouts, on_device(): planet = jnp.repeat(coriolis, levels, axis=0)  1.42 us
    reshape x1, local copies, waits for them, and re-layouts, on_device(): quad = jnp.repeat(weights, levels, axis=0)  1.4 us
  transfers between devices with their start and end apart: 6, of which 0 were waited for; matrix products, arithmetic and copies ran while one was open for 27% of the time, Pallas kernels for 0%

profile of v1, /device:TPU:3, one launch (start us, length us, event | category | flops | bytes accessed | tf_op | source)
XLA Modules:
  0.0 49.4 jit_solution(2324463743172162709)
XLA Ops:
  0.0 0.0 copy-start.11
  0.0 0.0 copy-start.10
  0.0 1.2 %dynamic_slice.8 = s32[1]{0:T(128)} dynamic-slice(s32[4]{0:T(128)} %param.10, s32[]{:T(128)S(6)} %select_n.67), dynamic_slice_sizes={1} | dynamic-slice | bytes 12 | tf_op jit(solution)/shard_map/jit(dynamic_index_in_dim)/dynamic_slice | solution.py:235
  1.3 1.3 %gather_fusion = s32[4]{0:T(128)S(1)} fusion(s32[4]{0:T(128)} %param.10, s32[1024]{0:T(1024)S(1)} %pad_clamp_fusion), kind=kCustom, calls=%fused_computation | custom fusion | bytes 48 | tf_op jit(solution)/shard_map/gather | solution.py:236
  3.2 0.1 pad_add_fusion.info_ref
  3.3 0.0 copy-start
  3.3 1.9 %copy-done = bf16[1,1280,1280]{2,1,0:T(8,128)(2,1)S(1)} copy-done((bf16[1,1280,1280]{2,1,0:T(8,128)(2,1)S(1)}, bf16[1,1280,1280]{2,1,0:T(8,128)(2,1)}, u32[]{:S(2)}) %copy-start) | copy-done | bytes 3276824
  5.2 0.8 %copy-done.7 = bf16[1,4,3,2,1280]{4,3,2,1,0:T(2,128)(2,1)S(1)} copy-done((bf16[1,4,3,2,1280]{4,3,2,1,0:T(2,128)(2,1)S(1)}, bf16[1,4,3,2,1280]{4,3,2,1,0:T(2,128)(2,1)}, u32[]{:S(2)}) %copy-start.7) | copy-done | bytes 61464
  6.1 0.7 %copy-done.8 = f32[4]{0:T(128)S(1)} copy-done((f32[4]{0:T(128)S(1)}, f32[4]{0:T(128)}, u32[]{:S(2)}) %copy-start.8) | copy-done | bytes 40
  6.7 3.3 %inverse.1 = (bf16[48,1280]{1,0:T(8,128)(2,1)}, f32[16,1280]{1,0:T(8,128)S(1)}, f32[2,1280]{1,0:T(2,128)}) custom-call(s32[5]{0:T(128)S(1)} %pad_add_fusion.info_ref, f32[4]{0:T(128)S(1)} %copy-done.8, bf16[1,4,3,2,1280]{4,3,2,1,0:T(2,128)(2,1)S(1)} %copy-done.7, bf16[1,1280,1280]{2,1,0:T(8,128)(2,1)S(1)} %copy-done), custom_call_target="tpu_custom_call" | custom-call | tf_op jit(solution)/shard_map/inverse/pallas_call | solution.py:245
  10.1 0.0 copy-start.5
  10.1 0.6 %copy-done.5 = f32[16,1280]{1,0:T(8,128)} copy-done((f32[16,1280]{1,0:T(8,128)}, f32[16,1280]{1,0:T(8,128)S(1)}, u32[]{:S(2)}) %copy-start.5) | copy-done | bytes 81944
  10.7 1.3 %collective-permute-start = (bf16[48,1280]{1,0:T(8,128)(2,1)}, bf16[48,1280]{1,0:T(8,128)(2,1)}, u32[]{:S(2)}, u32[]{:S(2)}) collective-permute-start(bf16[48,1280]{1,0:T(8,128)(2,1)} %get-tuple-element.8.refs_0_), channel_id=1, source_target_pairs={{0,4},{4,8},{8,12},{12,0},{1,5},{5,9},{9,13},{13,1},{2,6},{6,10},{... | collective-permute-start | bytes 368648 | tf_op jit(solution)/shard_map/ppermute | solution.py:275
  12.0 2.3 %collective-permute-start.1 = (bf16[48,1280]{1,0:T(8,128)(2,1)}, bf16[48,1280]{1,0:T(8,128)(2,1)}, u32[]{:S(2)}, u32[]{:S(2)}) collective-permute-start(bf16[48,1280]{1,0:T(8,128)(2,1)} %get-tuple-element.8.refs_0_), channel_id=1, source_target_pairs={{0,8},{4,12},{8,0},{12,4},{1,9},{5,13},{9,1},{13,5},{2,10},{6,14},... | collective-permute-start | bytes 368648 | tf_op jit(solution)/shard_map/ppermute | solution.py:275
  14.3 1.1 %collective-permute-start.2 = (bf16[48,1280]{1,0:T(8,128)(2,1)}, bf16[48,1280]{1,0:T(8,128)(2,1)}, u32[]{:S(2)}, u32[]{:S(2)}) collective-permute-start(bf16[48,1280]{1,0:T(8,128)(2,1)} %get-tuple-element.8.refs_0_), channel_id=1, source_target_pairs={{0,12},{4,0},{8,4},{12,8},{1,13},{5,1},{9,5},{13,9},{2,14},{6,2},{... | collective-permute-start | bytes 368648 | tf_op jit(solution)/shard_map/ppermute | solution.py:275
  15.4 3.4 %collective-permute-start.3 = (f32[2,1280]{1,0:T(2,128)}, f32[2,1280]{1,0:T(2,128)S(1)}, u32[]{:S(2)}, u32[]{:S(2)}) collective-permute-start(f32[2,1280]{1,0:T(2,128)} %get-tuple-element.9), channel_id=1, source_target_pairs={{1,0},{2,1},{3,2},{5,4},{6,5},{7,6},{9,8},{10,9},{11,10},{13,12},{... | collective-permute-start | bytes 30728 | tf_op jit(solution)/shard_map/ppermute | solution.py:267
  18.8 2.2 %collective-permute-start.4 = (f32[2,1280]{1,0:T(2,128)}, f32[2,1280]{1,0:T(2,128)S(1)}, u32[]{:S(2)}, u32[]{:S(2)}) collective-permute-start(f32[2,1280]{1,0:T(2,128)} %get-tuple-element.9), channel_id=1, source_target_pairs={{2,0},{3,1},{6,4},{7,5},{10,8},{11,9},{14,12},{15,13},{18,16},{19,... | collective-permute-start | bytes 30728 | tf_op jit(solution)/shard_map/ppermute | solution.py:267
  21.0 0.6 %compare_select_fusion.5 = f32[4]{0:T(128)} fusion(), kind=kLoop, calls=%fused_computation.24 | loop fusion | flops 8 | bytes 16 | tf_op jit(solution)/shard_map/jit(_where)/select_n | solution.py:216
  21.6 0.5 %iota_multiply_fusion = s32[4]{0:T(128)} fusion(), kind=kLoop, calls=%fused_computation.29 | loop fusion | flops 4 | bytes 16 | tf_op jit(solution)/shard_map/mul | solution.py:215
  22.7 0.0 copy-done.10
  22.8 0.9 %select_reduce_fusion = s32[1280]{0:T(1024)S(1)} fusion(s32[9]{0:T(128)S(1)} %get-tuple-element.13, s32[1280]{0:T(1024)S(1)} %compare_select_fusion, s32[9]{0:T(128)S(1)} %get-tuple-element.14, pred[1280]{0:T(1024)(128)(4,1)S(1)} %get-tuple-element.12), kind=kLoop, calls=%fused_computation.7 | loop fusion | flops 113920 | bytes 11592 | tf_op jit(solution)/shard_map/reduce_min | solution.py:200
  23.7 0.0 copy-done.11
  23.7 0.3 fusion.3
  24.0 0.0 copy-start.9
  24.0 0.7 %copy-done.9 = f32[54,1280]{1,0:T(8,128)} copy-done((f32[54,1280]{1,0:T(8,128)}, f32[54,1280]{1,0:T(8,128)S(1)}, u32[]{:S(2)}) %copy-start.9) | copy-done | bytes 276504
  24.8 0.8 %reshape.124 = f32[4,6,2,1280]{3,2,1,0:T(2,128)} reshape(f32[48,1280]{1,0:T(8,128)S(1)} %slice.10) | data formatting | bytes 491520 | tf_op jit(solution)/shard_map/reshape | solution.py:212
  25.6 0.8 %compare_select_fusion.1 = f32[4,1280]{1,0:T(4,128)S(1)} fusion(f32[4]{0:T(128)} %compare_select_fusion.5, s32[1280]{0:T(1024)} %param.11, s32[4]{0:T(128)} %iota_multiply_fusion), kind=kLoop, calls=%fused_computation.17 | loop fusion | flops 10240 | bytes 25632 | tf_op jit(solution)/shard_map/jit(_where)/select_n | solution.py:216
  26.4 1.0 %broadcast_multiply_fusion.refs_7_ = f32[4,6,2,1280]{3,2,1,0:T(2,128)S(1)} fusion(f32[4,6,2,1280]{3,2,1,0:T(2,128)} %reshape.124, f32[4,1280]{1,0:T(4,128)S(1)} %compare_select_fusion.1), kind=kLoop, calls=%fused_computation.5 | loop fusion | flops 61440 | bytes 512000 | tf_op jit(solution)/shard_map/mul | solution.py:217
  27.4 1.4 %slice_select_fusion = f32[6,1280]{1,0:T(8,128)} fusion(f32[54,1280]{1,0:T(8,128)} %copy-done.9, pred[1280]{0:T(1024)(128)(4,1)S(1)} %get-tuple-element.11), kind=kLoop, calls=%fused_computation.13 | loop fusion | flops 7680 | bytes 62720 | tf_op jit(solution)/shard_map/jit(_where)/select_n | solution.py:220
  30.7 0.0 collective-permute-done.3.refs_4_
  30.7 1.9 %collective-permute-start.5 = (f32[2,1280]{1,0:T(2,128)}, f32[2,1280]{1,0:T(2,128)}, u32[]{:S(2)}, u32[]{:S(2)}) collective-permute-start(f32[2,1280]{1,0:T(2,128)} %get-tuple-element.9), channel_id=1, source_target_pairs={{3,0},{7,4},{11,8},{15,12},{19,16},{23,20},{27,24},{31,28}} | collective-permute-start | bytes 30728 | tf_op jit(solution)/shard_map/ppermute | solution.py:267
  32.6 1.5 %bitcast_multiply_fusion.refs_8_ = f32[6,2,1280]{2,1,0:T(2,128)} fusion(f32[4,6,2,1280]{3,2,1,0:T(2,128)} %reshape.124, s32[]{:T(128)S(6)} %select_n.75, f32[6,1280]{1,0:T(8,128)} %slice_select_fusion), kind=kLoop, calls=%fused_computation.12 | loop fusion | flops 15360 | bytes 153604 | tf_op jit(solution)/shard_map/mul | solution.py:220
  34.1 1.3 %broadcast_in_dim.73 = f32[2,4,1280]{2,1,0:T(4,128)} broadcast(f32[2,1280]{1,0:T(2,128)} %param.12), dimensions={0,2} | broadcast | bytes 51200 | tf_op jit(solution)/shard_map/broadcast_in_dim | solution.py:280
  35.4 1.4 %reshape.125.refs_9_ = f32[8,1280]{1,0:T(8,128)} reshape(f32[2,4,1280]{2,1,0:T(4,128)} %broadcast_in_dim.73) | data formatting | bytes 81920 | tf_op jit(solution)/shard_map/reshape | solution.py:280
  36.9 1.3 %broadcast_in_dim.74 = f32[2,4,1280]{2,1,0:T(4,128)} broadcast(f32[2,1280]{1,0:T(2,128)} %param.13), dimensions={0,2} | broadcast | bytes 51200 | tf_op jit(solution)/shard_map/broadcast_in_dim | solution.py:281
  38.2 1.4 %reshape.126.refs_10_ = f32[8,1280]{1,0:T(8,128)} reshape(f32[2,4,1280]{2,1,0:T(4,128)} %broadcast_in_dim.74) | data formatting | bytes 81920 | tf_op jit(solution)/shard_map/reshape | solution.py:281
  39.6 0.0 collective-permute-done.4.refs_5_
  39.6 0.0 collective-permute-done.5.refs_6_
  39.6 0.0 collective-permute-done.refs_1_
  39.6 0.0 collective-permute-done.1.refs_2_
  39.6 0.0 collective-permute-done.2.refs_3_
  39.6 0.0 copy-done.1
  39.6 0.0 copy-start.2
  39.6 0.8 %copy-done.2 = f32[6,2,1280]{2,1,0:T(2,128)S(1)} copy-done((f32[6,2,1280]{2,1,0:T(2,128)S(1)}, f32[6,2,1280]{2,1,0:T(2,128)}, u32[]{:S(2)}) %copy-start.2) | copy-done | bytes 61464
  40.5 0.8 %copy-done.3 = f32[8,1280]{1,0:T(8,128)S(1)} copy-done((f32[8,1280]{1,0:T(8,128)S(1)}, f32[8,1280]{1,0:T(8,128)}, u32[]{:S(2)}) %copy-start.3) | copy-done | bytes 40984
  41.2 0.8 %copy-done.4 = f32[8,1280]{1,0:T(8,128)S(1)} copy-done((f32[8,1280]{1,0:T(8,128)S(1)}, f32[8,1280]{1,0:T(8,128)}, u32[]{:S(2)}) %copy-start.4) | copy-done | bytes 40984
  42.0 0.9 %copy-done.6 = f32[16,1280]{1,0:T(8,128)S(1)} copy-done((f32[16,1280]{1,0:T(8,128)S(1)}, f32[16,1280]{1,0:T(8,128)}, u32[]{:S(2)}) %copy-start.6) | copy-done | bytes 81944
  42.9 6.5 %direct.1 = bf16[1,4,3,2,1280]{4,3,2,1,0:T(2,128)(2,1)} custom-call(s32[5]{0:T(128)S(1)} %pad_add_fusion.info_ref, bf16[48,1280]{1,0:T(8,128)(2,1)} %get-tuple-element.8.refs_0_, bf16[48,1280]{1,0:T(8,128)(2,1)} %collective-permute-done.refs_1_, bf16[48,1280]{1,0:T(8,128)(2,1)} %collective-permute-done.1.refs_2_, ...), custom_call_target="tpu_custom_call" | custom-call | tf_op jit(solution)/shard_map/direct/pallas_call | solution.py:283
  (13 shorter events, 0.1 us)
Async XLA Ops:
  0.0 23.7 %copy-start.11 = (f32[54,10]{1,0:T(8,128)S(1)}, f32[54,10]{1,0:T(8,128)}, u32[]{:S(2)}) copy-start(f32[54,10]{1,0:T(8,128)} %constant.59.clone) | copy-start | bytes 6484
  0.0 22.7 %copy-start.10 = (s32[1280]{0:T(1024)S(1)}, s32[1280]{0:T(1024)}, u32[]{:S(2)}) copy-start(s32[1280]{0:T(1024)} %param.11) | copy-start | bytes 15364
  3.3 1.9 %copy-start = (bf16[1,1280,1280]{2,1,0:T(8,128)(2,1)S(1)}, bf16[1,1280,1280]{2,1,0:T(8,128)(2,1)}, u32[]{:S(2)}) copy-start(bf16[1,1280,1280]{2,1,0:T(8,128)(2,1)} %refs_12_.1) | copy-start | bytes 9830404
  5.2 0.8 %copy-start.7 = (bf16[1,4,3,2,1280]{4,3,2,1,0:T(2,128)(2,1)S(1)}, bf16[1,4,3,2,1280]{4,3,2,1,0:T(2,128)(2,1)}, u32[]{:S(2)}) copy-start(bf16[1,4,3,2,1280]{4,3,2,1,0:T(2,128)(2,1)} %spectra_ref.1) | copy-start | bytes 184324
  6.1 0.7 %copy-start.8 = (f32[4]{0:T(128)S(1)}, f32[4]{0:T(128)}, u32[]{:S(2)}) copy-start(f32[4]{0:T(128)} %thick_ref.1) | copy-start | bytes 52
  6.7 32.9 %copy-start.1 = (bf16[1,1280,1280]{2,1,0:T(8,128)(2,1)S(1)}, bf16[1,1280,1280]{2,1,0:T(8,128)(2,1)}, u32[]{:S(2)}) copy-start(bf16[1,1280,1280]{2,1,0:T(8,128)(2,1)} %refs_12_.1) | copy-start | bytes 9830404
  10.1 0.6 %copy-start.5 = (f32[16,1280]{1,0:T(8,128)}, f32[16,1280]{1,0:T(8,128)S(1)}, u32[]{:S(2)}) copy-start(f32[16,1280]{1,0:T(8,128)S(1)} %get-tuple-element.10.refs_11_) | copy-start | bytes 245764
  10.7 28.9 %collective-permute-start = (bf16[48,1280]{1,0:T(8,128)(2,1)}, bf16[48,1280]{1,0:T(8,128)(2,1)}, u32[]{:S(2)}, u32[]{:S(2)}) collective-permute-start(bf16[48,1280]{1,0:T(8,128)(2,1)} %get-tuple-element.8.refs_0_), channel_id=1, source_target_pairs={{0,4},{4,8},{8,12},{12,0},{1,5},{5,9},{9,13},{13,1},{2,6},{6,10},{... | collective-permute-start | bytes 368648 | tf_op jit(solution)/shard_map/ppermute | solution.py:275
  12.0 27.6 %collective-permute-start.1 = (bf16[48,1280]{1,0:T(8,128)(2,1)}, bf16[48,1280]{1,0:T(8,128)(2,1)}, u32[]{:S(2)}, u32[]{:S(2)}) collective-permute-start(bf16[48,1280]{1,0:T(8,128)(2,1)} %get-tuple-element.8.refs_0_), channel_id=1, source_target_pairs={{0,8},{4,12},{8,0},{12,4},{1,9},{5,13},{9,1},{13,5},{2,10},{6,14},... | collective-permute-start | bytes 368648 | tf_op jit(solution)/shard_map/ppermute | solution.py:275
  14.3 25.3 %collective-permute-start.2 = (bf16[48,1280]{1,0:T(8,128)(2,1)}, bf16[48,1280]{1,0:T(8,128)(2,1)}, u32[]{:S(2)}, u32[]{:S(2)}) collective-permute-start(bf16[48,1280]{1,0:T(8,128)(2,1)} %get-tuple-element.8.refs_0_), channel_id=1, source_target_pairs={{0,12},{4,0},{8,4},{12,8},{1,13},{5,1},{9,5},{13,9},{2,14},{6,2},{... | collective-permute-start | bytes 368648 | tf_op jit(solution)/shard_map/ppermute | solution.py:275
  15.4 15.4 %collective-permute-start.3 = (f32[2,1280]{1,0:T(2,128)}, f32[2,1280]{1,0:T(2,128)S(1)}, u32[]{:S(2)}, u32[]{:S(2)}) collective-permute-start(f32[2,1280]{1,0:T(2,128)} %get-tuple-element.9), channel_id=1, source_target_pairs={{1,0},{2,1},{3,2},{5,4},{6,5},{7,6},{9,8},{10,9},{11,10},{13,12},{... | collective-permute-start | bytes 30728 | tf_op jit(solution)/shard_map/ppermute | solution.py:267
  18.8 20.8 %collective-permute-start.4 = (f32[2,1280]{1,0:T(2,128)}, f32[2,1280]{1,0:T(2,128)S(1)}, u32[]{:S(2)}, u32[]{:S(2)}) collective-permute-start(f32[2,1280]{1,0:T(2,128)} %get-tuple-element.9), channel_id=1, source_target_pairs={{2,0},{3,1},{6,4},{7,5},{10,8},{11,9},{14,12},{15,13},{18,16},{19,... | collective-permute-start | bytes 30728 | tf_op jit(solution)/shard_map/ppermute | solution.py:267
  24.0 0.7 %copy-start.9 = (f32[54,1280]{1,0:T(8,128)}, f32[54,1280]{1,0:T(8,128)S(1)}, u32[]{:S(2)}) copy-start(f32[54,1280]{1,0:T(8,128)S(1)} %fusion.3) | copy-start | bytes 829444
  30.7 8.8 %collective-permute-start.5 = (f32[2,1280]{1,0:T(2,128)}, f32[2,1280]{1,0:T(2,128)}, u32[]{:S(2)}, u32[]{:S(2)}) collective-permute-start(f32[2,1280]{1,0:T(2,128)} %get-tuple-element.9), channel_id=1, source_target_pairs={{3,0},{7,4},{11,8},{15,12},{19,16},{23,20},{27,24},{31,28}} | collective-permute-start | bytes 30728 | tf_op jit(solution)/shard_map/ppermute | solution.py:267
  39.6 0.8 %copy-start.2 = (f32[6,2,1280]{2,1,0:T(2,128)S(1)}, f32[6,2,1280]{2,1,0:T(2,128)}, u32[]{:S(2)}) copy-start(f32[6,2,1280]{2,1,0:T(2,128)} %bitcast_multiply_fusion.refs_8_) | copy-start | bytes 184324
  40.5 0.8 %copy-start.3 = (f32[8,1280]{1,0:T(8,128)S(1)}, f32[8,1280]{1,0:T(8,128)}, u32[]{:S(2)}) copy-start(f32[8,1280]{1,0:T(8,128)} %reshape.125.refs_9_) | copy-start | bytes 122884
  41.2 0.8 %copy-start.4 = (f32[8,1280]{1,0:T(8,128)S(1)}, f32[8,1280]{1,0:T(8,128)}, u32[]{:S(2)}) copy-start(f32[8,1280]{1,0:T(8,128)} %reshape.126.refs_10_) | copy-start | bytes 122884
  42.0 0.9 %copy-start.6 = (f32[16,1280]{1,0:T(8,128)S(1)}, f32[16,1280]{1,0:T(8,128)}, u32[]{:S(2)}) copy-start(f32[16,1280]{1,0:T(8,128)} %copy-done.5) | copy-start | bytes 245764

commit v2 on v1

v2 whole, which is shorter than its diff:
```python
import functools
import math

import jax
import jax.numpy as jnp
from jax import lax
from jax.experimental import pallas as pl
from jax.experimental.pallas import tpu as pltpu
from jax.sharding import PartitionSpec as P


FIELDS = 3
TERMS = 4
LANES = 128
SUBLANES = 8


def round_up(value, multiple):
    return -(-value // multiple) * multiple


def slot_order(waves, few, slot):
    if not few:
        return slot
    return lax.rem(lax.axis_index("band") + waves - slot, waves)


def inverse_kernel(spacing, chunk, assign_ref, spectra_ref, table_ref, fourier_ref,
                   spectra_scr, rows_scr, table_scr, acc_scr, sem, sems):
    levels, coeffs = spectra_ref.shape[1], spectra_ref.shape[4]
    chunks = coeffs // chunk
    first = pltpu.make_async_copy(spectra_ref, spectra_scr, sem)
    first.start()
    copies = [
        pltpu.make_async_copy(table_ref.at[0, pl.ds(i * chunk, chunk)], table_scr.at[i], sems.at[i])
        for i in range(chunks)
    ]
    for copy in copies:
        copy.start()
    wave = spacing * assign_ref[lax.axis_index("band")]
    rows = levels * FIELDS * 2
    first.wait()
    for level in range(levels):
        for field in range(FIELDS):
            at = (level * FIELDS + field) * 2
            rows_scr[at:at + 2, :] = spectra_scr[0, level, field].astype(jnp.float32)
    coeff = lax.broadcasted_iota(jnp.int32, (rows, coeffs), 1)
    part = lax.broadcasted_iota(jnp.int32, (rows, coeffs), 0) % 2
    keep = (coeff < coeffs - wave) & ((part == 0) | (wave > 0))
    masked = jnp.where(keep, rows_scr[...], 0.0).astype(jnp.bfloat16)
    out_rows = 2 * rows
    place = lax.broadcasted_iota(jnp.int32, (out_rows, rows), 0)
    source = lax.broadcasted_iota(jnp.int32, (out_rows, rows), 1)
    chosen = (place // (2 * levels) == source % (2 * FIELDS)) & (place % levels == source // (2 * FIELDS))
    move = jnp.where(chosen, 1.0, 0.0).astype(jnp.bfloat16)
    spread = jnp.dot(move, masked, preferred_element_type=jnp.float32)
    odd = lax.broadcasted_iota(jnp.int32, (out_rows, coeffs), 1) % 2 == 1
    south = lax.broadcasted_iota(jnp.int32, (out_rows, coeffs), 0) // levels % 2 == 1
    signed = jnp.where(odd & south, -spread, spread).astype(jnp.bfloat16)
    for i in range(chunks):
        copies[i].wait()
        product = jnp.dot(signed[:, i * chunk:(i + 1) * chunk], table_scr[i], preferred_element_type=jnp.float32)
        if i == 0:
            acc_scr[...] = product
        elif i < chunks - 1:
            acc_scr[...] += product
        else:
            fourier_ref[...] = (acc_scr[...] + product).astype(jnp.bfloat16)


def cos_sin(turns):
    angle = turns * (2.0 * math.pi)
    square = angle * angle
    cosine = jnp.full_like(angle, 1.0 / math.factorial(18) * -1.0)
    sine = jnp.full_like(angle, 1.0 / math.factorial(17))
    for n in range(8, -1, -1):
        cosine = cosine * square + (-1.0) ** n / math.factorial(2 * n)
        if n < 8:
            sine = sine * square + (-1.0) ** n / math.factorial(2 * n + 1)
    return cosine, sine * angle


def aux_layout(waves, levels):
    half = (3 * (waves - 1) + 1) // 2 + 1
    angles = round_up(half, SUBLANES)
    pair = 2 * levels
    sizes = (("cosine", waves * angles), ("sine", waves * angles), ("own_cosine", angles), ("own_sine", angles),
             ("planet", pair), ("quad", pair), ("column", 2 * pair))
    starts, at = {}, 0
    for name, size in sizes:
        starts[name] = at
        at += size
    return half, angles, starts, at


def aux_kernel(waves, few, spacing, assign_ref, thick_ref, counts_ref, planet_ref, quad_ref, spectra_ref, after_ref,
               aux_ref, total_ref):
    del after_ref
    levels, coeffs = spectra_ref.shape[1], spectra_ref.shape[4]
    pair = 2 * levels
    half, angles, starts, _ = aux_layout(waves, levels)
    lats = aux_ref.shape[1]
    counts = counts_ref[...].astype(jnp.float32)
    most = 3 * (waves - 1) + 1

    def attempt(p, least):
        points = p * float(spacing)
        left = points - counts * jnp.floor((points + 0.5) / counts)
        return jnp.where((left == 0.0) & (least > p), p, least)

    least = jnp.full((1, lats), float(most), jnp.float32)
    if most <= 16:
        for p in range(1, most):
            least = attempt(float(p), least)
    else:
        least = lax.fori_loop(1, most, lambda p, least: attempt(p.astype(jnp.float32), least), least)
    number = jnp.broadcast_to(least, (angles, lats))
    j = lax.broadcasted_iota(jnp.int32, (angles, lats), 0).astype(jnp.float32)
    share = jnp.where(2.0 * j <= number, jnp.where((j == 0.0) | (2.0 * j == number), 1.0, 2.0), 0.0) / number

    def slot(k, carry):
        harmonic = assign_ref[slot_order(waves, few, k)]
        turn = j * harmonic.astype(jnp.float32)
        turn = turn - number * jnp.floor((turn + 0.5) / number)
        turn = jnp.where(2.0 * turn > number, turn - number, turn) / number
        cosine, sine = cos_sin(turn)
        seen = (2 * spacing * harmonic).astype(jnp.float32) < counts
        gain = jnp.where(seen, jnp.where(harmonic == 0, 1.0, 2.0), 0.0)
        at = pl.ds(pl.multiple_of(starts["cosine"] + k * angles, SUBLANES), angles)
        aux_ref[at, :] = cosine * gain
        at = pl.ds(pl.multiple_of(starts["sine"] + k * angles, SUBLANES), angles)
        aux_ref[at, :] = -sine * gain
        mine = share * jnp.where(seen, 1.0, 0.0)
        own = k == (0 if few else lax.axis_index("band"))

        @pl.when(own)
        def _():
            aux_ref[starts["own_cosine"]:starts["own_cosine"] + angles, :] = cosine * mine
            aux_ref[starts["own_sine"]:starts["own_sine"] + angles, :] = -sine * mine

        return carry

    lax.fori_loop(0, waves, slot, 0)
    north = lax.broadcasted_iota(jnp.int32, (pair, lats), 0) < levels
    for name, ref in (("planet", planet_ref), ("quad", quad_ref)):
        aux_ref[starts[name]:starts[name] + pair, :] = jnp.where(north, ref[0:1, :], ref[1:2, :])
    wave = spacing * assign_ref[lax.axis_index("band")]
    level_at = lax.broadcasted_iota(jnp.int32, (pair, coeffs), 0) % levels
    inside = lax.broadcasted_iota(jnp.int32, (2, coeffs), 1) < coeffs - wave
    keep = inside & ((lax.broadcasted_iota(jnp.int32, (2, coeffs), 0) == 0) | (wave > 0))
    columns = [jnp.zeros((pair, coeffs), jnp.float32)] * 2
    for level in range(levels):
        weighted = jnp.where(keep, spectra_ref[0, level, 2].astype(jnp.float32), 0.0) * thick_ref[level]
        for r in range(2):
            columns[r] += jnp.where(level_at <= level, weighted[r:r + 1], 0.0)
    for r in range(2):
        at = starts["column"] + r * pair
        aux_ref[at:at + pair, :] = columns[r]
        total_ref[r:r + 1, :] = columns[r][0:1]


def direct_kernel(waves, few, spacing, belows, chunk, assign_ref, *refs):
    slots = waves if few else 1
    fourier_refs, refs = refs[:slots], refs[slots:]
    below_refs, refs = refs[:belows], refs[belows:]
    aux_ref, table_ref, out_ref, fourier_scr, back_scr, sems = refs
    levels = out_ref.shape[1]
    coeffs, lats = table_ref.shape[1], table_ref.shape[2]
    half, angles, starts, _ = aux_layout(waves, levels)
    pair = 2 * levels
    chunks = coeffs // chunk
    copies = []
    for k, ref in enumerate(fourier_refs):
        target = fourier_scr.at[k] if few else fourier_scr
        copies.append(pltpu.make_async_copy(ref, target, sems.at[k]))
        copies[-1].start()
    wave = spacing * assign_ref[lax.axis_index("band")]
    for copy in copies:
        copy.wait()

    def lat_block(block, carry):
        lanes = pl.ds(pl.multiple_of(block * LANES, LANES), LANES)
        coefs = []
        for k in range(waves):
            fields = []
            for field in range(FIELDS):
                at = field * 2 * pair
                both = fourier_scr[k, at:at + 2 * pair, lanes].astype(jnp.float32)
                fields.append((both[:pair], both[pair:]))
            coefs.append(fields)
        planet = aux_ref[starts["planet"]:starts["planet"] + pair, lanes]
        zero = jnp.zeros((pair, LANES), jnp.float32)

        def trig(name, k, j):
            group, row = j
            at = starts[name] + k * angles + group * SUBLANES
            if isinstance(group, int):
                return aux_ref[at + row:at + row + 1, lanes]
            return aux_ref[pl.ds(pl.multiple_of(at, SUBLANES), SUBLANES), lanes][row:row + 1]

        def angle(j, sums):
            even = [zero] * FIELDS
            odd = [zero] * FIELDS
            for k in range(waves):
                cosine = trig("cosine", k, j)
                sine = trig("sine", k, j)
                for field in range(FIELDS):
                    real, imag = coefs[k][field]
                    even[field] = even[field] + real * cosine
                    odd[field] = odd[field] + imag * sine
            (z_e, d_e, t_e), (z_o, d_o, t_o) = even, odd
            a_e = z_e + planet
            cosine = trig("own_cosine", 0, j)
            sine = trig("own_sine", 0, j)
            kinds = (
                (-(a_e * d_e + z_o * d_o), -(a_e * d_o + z_o * d_e)),
                (a_e * z_e + z_o * z_o, (a_e + z_e) * z_o),
                (0.5 * (z_e * z_e + z_o * z_o + d_e * d_e + d_o * d_o), z_e * z_o + d_e * d_o),
                (-(t_e * d_e + t_o * d_o), -(t_e * d_o + t_o * d_e)),
            )
            out = []
            for q, (in_even, in_odd) in enumerate(kinds):
                out.append(sums[2 * q] + in_even * cosine)
                out.append(sums[2 * q + 1] + in_odd * sine)
            return out

        sums = [zero] * (2 * TERMS)
        if half <= SUBLANES:
            for row in range(half):
                sums = angle((0, row), sums)
        else:
            def group(g, sums):
                for row in range(SUBLANES):
                    sums = angle((g, row), sums)
                return sums

            sums = lax.fori_loop(0, angles // SUBLANES, group, sums)
        quad = aux_ref[starts["quad"]:starts["quad"] + pair, lanes]
        for q in range(TERMS):
            both = jnp.concatenate([sums[2 * q] * quad, sums[2 * q + 1] * quad], axis=0)
            back_scr[q * 2 * pair:(q + 1) * 2 * pair, lanes] = both.astype(jnp.bfloat16)
        return carry

    lax.fori_loop(0, lats // LANES, lat_block, 0)

    back = back_scr[...]
    groups = 2 * FIELDS
    place = lax.broadcasted_iota(jnp.int32, (levels * groups, groups * pair), 0)
    source = lax.broadcasted_iota(jnp.int32, (levels * groups, groups * pair), 1)
    chosen = (place % groups == source // pair) & (place // groups == source % pair)
    move = jnp.where(chosen, 1.0, 0.0).astype(jnp.bfloat16)
    truncation = coeffs - 1
    for i in range(chunks):
        span = slice(i * chunk, (i + 1) * chunk)
        product = lax.dot_general(back, table_ref[0, span, :], (((1,), (1,)), ((), ())),
                                  preferred_element_type=jnp.float32)
        coeff = lax.broadcasted_iota(jnp.int32, (pair, chunk), 1) + i * chunk
        lower = lax.broadcasted_iota(jnp.int32, (pair, chunk), 0) < levels
        flip = coeff % 2 == 1
        degree = wave + coeff
        laplace = (degree * (degree + 1)).astype(jnp.float32) / float(truncation * (truncation + 1))
        inside = coeff < coeffs - wave

        def both_rows(q, r):
            at = (2 * q + r) * pair
            rows = product[at:at + pair]
            south = pltpu.roll(rows, levels, 0)
            return rows + jnp.where(flip, -south, south)

        results = []
        for field in range(FIELDS):
            for r in range(2):
                if field == 0:
                    value = both_rows(0, r)
                elif field == 1:
                    at = starts["column"] + r * pair
                    column = aux_ref[at:at + pair, span]
                    for below in below_refs:
                        column = column + below[r:r + 1, span]
                    value = both_rows(1, r) + laplace * (column + both_rows(2, r))
                else:
                    value = both_rows(3, r)
                keep = inside & lower
                if r == 1:
                    keep = keep & (wave > 0)
                results.append(jnp.where(keep, value, 0.0))
        stacked_rows = jnp.concatenate(results, axis=0).astype(jnp.bfloat16)
        ordered = jnp.dot(move, stacked_rows, preferred_element_type=jnp.float32)
        for level in range(levels):
            for field in range(FIELDS):
                at = (level * FIELDS + field) * 2
                out_ref[0, level, field, :, span] = ordered[at:at + 2].astype(jnp.bfloat16)


def on_device(spectra, legendre, assignment, circle_longitudes, coriolis, weights, thickness):
    levels, coeffs = spectra.shape[1], spectra.shape[4]
    lats = legendre.shape[2]
    waves = lax.axis_size("band")
    spacing = coeffs // waves
    few = waves <= 8
    pair = 2 * levels
    rows = levels * FIELDS * 2
    chunk = 256 if coeffs % 256 == 0 else LANES
    chunks = coeffs // chunk
    smem = pl.BlockSpec(memory_space=pltpu.SMEM)
    vmem = pl.BlockSpec(memory_space=pltpu.VMEM)
    hbm = pl.BlockSpec(memory_space=pltpu.HBM)
    anywhere = pl.BlockSpec(memory_space=pl.ANY)

    fourier = pl.pallas_call(
        functools.partial(inverse_kernel, spacing, chunk),
        out_shape=jax.ShapeDtypeStruct((2 * rows, lats), jnp.bfloat16),
        in_specs=[smem, hbm, hbm],
        out_specs=vmem,
        scratch_shapes=[
            pltpu.VMEM(spectra.shape, jnp.bfloat16),
            pltpu.VMEM((rows, coeffs), jnp.float32),
            pltpu.VMEM((chunks, chunk, lats), jnp.bfloat16),
            pltpu.VMEM((2 * rows, lats), jnp.float32),
            pltpu.SemaphoreType.DMA,
            pltpu.SemaphoreType.DMA((chunks,)),
        ],
        compiler_params=pltpu.CompilerParams(vmem_limit_bytes=24 << 20),
        name="inverse",
    )(assignment, spectra, legendre)

    if few:
        fouriers = [fourier] + [
            lax.ppermute(fourier, "band", [(i, (i + k) % waves) for i in range(waves)]) for k in range(1, waves)
        ]
    else:
        fouriers = [lax.all_gather(fourier, "band")]

    half, angles, starts, aux_rows = aux_layout(waves, levels)
    aux, total = pl.pallas_call(
        functools.partial(aux_kernel, waves, few, spacing),
        out_shape=(
            jax.ShapeDtypeStruct((aux_rows, lats), jnp.float32),
            jax.ShapeDtypeStruct((2, coeffs), jnp.float32),
        ),
        in_specs=[smem, smem, vmem, vmem, vmem, vmem, anywhere],
        out_specs=(vmem, vmem),
        compiler_params=pltpu.CompilerParams(vmem_limit_bytes=(16 if few else 48) << 20),
        name="tables",
    )(assignment, thickness, circle_longitudes.reshape(1, lats), coriolis, weights, spectra, fourier)

    deep = ("fld", "sub")
    places = lax.axis_size(deep)
    belows = [
        lax.ppermute(total, deep, [(i, i - k) for i in range(k, places)]) for k in range(1, places)
    ]

    return pl.pallas_call(
        functools.partial(direct_kernel, waves, few, spacing, len(belows), chunk),
        out_shape=jax.ShapeDtypeStruct(spectra.shape, jnp.bfloat16),
        in_specs=[smem] + [anywhere] * len(fouriers) + [vmem] * (len(belows) + 2),
        out_specs=vmem,
        scratch_shapes=[
            pltpu.VMEM((waves, 2 * rows, lats), jnp.bfloat16),
            pltpu.VMEM((TERMS * 2 * pair, lats), jnp.bfloat16),
            pltpu.SemaphoreType.DMA((len(fouriers),)),
        ],
        compiler_params=pltpu.CompilerParams(vmem_limit_bytes=(24 if few else 56) << 20),
        name="direct",
    )(assignment, *fouriers, *belows, aux, legendre)


def solution(mesh):
    in_specs = (
        P(("member", "band"), ("fld", "sub"), None, None, None),
        P("band", None, None),
        P(),
        P(),
        P(),
        P(),
        P(("fld", "sub")),
    )
    out_specs = P(("member", "band"), ("fld", "sub"), None, None, None)
    return jax.shard_map(
        on_device, mesh=mesh, in_specs=in_specs, out_specs=out_specs, check_vma=False
    )
```

time: 50.4 us -> 26.4 us (0.52)
  the two profiles are of different devices: /device:TPU:3 before, /device:TPU:0 now
where the time goes in v2:
time: 26.4 us; the launch traced here: 26.1 us
  starting transfers between devices  9.98 us (38%)
  Pallas kernels  8.08 us (31%)
  waiting for transfers between devices  4.52 us (17%)
  local copies, waits for them, and re-layouts  3.44 us (13%)
    ppermute x3, starting transfers between devices, on_device(): lax.ppermute(fourier, 'band', [(i, (i + k) % waves) for i in range(waves)])  6.11 us
    pallas_call x1, Pallas kernels, on_device(): pl.pallas_call(functools.partial(direct_kernel, waves, few, spacing, len(...  4.17 us
    ppermute x3, waiting for transfers between devices, on_device(): lax.ppermute(total, deep, [(i, i - k) for i in range(k, places)])  4.16 us
    ppermute x3, starting transfers between devices, on_device(): lax.ppermute(total, deep, [(i, i - k) for i in range(k, places)])  3.86 us
    unnamed x18, local copies, waits for them, and re-layouts  3.43 us
    pallas_call x1, Pallas kernels, on_device(): pl.pallas_call(functools.partial(inverse_kernel, spacing, chunk), out_sha...  2.79 us
    pallas_call x1, Pallas kernels, on_device(): pl.pallas_call(functools.partial(aux_kernel, waves, few, spacing), out_sh...  1.12 us
  transfers between devices with their start and end apart: 6, of which 4 were waited for; matrix products, arithmetic and copies ran while one was open for 0% of the time, Pallas kernels for 4%

profile of v2, /device:TPU:0, one launch (start us, length us, event | category | flops | bytes accessed | tf_op | source)
XLA Modules:
  0.0 26.1 jit_solution(17777805947780175940)
XLA Ops:
  0.0 0.0 copy-start
  0.0 1.9 %copy-done = bf16[1,1280,1280]{2,1,0:T(8,128)(2,1)S(1)} copy-done((bf16[1,1280,1280]{2,1,0:T(8,128)(2,1)S(1)}, bf16[1,1280,1280]{2,1,0:T(8,128)(2,1)}, u32[]{:S(2)}) %copy-start) | copy-done | bytes 3276824
  1.9 0.0 copy-start.2
  1.9 0.8 %copy-done.2 = bf16[1,4,3,2,1280]{4,3,2,1,0:T(2,128)(2,1)S(1)} copy-done((bf16[1,4,3,2,1280]{4,3,2,1,0:T(2,128)(2,1)S(1)}, bf16[1,4,3,2,1280]{4,3,2,1,0:T(2,128)(2,1)}, u32[]{:S(2)}) %copy-start.2) | copy-done | bytes 61464
  2.8 0.0 copy-start.6
  2.8 0.7 %copy-done.6 = s32[4]{0:T(128)S(1)} copy-done((s32[4]{0:T(128)S(1)}, s32[4]{0:T(128)}, u32[]{:S(2)}) %copy-start.6) | copy-done | bytes 40
  3.4 0.0 copy-start.8
  3.4 0.0 copy-start.3
  3.4 0.0 copy-start.4
  3.4 0.0 copy-start.5
  3.4 0.0 copy-start.7
  3.4 0.0 copy-start.1
  3.4 2.8 %inverse.1.after_ref.refs_0_ = bf16[48,1280]{1,0:T(8,128)(2,1)S(1)} custom-call(s32[4]{0:T(128)S(1)} %copy-done.6, bf16[1,4,3,2,1280]{4,3,2,1,0:T(2,128)(2,1)S(1)} %copy-done.2, bf16[1,1280,1280]{2,1,0:T(8,128)(2,1)S(1)} %copy-done), custom_call_target="tpu_custom_call" | custom-call | tf_op jit(solution)/shard_map/inverse/pallas_call | solution.py:310
  6.2 5.1 %collective-permute-start.2 = (bf16[48,1280]{1,0:T(8,128)(2,1)S(1)}, bf16[48,1280]{1,0:T(8,128)(2,1)S(1)}, u32[]{:S(2)}, u32[]{:S(2)}) collective-permute-start(bf16[48,1280]{1,0:T(8,128)(2,1)S(1)} %inverse.1.after_ref.refs_0_), channel_id=1, source_target_pairs={{0,12},{4,0},{8,4},{12,8},{1,13},{5,1},{9,5},{13,9},{2,14},{6,2},{... | collective-permute-start | bytes 368648 | tf_op jit(solution)/shard_map/ppermute | solution.py:329
  11.3 0.0 collective-permute-start.1
  11.3 1.0 %collective-permute-start = (bf16[48,1280]{1,0:T(8,128)(2,1)S(1)}, bf16[48,1280]{1,0:T(8,128)(2,1)S(1)}, u32[]{:S(2)}, u32[]{:S(2)}) collective-permute-start(bf16[48,1280]{1,0:T(8,128)(2,1)S(1)} %inverse.1.after_ref.refs_0_), channel_id=1, source_target_pairs={{0,4},{4,8},{8,12},{12,0},{1,5},{5,9},{9,13},{13,1},{2,6},{6,10},{... | collective-permute-start | bytes 368648 | tf_op jit(solution)/shard_map/ppermute | solution.py:329
  12.4 0.0 copy-done.8
  12.4 0.0 copy-done.3
  12.4 0.0 copy-done.4
  12.4 0.0 copy-done.5
  12.4 0.0 copy-done.7
  12.4 1.1 %tables.1 = (f32[112,1280]{1,0:T(8,128)S(1)}, f32[2,1280]{1,0:T(2,128)S(1)}) custom-call(s32[4]{0:T(128)S(1)} %copy-done.6, f32[4]{0:T(128)S(1)} %copy-done.7, s32[1,1280]{1,0:T(1,128)S(1)} %reshape.3.counts_ref, f32[2,1280]{1,0:T(2,128)S(1)} %copy-done.4, f32[2,1280]{1,0:T(2,128)S(1)} %copy-done.5, bf16[1,4,3,2,1280]{4,3,2,1,0:T(2,128)(2,1)S(1)} %copy-done.3, ...), custom_call_target="tpu_custom_call" | custom-call | tf_op jit(solution)/shard_map/tables/pallas_call | solution.py:335
  13.5 1.3 %collective-permute-start.5 = (f32[2,1280]{1,0:T(2,128)S(1)}, f32[2,1280]{1,0:T(2,128)S(1)}, u32[]{:S(2)}, u32[]{:S(2)}) collective-permute-start(f32[2,1280]{1,0:T(2,128)S(1)} %get-tuple-element.7), channel_id=1, source_target_pairs={{3,0},{7,4},{11,8},{15,12},{19,16},{23,20},{27,24},{31,28}} | collective-permute-start | bytes 30728 | tf_op jit(solution)/shard_map/ppermute | solution.py:350
  14.8 1.3 %collective-permute-start.4 = (f32[2,1280]{1,0:T(2,128)S(1)}, f32[2,1280]{1,0:T(2,128)S(1)}, u32[]{:S(2)}, u32[]{:S(2)}) collective-permute-start(f32[2,1280]{1,0:T(2,128)S(1)} %get-tuple-element.7), channel_id=1, source_target_pairs={{2,0},{3,1},{6,4},{7,5},{10,8},{11,9},{14,12},{15,13},{18,16},{19,... | collective-permute-start | bytes 30728 | tf_op jit(solution)/shard_map/ppermute | solution.py:350
  16.1 2.4 %collective-permute-done.5.refs_6_ = f32[2,1280]{1,0:T(2,128)S(1)} collective-permute-done((f32[2,1280]{1,0:T(2,128)S(1)}, f32[2,1280]{1,0:T(2,128)S(1)}, u32[]{:S(2)}, u32[]{:S(2)}) %collective-permute-start.5) | collective-permute-done | bytes 10272 | tf_op jit(solution)/shard_map/ppermute | solution.py:350
  18.5 1.3 %collective-permute-start.3 = (f32[2,1280]{1,0:T(2,128)S(1)}, f32[2,1280]{1,0:T(2,128)S(1)}, u32[]{:S(2)}, u32[]{:S(2)}) collective-permute-start(f32[2,1280]{1,0:T(2,128)S(1)} %get-tuple-element.7), channel_id=1, source_target_pairs={{1,0},{2,1},{3,2},{5,4},{6,5},{7,6},{9,8},{10,9},{11,10},{13,12},{... | collective-permute-start | bytes 30728 | tf_op jit(solution)/shard_map/ppermute | solution.py:350
  19.8 0.6 %collective-permute-done.4.refs_5_ = f32[2,1280]{1,0:T(2,128)S(1)} collective-permute-done((f32[2,1280]{1,0:T(2,128)S(1)}, f32[2,1280]{1,0:T(2,128)S(1)}, u32[]{:S(2)}, u32[]{:S(2)}) %collective-permute-start.4) | collective-permute-done | bytes 10272 | tf_op jit(solution)/shard_map/ppermute | solution.py:350
  20.4 1.2 %collective-permute-done.3.refs_4_ = f32[2,1280]{1,0:T(2,128)S(1)} collective-permute-done((f32[2,1280]{1,0:T(2,128)S(1)}, f32[2,1280]{1,0:T(2,128)S(1)}, u32[]{:S(2)}, u32[]{:S(2)}) %collective-permute-start.3) | collective-permute-done | bytes 10272 | tf_op jit(solution)/shard_map/ppermute | solution.py:350
  21.6 0.0 collective-permute-done.2.refs_3_
  21.6 0.4 %collective-permute-done.1.refs_2_ = bf16[48,1280]{1,0:T(8,128)(2,1)S(1)} collective-permute-done((bf16[48,1280]{1,0:T(8,128)(2,1)S(1)}, bf16[48,1280]{1,0:T(8,128)(2,1)S(1)}, u32[]{:S(2)}, u32[]{:S(2)}) %collective-permute-start.1) | collective-permute-done | bytes 122912 | tf_op jit(solution)/shard_map/ppermute | solution.py:329
  21.9 0.0 collective-permute-done.refs_1_
  21.9 0.0 copy-done.1
  21.9 4.2 %direct.1 = bf16[1,4,3,2,1280]{4,3,2,1,0:T(2,128)(2,1)} custom-call(s32[4]{0:T(128)S(1)} %copy-done.6, bf16[48,1280]{1,0:T(8,128)(2,1)S(1)} %inverse.1.after_ref.refs_0_, bf16[48,1280]{1,0:T(8,128)(2,1)S(1)} %collective-permute-done.refs_1_, bf16[48,1280]{1,0:T(8,128)(2,1)S(1)} %collective-permute-done.1.refs_2_, ...), custom_call_target="tpu_custom_call" | custom-call | tf_op jit(solution)/shard_map/direct/pallas_call | solution.py:353
  (1 shorter events, 0.0 us)
Async XLA Ops:
  0.0 1.9 %copy-start = (bf16[1,1280,1280]{2,1,0:T(8,128)(2,1)S(1)}, bf16[1,1280,1280]{2,1,0:T(8,128)(2,1)}, u32[]{:S(2)}) copy-start(bf16[1,1280,1280]{2,1,0:T(8,128)(2,1)} %refs_8_.1) | copy-start | bytes 9830404
  1.9 0.8 %copy-start.2 = (bf16[1,4,3,2,1280]{4,3,2,1,0:T(2,128)(2,1)S(1)}, bf16[1,4,3,2,1280]{4,3,2,1,0:T(2,128)(2,1)}, u32[]{:S(2)}) copy-start(bf16[1,4,3,2,1280]{4,3,2,1,0:T(2,128)(2,1)} %spectra_ref.3) | copy-start | bytes 184324
  2.8 0.7 %copy-start.6 = (s32[4]{0:T(128)S(1)}, s32[4]{0:T(128)}, u32[]{:S(2)}) copy-start(s32[4]{0:T(128)} %assign_ref.5) | copy-start | bytes 52
  3.4 8.9 %copy-start.8 = (s32[1280]{0:T(1024)S(1)}, s32[1280]{0:T(1024)}, u32[]{:S(2)}) copy-start(s32[1280]{0:T(1024)} %param.10) | copy-start | bytes 15364
  3.4 8.9 %copy-start.3 = (bf16[1,4,3,2,1280]{4,3,2,1,0:T(2,128)(2,1)S(1)}, bf16[1,4,3,2,1280]{4,3,2,1,0:T(2,128)(2,1)}, u32[]{:S(2)}) copy-start(bf16[1,4,3,2,1280]{4,3,2,1,0:T(2,128)(2,1)} %spectra_ref.3) | copy-start | bytes 184324
  3.4 9.0 %copy-start.4 = (f32[2,1280]{1,0:T(2,128)S(1)}, f32[2,1280]{1,0:T(2,128)}, u32[]{:S(2)}) copy-start(f32[2,1280]{1,0:T(2,128)} %planet_ref.1) | copy-start | bytes 30724
  3.4 9.0 %copy-start.5 = (f32[2,1280]{1,0:T(2,128)S(1)}, f32[2,1280]{1,0:T(2,128)}, u32[]{:S(2)}) copy-start(f32[2,1280]{1,0:T(2,128)} %quad_ref.1) | copy-start | bytes 30724
  3.4 9.0 %copy-start.7 = (f32[4]{0:T(128)S(1)}, f32[4]{0:T(128)}, u32[]{:S(2)}) copy-start(f32[4]{0:T(128)} %thick_ref.1) | copy-start | bytes 52
  3.4 18.5 %copy-start.1 = (bf16[1,1280,1280]{2,1,0:T(8,128)(2,1)S(1)}, bf16[1,1280,1280]{2,1,0:T(8,128)(2,1)}, u32[]{:S(2)}) copy-start(bf16[1,1280,1280]{2,1,0:T(8,128)(2,1)} %refs_8_.1) | copy-start | bytes 9830404
  6.2 15.3 %collective-permute-start.2 = (bf16[48,1280]{1,0:T(8,128)(2,1)S(1)}, bf16[48,1280]{1,0:T(8,128)(2,1)S(1)}, u32[]{:S(2)}, u32[]{:S(2)}) collective-permute-start(bf16[48,1280]{1,0:T(8,128)(2,1)S(1)} %inverse.1.after_ref.refs_0_), channel_id=1, source_target_pairs={{0,12},{4,0},{8,4},{12,8},{1,13},{5,1},{9,5},{13,9},{2,14},{6,2},{... | collective-permute-start | bytes 368648 | tf_op jit(solution)/shard_map/ppermute | solution.py:329
  11.3 10.6 %collective-permute-start.1 = (bf16[48,1280]{1,0:T(8,128)(2,1)S(1)}, bf16[48,1280]{1,0:T(8,128)(2,1)S(1)}, u32[]{:S(2)}, u32[]{:S(2)}) collective-permute-start(bf16[48,1280]{1,0:T(8,128)(2,1)S(1)} %inverse.1.after_ref.refs_0_), channel_id=1, source_target_pairs={{0,8},{4,12},{8,0},{12,4},{1,9},{5,13},{9,1},{13,5},{2,10},{6,14},... | collective-permute-start | bytes 368648 | tf_op jit(solution)/shard_map/ppermute | solution.py:329
  11.3 10.6 %collective-permute-start = (bf16[48,1280]{1,0:T(8,128)(2,1)S(1)}, bf16[48,1280]{1,0:T(8,128)(2,1)S(1)}, u32[]{:S(2)}, u32[]{:S(2)}) collective-permute-start(bf16[48,1280]{1,0:T(8,128)(2,1)S(1)} %inverse.1.after_ref.refs_0_), channel_id=1, source_target_pairs={{0,4},{4,8},{8,12},{12,0},{1,5},{5,9},{9,13},{13,1},{2,6},{6,10},{... | collective-permute-start | bytes 368648 | tf_op jit(solution)/shard_map/ppermute | solution.py:329
  13.5 5.0 %collective-permute-start.5 = (f32[2,1280]{1,0:T(2,128)S(1)}, f32[2,1280]{1,0:T(2,128)S(1)}, u32[]{:S(2)}, u32[]{:S(2)}) collective-permute-start(f32[2,1280]{1,0:T(2,128)S(1)} %get-tuple-element.7), channel_id=1, source_target_pairs={{3,0},{7,4},{11,8},{15,12},{19,16},{23,20},{27,24},{31,28}} | collective-permute-start | bytes 30728 | tf_op jit(solution)/shard_map/ppermute | solution.py:350
  14.8 5.6 %collective-permute-start.4 = (f32[2,1280]{1,0:T(2,128)S(1)}, f32[2,1280]{1,0:T(2,128)S(1)}, u32[]{:S(2)}, u32[]{:S(2)}) collective-permute-start(f32[2,1280]{1,0:T(2,128)S(1)} %get-tuple-element.7), channel_id=1, source_target_pairs={{2,0},{3,1},{6,4},{7,5},{10,8},{11,9},{14,12},{15,13},{18,16},{19,... | collective-permute-start | bytes 30728 | tf_op jit(solution)/shard_map/ppermute | solution.py:350
  18.5 3.1 %collective-permute-start.3 = (f32[2,1280]{1,0:T(2,128)S(1)}, f32[2,1280]{1,0:T(2,128)S(1)}, u32[]{:S(2)}, u32[]{:S(2)}) collective-permute-start(f32[2,1280]{1,0:T(2,128)S(1)} %get-tuple-element.7), channel_id=1, source_target_pairs={{1,0},{2,1},{3,2},{5,4},{6,5},{7,6},{9,8},{10,9},{11,10},{13,12},{... | collective-permute-start | bytes 30728 | tf_op jit(solution)/shard_map/ppermute | solution.py:350

commit v3 on v2

v3 whole, which is shorter than its diff:
```python
import functools
import math

import jax
import jax.numpy as jnp
from jax import lax
from jax.experimental import pallas as pl
from jax.experimental.pallas import tpu as pltpu
from jax.sharding import PartitionSpec as P


FIELDS = 3
TERMS = 4
LANES = 128
SUBLANES = 8


def round_up(value, multiple):
    return -(-value // multiple) * multiple


def slot_position(waves, few, slot):
    return lax.axis_index("band") ^ slot if few else slot


def spectra_kernel(spacing, assign_ref, thick_ref, spectra_ref, signed_ref, total_ref,
                   assign_scr, thick_scr, spectra_scr, rows_scr, sems):
    copies = [
        pltpu.make_async_copy(source, target, sems.at[i])
        for i, (source, target) in enumerate(
            ((assign_ref, assign_scr), (thick_ref, thick_scr), (spectra_ref, spectra_scr)))
    ]
    for copy in copies:
        copy.start()
    levels, coeffs = spectra_ref.shape[1], spectra_ref.shape[4]
    rows = levels * FIELDS * 2
    out_rows = 2 * rows
    place = lax.broadcasted_iota(jnp.int32, (out_rows, rows), 0)
    source = lax.broadcasted_iota(jnp.int32, (out_rows, rows), 1)
    chosen = (place // (2 * levels) == source % (2 * FIELDS)) & (place % levels == source // (2 * FIELDS))
    move = jnp.where(chosen, 1.0, 0.0).astype(jnp.bfloat16)
    for copy in copies:
        copy.wait()
    wave = spacing * assign_scr[lax.axis_index("band")]
    for level in range(levels):
        for field in range(FIELDS):
            at = (level * FIELDS + field) * 2
            rows_scr[at:at + 2, :] = spectra_scr[0, level, field].astype(jnp.float32)
    coeff = lax.broadcasted_iota(jnp.int32, (rows, coeffs), 1)
    part = lax.broadcasted_iota(jnp.int32, (rows, coeffs), 0) % 2
    keep = (coeff < coeffs - wave) & ((part == 0) | (wave > 0))
    masked = jnp.where(keep, rows_scr[...], 0.0).astype(jnp.bfloat16)
    spread = jnp.dot(move, masked, preferred_element_type=jnp.float32)
    odd = lax.broadcasted_iota(jnp.int32, (out_rows, coeffs), 1) % 2 == 1
    south = lax.broadcasted_iota(jnp.int32, (out_rows, coeffs), 0) // levels % 2 == 1
    signed_ref[...] = jnp.where(odd & south, -spread, spread).astype(jnp.bfloat16)
    for r in range(2):
        at = (2 * 2 + r) * 2 * levels
        total = spread[at:at + 1] * thick_scr[0]
        for level in range(1, levels):
            total += spread[at + level:at + level + 1] * thick_scr[level]
        total_ref[r:r + 1, :] = total


def cos_sin(turns):
    angle = turns * (2.0 * math.pi)
    square = angle * angle
    cosine = jnp.full_like(angle, -1.0 / math.factorial(18))
    sine = jnp.full_like(angle, 1.0 / math.factorial(17))
    for n in range(8, -1, -1):
        cosine = cosine * square + (-1.0) ** n / math.factorial(2 * n)
        if n < 8:
            sine = sine * square + (-1.0) ** n / math.factorial(2 * n + 1)
    return cosine, sine * angle


def aux_layout(waves, levels):
    half = (3 * (waves - 1) + 1) // 2 + 1
    angles = round_up(half, SUBLANES)
    pair = 2 * levels
    sizes = (("cosine", waves * angles), ("sine", waves * angles), ("own_cosine", angles), ("own_sine", angles),
             ("planet", pair), ("quad", pair), ("column", 2 * pair), ("keep", 2), ("laplace", 1))
    starts, at = {}, 0
    for name, size in sizes:
        starts[name] = at
        at += size
    return half, angles, starts, round_up(at, SUBLANES)


def aux_kernel(waves, few, spacing, assign_ref, thick_ref, counts_ref, planet_ref, quad_ref, spectra_ref, after_ref,
               aux_ref):
    del after_ref
    levels, coeffs = spectra_ref.shape[1], spectra_ref.shape[4]
    pair = 2 * levels
    half, angles, starts, _ = aux_layout(waves, levels)
    lats = aux_ref.shape[1]
    counts = counts_ref[...].astype(jnp.float32)
    most = 3 * (waves - 1) + 1

    def attempt(p, least):
        points = p * float(spacing)
        left = points - counts * jnp.floor((points + 0.5) / counts)
        return jnp.where((left == 0.0) & (least > p), p, least)

    least = jnp.full((1, lats), float(most), jnp.float32)
    if most <= 16:
        for p in range(1, most):
            least = attempt(float(p), least)
    else:
        least = lax.fori_loop(1, most, lambda p, least: attempt(p.astype(jnp.float32), least), least)
    number = jnp.broadcast_to(least, (angles, lats))
    j = lax.broadcasted_iota(jnp.int32, (angles, lats), 0).astype(jnp.float32)
    share = jnp.where(2.0 * j <= number, jnp.where((j == 0.0) | (2.0 * j == number), 1.0, 2.0), 0.0) / number

    def slot(k, carry):
        harmonic = assign_ref[slot_position(waves, few, k)]
        turn = j * harmonic.astype(jnp.float32)
        turn = turn - number * jnp.floor((turn + 0.5) / number)
        turn = jnp.where(2.0 * turn > number, turn - number, turn) / number
        cosine, sine = cos_sin(turn)
        seen = (2 * spacing * harmonic).astype(jnp.float32) < counts
        gain = jnp.where(seen, jnp.where(harmonic == 0, 1.0, 2.0), 0.0)
        at = pl.ds(pl.multiple_of(starts["cosine"] + k * angles, SUBLANES), angles)
        aux_ref[at, :] = cosine * gain
        at = pl.ds(pl.multiple_of(starts["sine"] + k * angles, SUBLANES), angles)
        aux_ref[at, :] = -sine * gain
        mine = share * jnp.where(seen, 1.0, 0.0)
        own = k == (0 if few else lax.axis_index("band"))

        @pl.when(own)
        def _():
            aux_ref[starts["own_cosine"]:starts["own_cosine"] + angles, :] = cosine * mine
            aux_ref[starts["own_sine"]:starts["own_sine"] + angles, :] = -sine * mine

        return carry

    lax.fori_loop(0, waves, slot, 0)
    north = lax.broadcasted_iota(jnp.int32, (pair, lats), 0) < levels
    for name, ref in (("planet", planet_ref), ("quad", quad_ref)):
        aux_ref[starts[name]:starts[name] + pair, :] = jnp.where(north, ref[0:1, :], ref[1:2, :])
    wave = spacing * assign_ref[lax.axis_index("band")]
    level_at = lax.broadcasted_iota(jnp.int32, (pair, coeffs), 0) % levels
    coeff = lax.broadcasted_iota(jnp.int32, (2, coeffs), 1)
    keep = (coeff < coeffs - wave) & ((lax.broadcasted_iota(jnp.int32, (2, coeffs), 0) == 0) | (wave > 0))
    columns = [jnp.zeros((pair, coeffs), jnp.float32)] * 2
    for level in range(levels):
        weighted = jnp.where(keep, spectra_ref[0, level, 2].astype(jnp.float32), 0.0) * thick_ref[level]
        for r in range(2):
            columns[r] += jnp.where(level_at <= level, weighted[r:r + 1], 0.0)
    for r in range(2):
        at = starts["column"] + r * pair
        aux_ref[at:at + pair, :] = columns[r]
    aux_ref[starts["keep"]:starts["keep"] + 2, :] = jnp.where(keep, 1.0, 0.0)
    degree = wave + coeff[0:1]
    truncation = coeffs - 1
    aux_ref[starts["laplace"]:starts["laplace"] + 1, :] = (
        (degree * (degree + 1)).astype(jnp.float32) / float(truncation * (truncation + 1)))


def arrival(slots):
    return (2, 0, 1) if slots == 3 else range(slots)


def direct_kernel(waves, few, belows, begin, trim, parts, last, *refs):
    own_ref, refs = refs[0], refs[1:]
    slot_refs = [None] * len(parts)
    for at in arrival(len(parts)):
        slot_refs[at] = refs[:parts[at]]
        refs = refs[parts[at]:]
    below_refs, refs = refs[:belows], refs[belows:]
    aux_ref, table_ref, refs = refs[0], refs[1], refs[2:]
    if begin > 0:
        earlier_ref, refs = refs[0], refs[1:]
    if last:
        out_ref, back_scr, out_scr, below_scr, sems = refs
        place = lax.axis_index(("fld", "sub"))
        (below_ref,) = below_refs
        below = jnp.zeros(below_ref.shape[1:], jnp.float32)
        for p in range(1, below_ref.shape[0]):
            below += jnp.where(place < p, below_ref[p], 0.0)
        below_scr[...] = below
        levels = out_scr.shape[1]
    else:
        partial_ref, back_scr = refs
        levels = back_scr.shape[0] // (4 * TERMS)
    chunks, lats, chunk = table_ref.shape
    half, angles, starts, _ = aux_layout(waves, levels)
    pair = 2 * levels
    zero = jnp.zeros((pair, LANES), jnp.float32)

    def products(lane, slots):
        here = pl.ds(lane, LANES)
        lanes = pl.ds(begin + lane, LANES)
        coefs = []
        for k in range(slots):
            fields = []
            for field in range(FIELDS):
                rows = slice(field * 2 * pair, (field + 1) * 2 * pair)
                if not few:
                    both = slot_refs[0][0][k, rows, here].astype(jnp.float32)
                elif k == 0:
                    both = own_ref[rows, here].astype(jnp.float32)
                else:
                    there = pl.ds(lane - trim, LANES)
                    both = slot_refs[k - 1][0][rows, there].astype(jnp.float32)
                    for ref in slot_refs[k - 1][1:]:
                        both = both + ref[rows, there].astype(jnp.float32)
                fields.append((both[:pair], both[pair:]))
            coefs.append(fields)
        planet = aux_ref[starts["planet"]:starts["planet"] + pair, lanes]

        def trig(name, k, j):
            group, row = j
            at = starts[name] + k * angles + group * SUBLANES
            if isinstance(group, int):
                return aux_ref[at + row:at + row + 1, lanes]
            return aux_ref[pl.ds(pl.multiple_of(at, SUBLANES), SUBLANES), lanes][row:row + 1]

        def angle(j, sums):
            if isinstance(j[0], int) and (j[1] == 0 or 2 * j[1] == 3 * (waves - 1) + 1):
                return plain_angle(j, sums)
            even = [zero] * FIELDS
            odd = [zero] * FIELDS
            for k in range(slots):
                cosine = trig("cosine", k, j)
                sine = trig("sine", k, j)
                for field in range(FIELDS):
                    real, imag = coefs[k][field]
                    even[field] = even[field] + real * cosine if k else real * cosine
                    odd[field] = odd[field] + imag * sine if k else imag * sine
            (z_e, d_e, t_e), (z_o, d_o, t_o) = even, odd
            a_e = z_e + planet
            cosine = trig("own_cosine", 0, j)
            sine = trig("own_sine", 0, j)
            kinds = (
                (-(a_e * d_e + z_o * d_o), -(a_e * d_o + z_o * d_e)),
                (a_e * z_e + z_o * z_o, (a_e + z_e) * z_o),
                (0.5 * (z_e * z_e + z_o * z_o + d_e * d_e + d_o * d_o), z_e * z_o + d_e * d_o),
                (-(t_e * d_e + t_o * d_o), -(t_e * d_o + t_o * d_e)),
            )
            out = []
            for q, (in_even, in_odd) in enumerate(kinds):
                out.append(sums[2 * q] + in_even * cosine)
                out.append(sums[2 * q + 1] + in_odd * sine)
            return out

        def plain_angle(j, sums):
            even = [zero] * FIELDS
            for k in range(slots):
                cosine = trig("cosine", k, j)
                for field in range(FIELDS):
                    real = coefs[k][field][0]
                    even[field] = even[field] + real * cosine if k else real * cosine
            z, d, t = even
            a = z + planet
            cosine = trig("own_cosine", 0, j)
            kinds = (-(a * d), a * z, 0.5 * (z * z + d * d), -(t * d))
            out = list(sums)
            for q, kind in enumerate(kinds):
                out[2 * q] = sums[2 * q] + kind * cosine
            return out

        sums = [zero] * (2 * TERMS)
        if half <= SUBLANES:
            for row in range(half):
                sums = angle((0, row), sums)
        else:
            def group(g, sums):
                for row in range(SUBLANES):
                    sums = angle((g, row), sums)
                return sums

            sums = lax.fori_loop(0, angles // SUBLANES, group, sums)
        quad = aux_ref[starts["quad"]:starts["quad"] + pair, lanes]
        for q in range(TERMS):
            both = jnp.concatenate([sums[2 * q] * quad, sums[2 * q + 1] * quad], axis=0)
            back_scr[q * 2 * pair:(q + 1) * 2 * pair, here] = both.astype(jnp.bfloat16)

    for block in range(trim // LANES):
        products(block * LANES, 1)

    def lat_block(block, carry):
        products(pl.multiple_of(trim + block * LANES, LANES), waves)
        return carry

    lax.fori_loop(0, (lats - trim) // LANES, lat_block, 0)

    back = back_scr[...]
    groups = 2 * FIELDS
    place = lax.broadcasted_iota(jnp.int32, (levels * groups, groups * pair), 0)
    source = lax.broadcasted_iota(jnp.int32, (levels * groups, groups * pair), 1)
    chosen = (place % groups == source // pair) & (place // groups == source % pair)
    move = jnp.where(chosen, 1.0, 0.0).astype(jnp.bfloat16)
    copies = []
    for i in range(chunks):
        span = slice(i * chunk, (i + 1) * chunk)
        product = jnp.dot(back, table_ref[i], preferred_element_type=jnp.float32)
        if begin > 0:
            product = product + earlier_ref[:, span]
        if not last:
            partial_ref[:, span] = product
            continue
        odd = lax.broadcasted_iota(jnp.int32, (pair, chunk), 1) % 2 == 1
        laplace = aux_ref[starts["laplace"]:starts["laplace"] + 1, span]

        def both_rows(q, r):
            at = (2 * q + r) * pair
            rows = product[at:at + pair]
            south = pltpu.roll(rows, levels, 0)
            return rows + jnp.where(odd, -south, south)

        results = []
        for field in range(FIELDS):
            for r in range(2):
                if field == 0:
                    value = both_rows(0, r)
                elif field == 1:
                    at = starts["column"] + r * pair
                    column = aux_ref[at:at + pair, span]
                    column = column + below_scr[r:r + 1, span]
                    value = both_rows(1, r) + laplace * (column + both_rows(2, r))
                else:
                    value = both_rows(3, r)
                keep = aux_ref[starts["keep"] + r:starts["keep"] + r + 1, span]
                results.append(jnp.where(keep > 0.0, value, 0.0))
        stacked_rows = jnp.concatenate(results, axis=0).astype(jnp.bfloat16)
        ordered = jnp.dot(move, stacked_rows, preferred_element_type=jnp.float32)
        for level in range(levels):
            for field in range(FIELDS):
                at = (level * FIELDS + field) * 2
                out_scr[0, level, field, :, span] = ordered[at:at + 2].astype(jnp.bfloat16)
        there = (slice(None),) * 4 + (pl.ds(i * chunk, chunk),)
        copies.append(pltpu.make_async_copy(out_scr.at[there], out_ref.at[there], sems.at[i]))
        copies[-1].start()
    for copy in copies:
        copy.wait()


def gather_slots(waves, few, fourier, sent):
    if not few:
        return [[lax.all_gather(fourier, "band")]]
    return [[lax.ppermute(sent, "band", [(i, i ^ k) for i in range(waves)])] for k in range(1, waves)]


def on_device(spectra, legendre, assignment, circle_longitudes, coriolis, weights, thickness):
    levels, coeffs = spectra.shape[1], spectra.shape[4]
    lats = legendre.shape[2]
    waves = lax.axis_size("band")
    spacing = coeffs // waves
    few = waves == 4
    pair = 2 * levels
    rows = levels * FIELDS * 2
    chunk = 256 if coeffs % 256 == 0 else LANES
    chunks = coeffs // chunk
    smem = pl.BlockSpec(memory_space=pltpu.SMEM)
    vmem = pl.BlockSpec(memory_space=pltpu.VMEM)
    hbm = pl.BlockSpec(memory_space=pltpu.HBM)
    anywhere = pl.BlockSpec(memory_space=pl.ANY)
    trim = max(2 * spacing - 20, 0) // 4 // LANES * LANES if few else 0

    def pinned(x, space):
        return pltpu.with_memory_space_constraint(x, space)

    signed, total = pl.pallas_call(
        functools.partial(spectra_kernel, spacing),
        out_shape=(
            pltpu.VMEM((2 * rows, coeffs), jnp.bfloat16),
            jax.ShapeDtypeStruct((2, coeffs), jnp.float32),
        ),
        in_specs=[hbm] * 3,
        out_specs=(vmem, vmem),
        scratch_shapes=[
            pltpu.SMEM(assignment.shape, jnp.int32),
            pltpu.SMEM(thickness.shape, jnp.float32),
            pltpu.VMEM(spectra.shape, jnp.bfloat16),
            pltpu.VMEM((rows, coeffs), jnp.float32),
            pltpu.SemaphoreType.DMA((3,)),
        ],
        compiler_params=pltpu.CompilerParams(vmem_limit_bytes=8 << 20),
        name="spectra",
    )(*(pinned(x, pltpu.HBM) for x in (assignment, thickness, spectra)))
    fourier = jnp.dot(signed, legendre[0], preferred_element_type=jnp.float32).astype(jnp.bfloat16)
    gathered = gather_slots(waves, few, fourier, fourier[:, trim:])
    same = (jnp.arange(chunk)[:, None] == jnp.arange(chunk)[None, :]).astype(jnp.bfloat16)
    turned = jnp.einsum("kbh,ba->kha", legendre[0].reshape(chunks, chunk, lats), same,
                        preferred_element_type=jnp.float32).astype(jnp.bfloat16)

    deep = ("fld", "sub")
    places = lax.axis_size(deep)
    belows = [lax.all_gather(total, deep)]

    half, angles, starts, aux_rows = aux_layout(waves, levels)
    aux = pl.pallas_call(
        functools.partial(aux_kernel, waves, few, spacing),
        out_shape=jax.ShapeDtypeStruct((aux_rows, lats), jnp.float32),
        in_specs=[smem, smem, vmem, vmem, vmem, vmem, anywhere],
        out_specs=vmem,
        compiler_params=pltpu.CompilerParams(vmem_limit_bytes=(16 if few else 48) << 20),
        name="tables",
    )(assignment, thickness, circle_longitudes.reshape(1, lats), coriolis, weights, spectra, fourier)

    operands = [fourier] + sum((gathered[at] for at in arrival(len(gathered))), []) + belows + [aux, pinned(turned, pltpu.VMEM)]
    return pl.pallas_call(
        functools.partial(direct_kernel, waves, few, len(belows), 0, trim, tuple(len(g) for g in gathered), True),
        out_shape=jax.ShapeDtypeStruct(spectra.shape, jnp.bfloat16),
        in_specs=[vmem] * len(operands),
        out_specs=anywhere,
        scratch_shapes=[
            pltpu.VMEM((TERMS * 2 * pair, lats), jnp.bfloat16),
            pltpu.VMEM(spectra.shape, jnp.bfloat16),
            pltpu.VMEM(total.shape, jnp.float32),
            pltpu.SemaphoreType.DMA((chunks,)),
        ],
        compiler_params=pltpu.CompilerParams(vmem_limit_bytes=(24 if few else 56) << 20),
        name="direct",
    )(*operands)


def solution(mesh):
    in_specs = (
        P(("member", "band"), ("fld", "sub"), None, None, None),
        P("band", None, None),
        P(),
        P(),
        P(),
        P(),
        P(("fld", "sub")),
    )
    out_specs = P(("member", "band"), ("fld", "sub"), None, None, None)
    return jax.shard_map(
        on_device, mesh=mesh, in_specs=in_specs, out_specs=out_specs, check_vma=False
    )
```

time: 26.4 us -> 19 us (0.72)
  blocking collectives: 0 us -> 5.22 us
  waiting for transfers between devices: 4.52 us -> 0.01 us
  starting transfers between devices: 9.98 us -> 5.68 us
  Pallas kernels: 8.08 us -> 4.92 us
  local copies, waits for them, and re-layouts: 3.44 us -> 0.78 us
  matrix products: 0 us -> 2.08 us
    all_gather x0 -> x1, blocking collectives: none -> 5.22 us  [on_device(): belows = [lax.all_gather(total, deep)]]
    ppermute x6 -> x3, waiting for transfers between devices: 4.52 us -> 0.01 us  [gather_slots(): lax.ppermute(sent, 'band', [(i, i ^ k) for i in range(waves)])]
    ppermute x6 -> x3, starting transfers between devices: 9.98 us -> 5.68 us  [gather_slots(): lax.ppermute(sent, 'band', [(i, i ^ k) for i in range(waves)])]
    pallas_call x2, Pallas kernels: 6.96 us -> 3.81 us  [the longest x1 2.58 us: on_device(): pl.pallas_call(functools.partial(direct_kernel, waves, few, len(belows),...]
    unnamed x18 -> x14, local copies, waits for them, and re-layouts: 3.43 us -> 0.75 us
    dot_general x0 -> x2, matrix products: none -> 2.08 us  [the longest x1 1.41 us: on_device(): jnp.einsum('kbh,ba->kha', legendre[0].reshape(chunks, chunk, lats), same,...]
  transfers between devices with their start and end apart: 6 -> 3, of which waited for: 4 -> 0; matrix products, arithmetic and copies ran while one was open for 0% -> 8% of each run, Pallas kernels for 4% -> 6%
where the time goes in v3:
time: 19 us; the launch traced here: 18.8 us
  starting transfers between devices  5.68 us (30%)
  blocking collectives  5.22 us (27%)
  Pallas kernels  4.92 us (26%)
  matrix products  2.08 us (11%)
  local copies, waits for them, and re-layouts  0.78 us (4%)
    ppermute x3, starting transfers between devices, gather_slots(): lax.ppermute(sent, 'band', [(i, i ^ k) for i in range(waves)])  5.68 us
    all_gather x1, blocking collectives, on_device(): belows = [lax.all_gather(total, deep)]  5.22 us
    pallas_call x1, Pallas kernels, on_device(): pl.pallas_call(functools.partial(direct_kernel, waves, few, len(belows),...  2.58 us
    dot_general x1, matrix products, on_device(): jnp.einsum('kbh,ba->kha', legendre[0].reshape(chunks, chunk, lats), same,...  1.41 us
    pallas_call x1, Pallas kernels, on_device(): pl.pallas_call(functools.partial(spectra_kernel, spacing), out_shape=(plt...  1.23 us
    pallas_call x1, Pallas kernels, on_device(): pl.pallas_call(functools.partial(aux_kernel, waves, few, spacing), out_sh...  1.11 us
    unnamed x14, local copies, waits for them, and re-layouts  0.75 us
    dot_general x1, matrix products, on_device(): jnp.dot(signed, legendre[0], preferred_element_type=jnp.float32)  0.68 us
  transfers between devices with their start and end apart: 3, of which 0 were waited for; matrix products, arithmetic and copies ran while one was open for 8% of the time, Pallas kernels for 6%

profile of v3, /device:TPU:0, one launch (start us, length us, event | category | flops | bytes accessed | tf_op | source)
XLA Modules:
  0.0 18.8 jit_solution(11432796128424284308)
XLA Ops:
  0.0 0.0 copy-start
  0.0 1.2 %spectra.1 = (bf16[48,1280]{1,0:T(8,128)(2,1)S(1)}, f32[2,1280]{1,0:T(2,128)S(1)}) custom-call(s32[4]{0:T(128)} %assign_ref.3, f32[4]{0:T(128)} %thick_ref.3, bf16[1,4,3,2,1280]{4,3,2,1,0:T(2,128)(2,1)} %spectra_ref.3), custom_call_target="tpu_custom_call" | custom-call | tf_op jit(solution)/shard_map/spectra/pallas_call | solution.py:364
  1.2 0.7 %copy-done = bf16[1,1280,1280]{2,1,0:T(8,128)(2,1)S(1)} copy-done((bf16[1,1280,1280]{2,1,0:T(8,128)(2,1)S(1)}, bf16[1,1280,1280]{2,1,0:T(8,128)(2,1)}, u32[]{:S(2)}) %copy-start) | copy-done | bytes 3276824
  2.0 0.7 %fusion.3.after_ref.refs_0_ = bf16[48,1280]{1,0:T(8,128)(2,1)S(1)} fusion(bf16[48,1280]{1,0:T(8,128)(2,1)S(1)} %get-tuple-element.7, bf16[1,1280,1280]{2,1,0:T(8,128)(2,1)S(1)} %copy-done), kind=kOutput, calls=%fused_computation.4 | convolution fusion | flops 157347840 | bytes 3522560 | tf_op jit(solution)/shard_map/dot_general | solution.py:382
  2.7 4.1 %collective-permute-start.2 = (bf16[48,1152]{1,0:T(8,128)(2,1)S(1)}, bf16[48,1152]{1,0:T(8,128)(2,1)S(1)}, u32[]{:S(2)}, u32[]{:S(2)}) collective-permute-start(bf16[48,1152]{1,0:T(8,128)(2,1)S(1)} %slice.4), channel_id=1, source_target_pairs={{0,8},{4,12},{8,0},{12,4},{1,9},{5,13},{9,1},{13,5},{2,10},{6,14},... | collective-permute-start | bytes 331784 | tf_op jit(solution)/shard_map/ppermute | solution.py:342
  6.8 1.6 %collective-permute-start.1 = (bf16[48,1152]{1,0:T(8,128)(2,1)S(1)}, bf16[48,1152]{1,0:T(8,128)(2,1)S(1)}, u32[]{:S(2)}, u32[]{:S(2)}) collective-permute-start(bf16[48,1152]{1,0:T(8,128)(2,1)S(1)} %slice.4), channel_id=1, source_target_pairs={{0,4},{4,0},{8,12},{12,8},{1,5},{5,1},{9,13},{13,9},{2,6},{6,2},{1... | collective-permute-start | bytes 331784 | tf_op jit(solution)/shard_map/ppermute | solution.py:342
  8.3 0.0 collective-permute-start
  8.3 0.0 copy-start.6
  8.4 0.0 copy-start.1
  8.4 0.0 copy-start.2
  8.4 0.0 copy-start.3
  8.4 0.0 copy-start.4
  8.4 0.0 copy-start.5
  8.4 1.4 %fusion.refs_6_ = bf16[5,1280,256]{2,1,0:T(8,128)(2,1)S(1)} fusion(bf16[5,256,1280]{2,1,0:T(8,128)(2,1)S(1)} %bitcast.14), kind=kOutput, calls=%fused_computation.1 | convolution fusion | flops 840564736 | bytes 6553600 | tf_op jit(solution)/shard_map/kbh,ba->kha/dot_general | solution.py:385
  9.8 0.0 copy-done.6
  9.8 0.0 copy-done.1
  9.8 0.0 copy-done.2
  9.9 0.0 copy-done.3
  9.9 0.0 copy-done.4
  9.9 0.0 copy-done.5
  9.9 1.1 %tables.1.refs_5_ = f32[120,1280]{1,0:T(8,128)S(1)} custom-call(s32[4]{0:T(128)S(1)} %copy-done.4, f32[4]{0:T(128)S(1)} %copy-done.5, s32[1,1280]{1,0:T(1,128)S(1)} %reshape.3.counts_ref, f32[2,1280]{1,0:T(2,128)S(1)} %copy-done.2, f32[2,1280]{1,0:T(2,128)S(1)} %copy-done.3, bf16[1,4,3,2,1280]{4,3,2,1,0:T(2,128)(2,1)S(1)} %copy-done.1, ...), custom_call_target="tpu_custom_call" | custom-call | tf_op jit(solution)/shard_map/tables/pallas_call | solution.py:393
  11.0 5.2 %all-gather.1.refs_4_ = f32[4,2,1280]{2,1,0:T(2,128)S(1)} all-gather(f32[1,2,1280]{2,1,0:T(2,128)S(1)} %bitcast.15), channel_id=2, replica_groups=mesh['member'=2,'band'=4,'fld'=2,'sub'=2] {'fld','sub'}, dimensions={0}, use_global_device_ids=true | all-gather | bytes 51200 | tf_op jit(solution)/shard_map/all_gather | solution.py:390
  16.2 0.0 collective-permute-done.2.refs_3_
  16.2 0.0 collective-permute-done.1.refs_2_
  16.2 0.0 collective-permute-done.refs_1_
  16.2 2.6 %direct.1 = bf16[1,4,3,2,1280]{4,3,2,1,0:T(2,128)(2,1)} custom-call(bf16[48,1280]{1,0:T(8,128)(2,1)S(1)} %fusion.3.after_ref.refs_0_, bf16[48,1152]{1,0:T(8,128)(2,1)S(1)} %collective-permute-done.refs_1_, bf16[48,1152]{1,0:T(8,128)(2,1)S(1)} %collective-permute-done.1.refs_2_, bf16[48,1152]{1,0:T(8,128)(2,1)S(1)} %collective-permute-done.2.refs_3_, ...), custom_call_target="tpu_custom_call" | custom-call | tf_op jit(solution)/shard_map/direct/pallas_call | solution.py:403
  (2 shorter events, 0.0 us)
Async XLA Ops:
  0.0 2.0 %copy-start = (bf16[1,1280,1280]{2,1,0:T(8,128)(2,1)S(1)}, bf16[1,1280,1280]{2,1,0:T(8,128)(2,1)}, u32[]{:S(2)}) copy-start(bf16[1,1280,1280]{2,1,0:T(8,128)(2,1)} %param.8) | copy-start | bytes 9830404
  2.7 13.6 %collective-permute-start.2 = (bf16[48,1152]{1,0:T(8,128)(2,1)S(1)}, bf16[48,1152]{1,0:T(8,128)(2,1)S(1)}, u32[]{:S(2)}, u32[]{:S(2)}) collective-permute-start(bf16[48,1152]{1,0:T(8,128)(2,1)S(1)} %slice.4), channel_id=1, source_target_pairs={{0,8},{4,12},{8,0},{12,4},{1,9},{5,13},{9,1},{13,5},{2,10},{6,14},... | collective-permute-start | bytes 331784 | tf_op jit(solution)/shard_map/ppermute | solution.py:342
  6.8 9.5 %collective-permute-start.1 = (bf16[48,1152]{1,0:T(8,128)(2,1)S(1)}, bf16[48,1152]{1,0:T(8,128)(2,1)S(1)}, u32[]{:S(2)}, u32[]{:S(2)}) collective-permute-start(bf16[48,1152]{1,0:T(8,128)(2,1)S(1)} %slice.4), channel_id=1, source_target_pairs={{0,4},{4,0},{8,12},{12,8},{1,5},{5,1},{9,13},{13,9},{2,6},{6,2},{1... | collective-permute-start | bytes 331784 | tf_op jit(solution)/shard_map/ppermute | solution.py:342
  8.3 7.9 %collective-permute-start = (bf16[48,1152]{1,0:T(8,128)(2,1)S(1)}, bf16[48,1152]{1,0:T(8,128)(2,1)S(1)}, u32[]{:S(2)}, u32[]{:S(2)}) collective-permute-start(bf16[48,1152]{1,0:T(8,128)(2,1)S(1)} %slice.4), channel_id=1, source_target_pairs={{0,12},{4,8},{8,4},{12,0},{1,13},{5,9},{9,5},{13,1},{2,14},{6,10},... | collective-permute-start | bytes 331784 | tf_op jit(solution)/shard_map/ppermute | solution.py:342
  8.3 1.5 %copy-start.6 = (s32[1280]{0:T(1024)S(1)}, s32[1280]{0:T(1024)}, u32[]{:S(2)}) copy-start(s32[1280]{0:T(1024)} %param.10) | copy-start | bytes 15364
  8.4 1.5 %copy-start.1 = (bf16[1,4,3,2,1280]{4,3,2,1,0:T(2,128)(2,1)S(1)}, bf16[1,4,3,2,1280]{4,3,2,1,0:T(2,128)(2,1)}, u32[]{:S(2)}) copy-start(bf16[1,4,3,2,1280]{4,3,2,1,0:T(2,128)(2,1)} %spectra_ref.3) | copy-start | bytes 184324
  8.4 1.5 %copy-start.2 = (f32[2,1280]{1,0:T(2,128)S(1)}, f32[2,1280]{1,0:T(2,128)}, u32[]{:S(2)}) copy-start(f32[2,1280]{1,0:T(2,128)} %planet_ref.1) | copy-start | bytes 30724
  8.4 1.5 %copy-start.3 = (f32[2,1280]{1,0:T(2,128)S(1)}, f32[2,1280]{1,0:T(2,128)}, u32[]{:S(2)}) copy-start(f32[2,1280]{1,0:T(2,128)} %quad_ref.1) | copy-start | bytes 30724
  8.4 1.5 %copy-start.4 = (s32[4]{0:T(128)S(1)}, s32[4]{0:T(128)}, u32[]{:S(2)}) copy-start(s32[4]{0:T(128)} %assign_ref.3) | copy-start | bytes 52
  8.4 1.5 %copy-start.5 = (f32[4]{0:T(128)S(1)}, f32[4]{0:T(128)}, u32[]{:S(2)}) copy-start(f32[4]{0:T(128)} %thick_ref.3) | copy-start | bytes 52

commit v4 on v3

--- a/solution.py
+++ b/solution.py
@@ -13,6 +13,7 @@
 TERMS = 4
 LANES = 128
 SUBLANES = 8
+STEP = 256
 
 
 def round_up(value, multiple):
@@ -23,23 +24,29 @@
     return lax.axis_index("band") ^ slot if few else slot
 
 
-def spectra_kernel(spacing, assign_ref, thick_ref, spectra_ref, signed_ref, total_ref,
-                   assign_scr, thick_scr, spectra_scr, rows_scr, sems):
-    copies = [
-        pltpu.make_async_copy(source, target, sems.at[i])
-        for i, (source, target) in enumerate(
-            ((assign_ref, assign_scr), (thick_ref, thick_scr), (spectra_ref, spectra_scr)))
+def inverse_kernel(spacing, chunk, assign_ref, spectra_ref, legendre_ref, fourier_ref, table_ref,
+                   assign_scr, spectra_scr, rows_scr, acc_scr, sems):
+    coeffs = table_ref.shape[0]
+    chunks = coeffs // chunk
+    heads = [
+        pltpu.make_async_copy(assign_ref, assign_scr, sems.at[chunks]),
+        pltpu.make_async_copy(spectra_ref, spectra_scr, sems.at[chunks + 1]),
     ]
-    for copy in copies:
+    for copy in heads:
         copy.start()
-    levels, coeffs = spectra_ref.shape[1], spectra_ref.shape[4]
+    copies = []
+    for i in range(chunks):
+        span = pl.ds(i * chunk, chunk)
+        copies.append(pltpu.make_async_copy(legendre_ref.at[0, span], table_ref.at[span], sems.at[i]))
+        copies[-1].start()
+    levels = spectra_ref.shape[1]
     rows = levels * FIELDS * 2
     out_rows = 2 * rows
     place = lax.broadcasted_iota(jnp.int32, (out_rows, rows), 0)
     source = lax.broadcasted_iota(jnp.int32, (out_rows, rows), 1)
     chosen = (place // (2 * levels) == source % (2 * FIELDS)) & (place % levels == source // (2 * FIELDS))
     move = jnp.where(chosen, 1.0, 0.0).astype(jnp.bfloat16)
-    for copy in copies:
+    for copy in heads:
         copy.wait()
     wave = spacing * assign_scr[lax.axis_index("band")]
     for level in range(levels):
@@ -53,13 +60,17 @@
     spread = jnp.dot(move, masked, preferred_element_type=jnp.float32)
     odd = lax.broadcasted_iota(jnp.int32, (out_rows, coeffs), 1) % 2 == 1
     south = lax.broadcasted_iota(jnp.int32, (out_rows, coeffs), 0) // levels % 2 == 1
-    signed_ref[...] = jnp.where(odd & south, -spread, spread).astype(jnp.bfloat16)
-    for r in range(2):
-        at = (2 * 2 + r) * 2 * levels
-        total = spread[at:at + 1] * thick_scr[0]
-        for level in range(1, levels):
-            total += spread[at + level:at + level + 1] * thick_scr[level]
-        total_ref[r:r + 1, :] = total
+    signed = jnp.where(odd & south, -spread, spread).astype(jnp.bfloat16)
+    for i in range(chunks):
+        copies[i].wait()
+        span = slice(i * chunk, (i + 1) * chunk)
+        product = jnp.dot(signed[:, span], table_ref[span, :], preferred_element_type=jnp.float32)
+        if i == 0:
+            acc_scr[...] = product
+        elif i < chunks - 1:
+            acc_scr[...] += product
+        else:
+            fourier_ref[...] = (acc_scr[...] + product).astype(jnp.bfloat16)
 
 
 def cos_sin(turns):
@@ -88,7 +99,7 @@
 
 
 def aux_kernel(waves, few, spacing, assign_ref, thick_ref, counts_ref, planet_ref, quad_ref, spectra_ref, after_ref,
-               aux_ref):
+               aux_ref, total_ref):
     del after_ref
     levels, coeffs = spectra_ref.shape[1], spectra_ref.shape[4]
     pair = 2 * levels
@@ -150,6 +161,7 @@
     for r in range(2):
         at = starts["column"] + r * pair
         aux_ref[at:at + pair, :] = columns[r]
+        total_ref[r:r + 1, :] = columns[r][0:1]
     aux_ref[starts["keep"]:starts["keep"] + 2, :] = jnp.where(keep, 1.0, 0.0)
     degree = wave + coeff[0:1]
     truncation = coeffs - 1
@@ -161,50 +173,36 @@
     return (2, 0, 1) if slots == 3 else range(slots)
 
 
-def direct_kernel(waves, few, belows, begin, trim, parts, last, *refs):
-    own_ref, refs = refs[0], refs[1:]
-    slot_refs = [None] * len(parts)
-    for at in arrival(len(parts)):
-        slot_refs[at] = refs[:parts[at]]
-        refs = refs[parts[at]:]
-    below_refs, refs = refs[:belows], refs[belows:]
-    aux_ref, table_ref, refs = refs[0], refs[1], refs[2:]
-    if begin > 0:
-        earlier_ref, refs = refs[0], refs[1:]
-    if last:
-        out_ref, back_scr, out_scr, below_scr, sems = refs
-        place = lax.axis_index(("fld", "sub"))
-        (below_ref,) = below_refs
-        below = jnp.zeros(below_ref.shape[1:], jnp.float32)
-        for p in range(1, below_ref.shape[0]):
-            below += jnp.where(place < p, below_ref[p], 0.0)
-        below_scr[...] = below
-        levels = out_scr.shape[1]
-    else:
-        partial_ref, back_scr = refs
-        levels = back_scr.shape[0] // (4 * TERMS)
+def direct_kernel(waves, few, trim, own_ref, *refs):
+    count = waves - 1 if few else 1
+    slot_refs = [None] * count
+    for at, ref in zip(arrival(count), refs):
+        slot_refs[at] = ref
+    below_ref, aux_ref, table_ref, out_ref, back_scr, acc_scr, out_scr, below_scr, sems = refs[count:]
+    below = jnp.zeros(below_ref.shape[1:], jnp.float32)
+    for p in range(1, below_ref.shape[0]):
+        below += jnp.where(lax.axis_index(("fld", "sub")) < p, below_ref[p], 0.0)
+    below_scr[...] = below
+    levels = out_scr.shape[1]
     chunks, lats, chunk = table_ref.shape
     half, angles, starts, _ = aux_layout(waves, levels)
     pair = 2 * levels
     zero = jnp.zeros((pair, LANES), jnp.float32)
 
     def products(lane, slots):
-        here = pl.ds(lane, LANES)
-        lanes = pl.ds(begin + lane, LANES)
+        lanes = pl.ds(lane, LANES)
         coefs = []
         for k in range(slots):
             fields = []
             for field in range(FIELDS):
                 rows = slice(field * 2 * pair, (field + 1) * 2 * pair)
                 if not few:
-                    both = slot_refs[0][0][k, rows, here].astype(jnp.float32)
+                    both = slot_refs[0][k, rows, lanes].astype(jnp.float32)
                 elif k == 0:
-                    both = own_ref[rows, here].astype(jnp.float32)
+                    both = own_ref[rows, lanes].astype(jnp.float32)
                 else:
                     there = pl.ds(lane - trim, LANES)
-                    both = slot_refs[k - 1][0][rows, there].astype(jnp.float32)
-                    for ref in slot_refs[k - 1][1:]:
-                        both = both + ref[rows, there].astype(jnp.float32)
+                    both = slot_refs[k - 1][rows, there].astype(jnp.float32)
                 fields.append((both[:pair], both[pair:]))
             coefs.append(fields)
         planet = aux_ref[starts["planet"]:starts["planet"] + pair, lanes]
@@ -274,18 +272,32 @@
         quad = aux_ref[starts["quad"]:starts["quad"] + pair, lanes]
         for q in range(TERMS):
             both = jnp.concatenate([sums[2 * q] * quad, sums[2 * q + 1] * quad], axis=0)
-            back_scr[q * 2 * pair:(q + 1) * 2 * pair, here] = both.astype(jnp.bfloat16)
-
-    for block in range(trim // LANES):
-        products(block * LANES, 1)
-
-    def lat_block(block, carry):
-        products(pl.multiple_of(trim + block * LANES, LANES), waves)
-        return carry
-
-    lax.fori_loop(0, (lats - trim) // LANES, lat_block, 0)
-
-    back = back_scr[...]
+            back_scr[q * 2 * pair:(q + 1) * 2 * pair, lanes] = both.astype(jnp.bfloat16)
+
+    def share(first, size):
+        for i in range(chunks):
+            span = slice(i * chunk, (i + 1) * chunk)
+            product = jnp.dot(back_scr[:, first:first + size], table_ref[i, first:first + size, :],
+                              preferred_element_type=jnp.float32)
+            if first == 0:
+                acc_scr[:, span] = product
+            else:
+                acc_scr[:, span] += product
+
+    if few:
+        step = STEP if lats % STEP == 0 else LANES
+        for first in range(0, lats, step):
+            for lane in range(first, first + step, LANES):
+                products(lane, waves if lane >= trim else 1)
+            share(first, step)
+    else:
+        def lat_block(block, carry):
+            products(pl.multiple_of(block * LANES, LANES), waves)
+            return carry
+
+        lax.fori_loop(0, lats // LANES, lat_block, 0)
+        share(0, lats)
+
     groups = 2 * FIELDS
     place = lax.broadcasted_iota(jnp.int32, (levels * groups, groups * pair), 0)
     source = lax.broadcasted_iota(jnp.int32, (levels * groups, groups * pair), 1)
@@ -294,18 +306,12 @@
     copies = []
     for i in range(chunks):
         span = slice(i * chunk, (i + 1) * chunk)
-        product = jnp.dot(back, table_ref[i], preferred_element_type=jnp.float32)
-        if begin > 0:
-            product = product + earlier_ref[:, span]
-        if not last:
-            partial_ref[:, span] = product
-            continue
         odd = lax.broadcasted_iota(jnp.int32, (pair, chunk), 1) % 2 == 1
         laplace = aux_ref[starts["laplace"]:starts["laplace"] + 1, span]
 
         def both_rows(q, r):
             at = (2 * q + r) * pair
-            rows = product[at:at + pair]
+            rows = acc_scr[at:at + pair, span]
             south = pltpu.roll(rows, levels, 0)
             return rows + jnp.where(odd, -south, south)
 
@@ -316,8 +322,7 @@
                     value = both_rows(0, r)
                 elif field == 1:
                     at = starts["column"] + r * pair
-                    column = aux_ref[at:at + pair, span]
-                    column = column + below_scr[r:r + 1, span]
+                    column = aux_ref[at:at + pair, span] + below_scr[r:r + 1, span]
                     value = both_rows(1, r) + laplace * (column + both_rows(2, r))
                 else:
                     value = both_rows(3, r)
@@ -338,8 +343,8 @@
 
 def gather_slots(waves, few, fourier, sent):
     if not few:
-        return [[lax.all_gather(fourier, "band")]]
-    return [[lax.ppermute(sent, "band", [(i, i ^ k) for i in range(waves)])] for k in range(1, waves)]
+        return [lax.all_gather(fourier, "band")]
+    return [lax.ppermute(sent, "band", [(i, i ^ k) for i in range(waves)]) for k in range(1, waves)]
 
 
 def on_device(spectra, legendre, assignment, circle_longitudes, coriolis, weights, thickness):
@@ -361,52 +366,53 @@
     def pinned(x, space):
         return pltpu.with_memory_space_constraint(x, space)
 
-    signed, total = pl.pallas_call(
-        functools.partial(spectra_kernel, spacing),
+    fourier, table = pl.pallas_call(
+        functools.partial(inverse_kernel, spacing, chunk),
         out_shape=(
-            pltpu.VMEM((2 * rows, coeffs), jnp.bfloat16),
-            jax.ShapeDtypeStruct((2, coeffs), jnp.float32),
+            jax.ShapeDtypeStruct((2 * rows, lats), jnp.bfloat16),
+            pltpu.VMEM((coeffs, lats), jnp.bfloat16),
         ),
         in_specs=[hbm] * 3,
         out_specs=(vmem, vmem),
         scratch_shapes=[
             pltpu.SMEM(assignment.shape, jnp.int32),
-            pltpu.SMEM(thickness.shape, jnp.float32),
             pltpu.VMEM(spectra.shape, jnp.bfloat16),
             pltpu.VMEM((rows, coeffs), jnp.float32),
-            pltpu.SemaphoreType.DMA((3,)),
+            pltpu.VMEM((2 * rows, lats), jnp.float32),
+            pltpu.SemaphoreType.DMA((chunks + 2,)),
         ],
-        compiler_params=pltpu.CompilerParams(vmem_limit_bytes=8 << 20),
-        name="spectra",
-    )(*(pinned(x, pltpu.HBM) for x in (assignment, thickness, spectra)))
-    fourier = jnp.dot(signed, legendre[0], preferred_element_type=jnp.float32).astype(jnp.bfloat16)
+        compiler_params=pltpu.CompilerParams(vmem_limit_bytes=16 << 20),
+        name="inverse",
+    )(*(pinned(x, pltpu.HBM) for x in (assignment, spectra, legendre)))
     gathered = gather_slots(waves, few, fourier, fourier[:, trim:])
     same = (jnp.arange(chunk)[:, None] == jnp.arange(chunk)[None, :]).astype(jnp.bfloat16)
-    turned = jnp.einsum("kbh,ba->kha", legendre[0].reshape(chunks, chunk, lats), same,
+    turned = jnp.einsum("kbh,ba->kha", table.reshape(chunks, chunk, lats), same,
                         preferred_element_type=jnp.float32).astype(jnp.bfloat16)
 
-    deep = ("fld", "sub")
-    places = lax.axis_size(deep)
-    belows = [lax.all_gather(total, deep)]
-
     half, angles, starts, aux_rows = aux_layout(waves, levels)
-    aux = pl.pallas_call(
+    aux, total = pl.pallas_call(
         functools.partial(aux_kernel, waves, few, spacing),
-        out_shape=jax.ShapeDtypeStruct((aux_rows, lats), jnp.float32),
+        out_shape=(
+            jax.ShapeDtypeStruct((aux_rows, lats), jnp.float32),
+            jax.ShapeDtypeStruct((2, coeffs), jnp.float32),
+        ),
         in_specs=[smem, smem, vmem, vmem, vmem, vmem, anywhere],
-        out_specs=vmem,
+        out_specs=(vmem, vmem),
         compiler_params=pltpu.CompilerParams(vmem_limit_bytes=(16 if few else 48) << 20),
         name="tables",
     )(assignment, thickness, circle_longitudes.reshape(1, lats), coriolis, weights, spectra, fourier)
 
-    operands = [fourier] + sum((gathered[at] for at in arrival(len(gathered))), []) + belows + [aux, pinned(turned, pltpu.VMEM)]
+    totals = lax.all_gather(total, ("fld", "sub"))
+
+    operands = [fourier] + [gathered[at] for at in arrival(len(gathered))] + [totals, aux, pinned(turned, pltpu.VMEM)]
     return pl.pallas_call(
-        functools.partial(direct_kernel, waves, few, len(belows), 0, trim, tuple(len(g) for g in gathered), True),
+        functools.partial(direct_kernel, waves, few, trim),
         out_shape=jax.ShapeDtypeStruct(spectra.shape, jnp.bfloat16),
         in_specs=[vmem] * len(operands),
         out_specs=anywhere,
         scratch_shapes=[
             pltpu.VMEM((TERMS * 2 * pair, lats), jnp.bfloat16),
+            pltpu.VMEM((TERMS * 2 * pair, coeffs), jnp.float32),
             pltpu.VMEM(spectra.shape, jnp.bfloat16),
             pltpu.VMEM(total.shape, jnp.float32),
             pltpu.SemaphoreType.DMA((chunks,)),

time: 19 us -> 17.4 us (0.916)
  matrix products: 2.08 us -> 1.07 us
  local copies, waits for them, and re-layouts: 0.78 us -> 0.05 us
    dot_general x2 -> x1, matrix products: 2.08 us -> 1.07 us  [on_device(): jnp.einsum('kbh,ba->kha', table.reshape(chunks, chunk, lats), same, prefe...]
    unnamed x14 -> x12, local copies, waits for them, and re-layouts: 0.75 us -> 0.03 us
  transfers between devices with their start and end apart: 3 -> 3, of which waited for: 0 -> 0; matrix products, arithmetic and copies ran while one was open for 8% -> 6% of each run, Pallas kernels for 6% -> 6%
where the time goes in v4:
time: 17.4 us; the launch traced here: 17.2 us
  starting transfers between devices  5.68 us (33%)
  blocking collectives  5.22 us (30%)
  Pallas kernels  5.08 us (29%)
  matrix products  1.07 us (6%)
    ppermute x3, starting transfers between devices, gather_slots(): lax.ppermute(sent, 'band', [(i, i ^ k) for i in range(waves)])  5.68 us
    all_gather x1, blocking collectives, on_device(): totals = lax.all_gather(total, ('fld', 'sub'))  5.22 us
    pallas_call x1, Pallas kernels, on_device(): pl.pallas_call(functools.partial(inverse_kernel, spacing, chunk), out_sha...  2.22 us
    pallas_call x1, Pallas kernels, on_device(): pl.pallas_call(functools.partial(direct_kernel, waves, few, trim), out_sh...  1.74 us
    pallas_call x1, Pallas kernels, on_device(): pl.pallas_call(functools.partial(aux_kernel, waves, few, spacing), out_sh...  1.12 us
    dot_general x1, matrix products, on_device(): jnp.einsum('kbh,ba->kha', table.reshape(chunks, chunk, lats), same, prefe...  1.07 us
  transfers between devices with their start and end apart: 3, of which 0 were waited for; matrix products, arithmetic and copies ran while one was open for 6% of the time, Pallas kernels for 6%

profile of v4, /device:TPU:0, one launch (start us, length us, event | category | flops | bytes accessed | tf_op | source)
XLA Modules:
  0.0 17.2 jit_solution(5107765215029786372)
XLA Ops:
  0.0 2.2 %inverse.1 = (bf16[48,1280]{1,0:T(8,128)(2,1)S(1)}, bf16[1280,1280]{1,0:T(8,128)(2,1)S(1)}) custom-call(s32[4]{0:T(128)} %assign_ref.3, bf16[1,4,3,2,1280]{4,3,2,1,0:T(2,128)(2,1)} %spectra_ref.3, bf16[1,1280,1280]{2,1,0:T(8,128)(2,1)} %legendre_ref.1), custom_call_target="tpu_custom_call" | custom-call | tf_op jit(solution)/shard_map/inverse/pallas_call | solution.py:369
  2.2 4.1 %collective-permute-start.2 = (bf16[48,1152]{1,0:T(8,128)(2,1)S(1)}, bf16[48,1152]{1,0:T(8,128)(2,1)S(1)}, u32[]{:S(2)}, u32[]{:S(2)}) collective-permute-start(bf16[48,1152]{1,0:T(8,128)(2,1)S(1)} %slice.3), channel_id=1, source_target_pairs={{0,8},{4,12},{8,0},{12,4},{1,9},{5,13},{9,1},{13,5},{2,10},{6,14},... | collective-permute-start | bytes 331784 | tf_op jit(solution)/shard_map/ppermute | solution.py:347
  6.3 1.6 %collective-permute-start.1 = (bf16[48,1152]{1,0:T(8,128)(2,1)S(1)}, bf16[48,1152]{1,0:T(8,128)(2,1)S(1)}, u32[]{:S(2)}, u32[]{:S(2)}) collective-permute-start(bf16[48,1152]{1,0:T(8,128)(2,1)S(1)} %slice.3), channel_id=1, source_target_pairs={{0,4},{4,0},{8,12},{12,8},{1,5},{5,1},{9,13},{13,9},{2,6},{6,2},{1... | collective-permute-start | bytes 331784 | tf_op jit(solution)/shard_map/ppermute | solution.py:347
  7.9 0.0 collective-permute-start
  7.9 0.0 copy-start.5
  7.9 0.0 copy-start
  7.9 0.0 copy-start.1
  7.9 0.0 copy-start.2
  8.0 0.0 copy-start.3
  8.0 0.0 copy-start.4
  8.0 1.1 %convolution_convert_fusion.refs_5_ = bf16[5,1280,256]{2,1,0:T(8,128)(2,1)S(1)} fusion(bf16[5,256,1280]{2,1,0:T(8,128)(2,1)S(1)} %bitcast.6), kind=kOutput, calls=%fused_computation | convolution fusion | flops 840564736 | bytes 6553600 | tf_op jit(solution)/shard_map/kbh,ba->kha/dot_general | solution.py:389
  9.1 0.0 copy-done.5
  9.1 0.0 copy-done
  9.1 0.0 copy-done.1
  9.1 0.0 copy-done.2
  9.1 0.0 copy-done.3
  9.1 0.0 copy-done.4
  9.1 1.1 %tables.1 = (f32[120,1280]{1,0:T(8,128)S(1)}, f32[2,1280]{1,0:T(2,128)S(1)}) custom-call(s32[4]{0:T(128)S(1)} %copy-done.3, f32[4]{0:T(128)S(1)} %copy-done.4, s32[1,1280]{1,0:T(1,128)S(1)} %reshape.6.counts_ref, f32[2,1280]{1,0:T(2,128)S(1)} %copy-done.1, f32[2,1280]{1,0:T(2,128)S(1)} %copy-done.2, bf16[1,4,3,2,1280]{4,3,2,1,0:T(2,128)(2,1)S(1)} %copy-done, ...), custom_call_target="tpu_custom_call" | custom-call | tf_op jit(solution)/shard_map/tables/pallas_call | solution.py:393
  10.3 5.2 %all-gather.1.refs_3_ = f32[4,2,1280]{2,1,0:T(2,128)S(1)} all-gather(f32[1,2,1280]{2,1,0:T(2,128)S(1)} %bitcast.7), channel_id=2, replica_groups=mesh['member'=2,'band'=4,'fld'=2,'sub'=2] {'fld','sub'}, dimensions={0}, use_global_device_ids=true | all-gather | bytes 51200 | tf_op jit(solution)/shard_map/all_gather | solution.py:405
  15.5 0.0 collective-permute-done.2.refs_2_
  15.5 0.0 collective-permute-done.1.refs_1_
  15.5 0.0 collective-permute-done.refs_0_
  15.5 1.7 %direct.1 = bf16[1,4,3,2,1280]{4,3,2,1,0:T(2,128)(2,1)} custom-call(bf16[48,1280]{1,0:T(8,128)(2,1)S(1)} %get-tuple-element.9.after_ref.own_ref, bf16[48,1152]{1,0:T(8,128)(2,1)S(1)} %collective-permute-done.refs_0_, bf16[48,1152]{1,0:T(8,128)(2,1)S(1)} %collective-permute-done.1.refs_1_, bf16[48,1152]{1,0:T(8,128)(2,1)S(1)} %collective-permute-done.2.refs_2_, ...), custom_call_target="tpu_custom_call" | custom-call | tf_op jit(solution)/shard_map/direct/pallas_call | solution.py:408
  (2 shorter events, 0.0 us)
Async XLA Ops:
  2.2 13.2 %collective-permute-start.2 = (bf16[48,1152]{1,0:T(8,128)(2,1)S(1)}, bf16[48,1152]{1,0:T(8,128)(2,1)S(1)}, u32[]{:S(2)}, u32[]{:S(2)}) collective-permute-start(bf16[48,1152]{1,0:T(8,128)(2,1)S(1)} %slice.3), channel_id=1, source_target_pairs={{0,8},{4,12},{8,0},{12,4},{1,9},{5,13},{9,1},{13,5},{2,10},{6,14},... | collective-permute-start | bytes 331784 | tf_op jit(solution)/shard_map/ppermute | solution.py:347
  6.3 9.1 %collective-permute-start.1 = (bf16[48,1152]{1,0:T(8,128)(2,1)S(1)}, bf16[48,1152]{1,0:T(8,128)(2,1)S(1)}, u32[]{:S(2)}, u32[]{:S(2)}) collective-permute-start(bf16[48,1152]{1,0:T(8,128)(2,1)S(1)} %slice.3), channel_id=1, source_target_pairs={{0,4},{4,0},{8,12},{12,8},{1,5},{5,1},{9,13},{13,9},{2,6},{6,2},{1... | collective-permute-start | bytes 331784 | tf_op jit(solution)/shard_map/ppermute | solution.py:347
  7.9 7.5 %collective-permute-start = (bf16[48,1152]{1,0:T(8,128)(2,1)S(1)}, bf16[48,1152]{1,0:T(8,128)(2,1)S(1)}, u32[]{:S(2)}, u32[]{:S(2)}) collective-permute-start(bf16[48,1152]{1,0:T(8,128)(2,1)S(1)} %slice.3), channel_id=1, source_target_pairs={{0,12},{4,8},{8,4},{12,0},{1,13},{5,9},{9,5},{13,1},{2,14},{6,10},... | collective-permute-start | bytes 331784 | tf_op jit(solution)/shard_map/ppermute | solution.py:347
  7.9 1.1 %copy-start.5 = (s32[1280]{0:T(1024)S(1)}, s32[1280]{0:T(1024)}, u32[]{:S(2)}) copy-start(s32[1280]{0:T(1024)} %param.10) | copy-start | bytes 15364
  7.9 1.1 %copy-start = (bf16[1,4,3,2,1280]{4,3,2,1,0:T(2,128)(2,1)S(1)}, bf16[1,4,3,2,1280]{4,3,2,1,0:T(2,128)(2,1)}, u32[]{:S(2)}) copy-start(bf16[1,4,3,2,1280]{4,3,2,1,0:T(2,128)(2,1)} %spectra_ref.3) | copy-start | bytes 184324
  7.9 1.2 %copy-start.1 = (f32[2,1280]{1,0:T(2,128)S(1)}, f32[2,1280]{1,0:T(2,128)}, u32[]{:S(2)}) copy-start(f32[2,1280]{1,0:T(2,128)} %planet_ref.1) | copy-start | bytes 30724
  7.9 1.2 %copy-start.2 = (f32[2,1280]{1,0:T(2,128)S(1)}, f32[2,1280]{1,0:T(2,128)}, u32[]{:S(2)}) copy-start(f32[2,1280]{1,0:T(2,128)} %quad_ref.1) | copy-start | bytes 30724
  8.0 1.2 %copy-start.3 = (s32[4]{0:T(128)S(1)}, s32[4]{0:T(128)}, u32[]{:S(2)}) copy-start(s32[4]{0:T(128)} %assign_ref.3) | copy-start | bytes 52
  8.0 1.2 %copy-start.4 = (f32[4]{0:T(128)S(1)}, f32[4]{0:T(128)}, u32[]{:S(2)}) copy-start(f32[4]{0:T(128)} %thick_ref.1) | copy-start | bytes 52

commit v5 on v4

--- a/solution.py
+++ b/solution.py
@@ -123,29 +123,49 @@
     j = lax.broadcasted_iota(jnp.int32, (angles, lats), 0).astype(jnp.float32)
     share = jnp.where(2.0 * j <= number, jnp.where((j == 0.0) | (2.0 * j == number), 1.0, 2.0), 0.0) / number
 
+    def trig(multiple):
+        turn = j * multiple
+        turn = turn - number * jnp.floor((turn + 0.5) / number)
+        turn = jnp.where(2.0 * turn > number, turn - number, turn) / number
+        return cos_sin(turn)
+
+    if few:
+        harmonics = [(jnp.ones_like(j), jnp.zeros_like(j)), trig(1.0)]
+        for _ in range(2, waves):
+            (cosine, sine), (once, across) = harmonics[-1], harmonics[1]
+            harmonics.append((cosine * once - sine * across, sine * once + cosine * across))
+
     def slot(k, carry):
         harmonic = assign_ref[slot_position(waves, few, k)]
-        turn = j * harmonic.astype(jnp.float32)
-        turn = turn - number * jnp.floor((turn + 0.5) / number)
-        turn = jnp.where(2.0 * turn > number, turn - number, turn) / number
-        cosine, sine = cos_sin(turn)
+        if few:
+            cosine, sine = harmonics[0]
+            for a in range(1, waves):
+                cosine = jnp.where(harmonic == a, harmonics[a][0], cosine)
+                sine = jnp.where(harmonic == a, harmonics[a][1], sine)
+        else:
+            cosine, sine = trig(harmonic.astype(jnp.float32))
         seen = (2 * spacing * harmonic).astype(jnp.float32) < counts
         gain = jnp.where(seen, jnp.where(harmonic == 0, 1.0, 2.0), 0.0)
-        at = pl.ds(pl.multiple_of(starts["cosine"] + k * angles, SUBLANES), angles)
-        aux_ref[at, :] = cosine * gain
-        at = pl.ds(pl.multiple_of(starts["sine"] + k * angles, SUBLANES), angles)
-        aux_ref[at, :] = -sine * gain
+        for name, value in (("cosine", cosine * gain), ("sine", -sine * gain)):
+            at = starts[name] + k * angles
+            aux_ref[pl.ds(at if few else pl.multiple_of(at, SUBLANES), angles), :] = value
         mine = share * jnp.where(seen, 1.0, 0.0)
-        own = k == (0 if few else lax.axis_index("band"))
-
-        @pl.when(own)
-        def _():
+
+        def keep_own():
             aux_ref[starts["own_cosine"]:starts["own_cosine"] + angles, :] = cosine * mine
             aux_ref[starts["own_sine"]:starts["own_sine"] + angles, :] = -sine * mine
 
+        if not few:
+            pl.when(k == lax.axis_index("band"))(keep_own)
+        elif k == 0:
+            keep_own()
         return carry
 
-    lax.fori_loop(0, waves, slot, 0)
+    if few:
+        for k in range(waves):
+            slot(k, 0)
+    else:
+        lax.fori_loop(0, waves, slot, 0)
     north = lax.broadcasted_iota(jnp.int32, (pair, lats), 0) < levels
     for name, ref in (("planet", planet_ref), ("quad", quad_ref)):
         aux_ref[starts[name]:starts[name] + pair, :] = jnp.where(north, ref[0:1, :], ref[1:2, :])

time: 17.4 us -> 17.2 us (0.989)
  Pallas kernels: 5.08 us -> 4.78 us
    pallas_call x1, Pallas kernels: 1.12 us -> 0.82 us  [on_device(): pl.pallas_call(functools.partial(aux_kernel, waves, few, spacing), out_sh...]
  transfers between devices with their start and end apart: 3 -> 3, of which waited for: 0 -> 1; matrix products, arithmetic and copies ran while one was open for 6% -> 6% of each run, Pallas kernels for 6% -> 5%
where the time goes in v5:
time: 17.2 us; the launch traced here: 17.1 us
  starting transfers between devices  5.68 us (33%)
  blocking collectives  5.22 us (30%)
  Pallas kernels  4.78 us (28%)
  matrix products  1.07 us (6%)
    ppermute x3, starting transfers between devices, gather_slots(): lax.ppermute(sent, 'band', [(i, i ^ k) for i in range(waves)])  5.68 us
    all_gather x1, blocking collectives, on_device(): totals = lax.all_gather(total, ('fld', 'sub'))  5.22 us
    pallas_call x1, Pallas kernels, on_device(): pl.pallas_call(functools.partial(inverse_kernel, spacing, chunk), out_sha...  2.22 us
    pallas_call x1, Pallas kernels, on_device(): pl.pallas_call(functools.partial(direct_kernel, waves, few, trim), out_sh...  1.74 us
    dot_general x1, matrix products, on_device(): jnp.einsum('kbh,ba->kha', table.reshape(chunks, chunk, lats), same, prefe...  1.07 us
    pallas_call x1, Pallas kernels, on_device(): pl.pallas_call(functools.partial(aux_kernel, waves, few, spacing), out_sh...  0.82 us
  transfers between devices with their start and end apart: 3, of which 1 were waited for; matrix products, arithmetic and copies ran while one was open for 6% of the time, Pallas kernels for 5%

profile of v5, /device:TPU:0, one launch (start us, length us, event | category | flops | bytes accessed | tf_op | source)
XLA Modules:
  0.0 17.1 jit_solution(15496635846332439747)
XLA Ops:
  0.0 2.2 %inverse.1 = (bf16[48,1280]{1,0:T(8,128)(2,1)S(1)}, bf16[1280,1280]{1,0:T(8,128)(2,1)S(1)}) custom-call(s32[4]{0:T(128)} %assign_ref.3, bf16[1,4,3,2,1280]{4,3,2,1,0:T(2,128)(2,1)} %spectra_ref.3, bf16[1,1280,1280]{2,1,0:T(8,128)(2,1)} %legendre_ref.1), custom_call_target="tpu_custom_call" | custom-call | tf_op jit(solution)/shard_map/inverse/pallas_call | solution.py:389
  2.2 4.1 %collective-permute-start.2 = (bf16[48,1152]{1,0:T(8,128)(2,1)S(1)}, bf16[48,1152]{1,0:T(8,128)(2,1)S(1)}, u32[]{:S(2)}, u32[]{:S(2)}) collective-permute-start(bf16[48,1152]{1,0:T(8,128)(2,1)S(1)} %slice.3), channel_id=1, source_target_pairs={{0,8},{4,12},{8,0},{12,4},{1,9},{5,13},{9,1},{13,5},{2,10},{6,14},... | collective-permute-start | bytes 331784 | tf_op jit(solution)/shard_map/ppermute | solution.py:367
  6.3 1.6 %collective-permute-start.1 = (bf16[48,1152]{1,0:T(8,128)(2,1)S(1)}, bf16[48,1152]{1,0:T(8,128)(2,1)S(1)}, u32[]{:S(2)}, u32[]{:S(2)}) collective-permute-start(bf16[48,1152]{1,0:T(8,128)(2,1)S(1)} %slice.3), channel_id=1, source_target_pairs={{0,4},{4,0},{8,12},{12,8},{1,5},{5,1},{9,13},{13,9},{2,6},{6,2},{1... | collective-permute-start | bytes 331784 | tf_op jit(solution)/shard_map/ppermute | solution.py:367
  7.9 0.0 collective-permute-start
  7.9 0.0 copy-start.5
  7.9 0.0 copy-start
  7.9 0.0 copy-start.1
  7.9 0.0 copy-start.2
  8.0 0.0 copy-start.3
  8.0 0.0 copy-start.4
  8.0 1.1 %convolution_convert_fusion.refs_5_ = bf16[5,1280,256]{2,1,0:T(8,128)(2,1)S(1)} fusion(bf16[5,256,1280]{2,1,0:T(8,128)(2,1)S(1)} %bitcast.6), kind=kOutput, calls=%fused_computation | convolution fusion | flops 840564736 | bytes 6553600 | tf_op jit(solution)/shard_map/kbh,ba->kha/dot_general | solution.py:409
  9.1 0.0 copy-done.5
  9.1 0.0 copy-done
  9.1 0.0 copy-done.1
  9.1 0.0 copy-done.2
  9.1 0.0 copy-done.3
  9.1 0.0 copy-done.4
  9.1 0.8 %tables.1 = (f32[120,1280]{1,0:T(8,128)S(1)}, f32[2,1280]{1,0:T(2,128)S(1)}) custom-call(s32[4]{0:T(128)S(1)} %copy-done.3, f32[4]{0:T(128)S(1)} %copy-done.4, s32[1,1280]{1,0:T(1,128)S(1)} %reshape.6.counts_ref, f32[2,1280]{1,0:T(2,128)S(1)} %copy-done.1, f32[2,1280]{1,0:T(2,128)S(1)} %copy-done.2, bf16[1,4,3,2,1280]{4,3,2,1,0:T(2,128)(2,1)S(1)} %copy-done, ...), custom_call_target="tpu_custom_call" | custom-call | tf_op jit(solution)/shard_map/tables/pallas_call | solution.py:413
  10.0 5.2 %all-gather.1.refs_3_ = f32[4,2,1280]{2,1,0:T(2,128)S(1)} all-gather(f32[1,2,1280]{2,1,0:T(2,128)S(1)} %bitcast.7), channel_id=2, replica_groups=mesh['member'=2,'band'=4,'fld'=2,'sub'=2] {'fld','sub'}, dimensions={0}, use_global_device_ids=true | all-gather | bytes 51200 | tf_op jit(solution)/shard_map/all_gather | solution.py:425
  15.2 0.0 collective-permute-done.2.refs_2_
  15.2 0.0 collective-permute-done.1.refs_1_
  15.2 0.1 collective-permute-done.refs_0_
  15.3 1.7 %direct.1 = bf16[1,4,3,2,1280]{4,3,2,1,0:T(2,128)(2,1)} custom-call(bf16[48,1280]{1,0:T(8,128)(2,1)S(1)} %get-tuple-element.9.after_ref.own_ref, bf16[48,1152]{1,0:T(8,128)(2,1)S(1)} %collective-permute-done.refs_0_, bf16[48,1152]{1,0:T(8,128)(2,1)S(1)} %collective-permute-done.1.refs_1_, bf16[48,1152]{1,0:T(8,128)(2,1)S(1)} %collective-permute-done.2.refs_2_, ...), custom_call_target="tpu_custom_call" | custom-call | tf_op jit(solution)/shard_map/direct/pallas_call | solution.py:428
  (2 shorter events, 0.0 us)
Async XLA Ops:
  2.2 12.9 %collective-permute-start.2 = (bf16[48,1152]{1,0:T(8,128)(2,1)S(1)}, bf16[48,1152]{1,0:T(8,128)(2,1)S(1)}, u32[]{:S(2)}, u32[]{:S(2)}) collective-permute-start(bf16[48,1152]{1,0:T(8,128)(2,1)S(1)} %slice.3), channel_id=1, source_target_pairs={{0,8},{4,12},{8,0},{12,4},{1,9},{5,13},{9,1},{13,5},{2,10},{6,14},... | collective-permute-start | bytes 331784 | tf_op jit(solution)/shard_map/ppermute | solution.py:367
  6.3 8.8 %collective-permute-start.1 = (bf16[48,1152]{1,0:T(8,128)(2,1)S(1)}, bf16[48,1152]{1,0:T(8,128)(2,1)S(1)}, u32[]{:S(2)}, u32[]{:S(2)}) collective-permute-start(bf16[48,1152]{1,0:T(8,128)(2,1)S(1)} %slice.3), channel_id=1, source_target_pairs={{0,4},{4,0},{8,12},{12,8},{1,5},{5,1},{9,13},{13,9},{2,6},{6,2},{1... | collective-permute-start | bytes 331784 | tf_op jit(solution)/shard_map/ppermute | solution.py:367
  7.9 7.4 %collective-permute-start = (bf16[48,1152]{1,0:T(8,128)(2,1)S(1)}, bf16[48,1152]{1,0:T(8,128)(2,1)S(1)}, u32[]{:S(2)}, u32[]{:S(2)}) collective-permute-start(bf16[48,1152]{1,0:T(8,128)(2,1)S(1)} %slice.3), channel_id=1, source_target_pairs={{0,12},{4,8},{8,4},{12,0},{1,13},{5,9},{9,5},{13,1},{2,14},{6,10},... | collective-permute-start | bytes 331784 | tf_op jit(solution)/shard_map/ppermute | solution.py:367
  7.9 1.1 %copy-start.5 = (s32[1280]{0:T(1024)S(1)}, s32[1280]{0:T(1024)}, u32[]{:S(2)}) copy-start(s32[1280]{0:T(1024)} %param.10) | copy-start | bytes 15364
  7.9 1.1 %copy-start = (bf16[1,4,3,2,1280]{4,3,2,1,0:T(2,128)(2,1)S(1)}, bf16[1,4,3,2,1280]{4,3,2,1,0:T(2,128)(2,1)}, u32[]{:S(2)}) copy-start(bf16[1,4,3,2,1280]{4,3,2,1,0:T(2,128)(2,1)} %spectra_ref.3) | copy-start | bytes 184324
  7.9 1.2 %copy-start.1 = (f32[2,1280]{1,0:T(2,128)S(1)}, f32[2,1280]{1,0:T(2,128)}, u32[]{:S(2)}) copy-start(f32[2,1280]{1,0:T(2,128)} %planet_ref.1) | copy-start | bytes 30724
  7.9 1.2 %copy-start.2 = (f32[2,1280]{1,0:T(2,128)S(1)}, f32[2,1280]{1,0:T(2,128)}, u32[]{:S(2)}) copy-start(f32[2,1280]{1,0:T(2,128)} %quad_ref.1) | copy-start | bytes 30724
  8.0 1.2 %copy-start.3 = (s32[4]{0:T(128)S(1)}, s32[4]{0:T(128)}, u32[]{:S(2)}) copy-start(s32[4]{0:T(128)} %assign_ref.3) | copy-start | bytes 52
  8.0 1.2 %copy-start.4 = (f32[4]{0:T(128)S(1)}, f32[4]{0:T(128)}, u32[]{:S(2)}) copy-start(f32[4]{0:T(128)} %thick_ref.1) | copy-start | bytes 52

commit v6 on v5

--- a/solution.py
+++ b/solution.py
@@ -24,19 +24,20 @@
     return lax.axis_index("band") ^ slot if few else slot
 
 
-def inverse_kernel(spacing, chunk, assign_ref, spectra_ref, legendre_ref, fourier_ref, table_ref,
+def inverse_kernel(spacing, chunk, trim, assign_ref, spectra_ref, legendre_ref, head_ref, fourier_ref, table_ref,
                    assign_scr, spectra_scr, rows_scr, acc_scr, sems):
     coeffs = table_ref.shape[0]
     chunks = coeffs // chunk
     heads = [
-        pltpu.make_async_copy(assign_ref, assign_scr, sems.at[chunks]),
-        pltpu.make_async_copy(spectra_ref, spectra_scr, sems.at[chunks + 1]),
+        pltpu.make_async_copy(assign_ref, assign_scr, sems.at[chunks + 1]),
+        pltpu.make_async_copy(spectra_ref, spectra_scr, sems.at[chunks + 2]),
     ]
     for copy in heads:
         copy.start()
+    cuts = list(range(0, coeffs, chunk)) + [coeffs - chunk // 2, coeffs]
     copies = []
-    for i in range(chunks):
-        span = pl.ds(i * chunk, chunk)
+    for i, (first, end) in enumerate(zip(cuts[:-1], cuts[1:])):
+        span = pl.ds(first, end - first)
         copies.append(pltpu.make_async_copy(legendre_ref.at[0, span], table_ref.at[span], sems.at[i]))
         copies[-1].start()
     levels = spectra_ref.shape[1]
@@ -61,16 +62,19 @@
     odd = lax.broadcasted_iota(jnp.int32, (out_rows, coeffs), 1) % 2 == 1
     south = lax.broadcasted_iota(jnp.int32, (out_rows, coeffs), 0) // levels % 2 == 1
     signed = jnp.where(odd & south, -spread, spread).astype(jnp.bfloat16)
+    chunks = len(copies)
     for i in range(chunks):
         copies[i].wait()
-        span = slice(i * chunk, (i + 1) * chunk)
+        span = slice(cuts[i], cuts[i + 1])
         product = jnp.dot(signed[:, span], table_ref[span, :], preferred_element_type=jnp.float32)
         if i == 0:
             acc_scr[...] = product
         elif i < chunks - 1:
             acc_scr[...] += product
         else:
-            fourier_ref[...] = (acc_scr[...] + product).astype(jnp.bfloat16)
+            if trim:
+                head_ref[...] = (acc_scr[:, 0:trim] + product[:, 0:trim]).astype(jnp.bfloat16)
+            fourier_ref[...] = (acc_scr[:, trim:] + product[:, trim:]).astype(jnp.bfloat16)
 
 
 def cos_sin(turns):
@@ -193,7 +197,7 @@
     return (2, 0, 1) if slots == 3 else range(slots)
 
 
-def direct_kernel(waves, few, trim, own_ref, *refs):
+def direct_kernel(waves, few, trim, head_ref, own_ref, *refs):
     count = waves - 1 if few else 1
     slot_refs = [None] * count
     for at, ref in zip(arrival(count), refs):
@@ -218,11 +222,11 @@
                 rows = slice(field * 2 * pair, (field + 1) * 2 * pair)
                 if not few:
                     both = slot_refs[0][k, rows, lanes].astype(jnp.float32)
-                elif k == 0:
-                    both = own_ref[rows, lanes].astype(jnp.float32)
+                elif lane < trim:
+                    both = head_ref[rows, lanes].astype(jnp.float32)
                 else:
-                    there = pl.ds(lane - trim, LANES)
-                    both = slot_refs[k - 1][rows, there].astype(jnp.float32)
+                    ref = slot_refs[k - 1] if k else own_ref
+                    both = ref[rows, pl.ds(lane - trim, LANES)].astype(jnp.float32)
                 fields.append((both[:pair], both[pair:]))
             coefs.append(fields)
         planet = aux_ref[starts["planet"]:starts["planet"] + pair, lanes]
@@ -386,25 +390,26 @@
     def pinned(x, space):
         return pltpu.with_memory_space_constraint(x, space)
 
-    fourier, table = pl.pallas_call(
-        functools.partial(inverse_kernel, spacing, chunk),
+    head, fourier, table = pl.pallas_call(
+        functools.partial(inverse_kernel, spacing, chunk, trim),
         out_shape=(
-            jax.ShapeDtypeStruct((2 * rows, lats), jnp.bfloat16),
+            jax.ShapeDtypeStruct((2 * rows, max(trim, LANES)), jnp.bfloat16),
+            jax.ShapeDtypeStruct((2 * rows, lats - trim), jnp.bfloat16),
             pltpu.VMEM((coeffs, lats), jnp.bfloat16),
         ),
         in_specs=[hbm] * 3,
-        out_specs=(vmem, vmem),
+        out_specs=(vmem, vmem, vmem),
         scratch_shapes=[
             pltpu.SMEM(assignment.shape, jnp.int32),
             pltpu.VMEM(spectra.shape, jnp.bfloat16),
             pltpu.VMEM((rows, coeffs), jnp.float32),
             pltpu.VMEM((2 * rows, lats), jnp.float32),
-            pltpu.SemaphoreType.DMA((chunks + 2,)),
+            pltpu.SemaphoreType.DMA((chunks + 3,)),
         ],
         compiler_params=pltpu.CompilerParams(vmem_limit_bytes=16 << 20),
         name="inverse",
     )(*(pinned(x, pltpu.HBM) for x in (assignment, spectra, legendre)))
-    gathered = gather_slots(waves, few, fourier, fourier[:, trim:])
+    gathered = gather_slots(waves, few, fourier, fourier)
     same = (jnp.arange(chunk)[:, None] == jnp.arange(chunk)[None, :]).astype(jnp.bfloat16)
     turned = jnp.einsum("kbh,ba->kha", table.reshape(chunks, chunk, lats), same,
                         preferred_element_type=jnp.float32).astype(jnp.bfloat16)
@@ -424,7 +429,7 @@
 
     totals = lax.all_gather(total, ("fld", "sub"))
 
-    operands = [fourier] + [gathered[at] for at in arrival(len(gathered))] + [totals, aux, pinned(turned, pltpu.VMEM)]
+    operands = [head, fourier] + [gathered[at] for at in arrival(len(gathered))] + [totals, aux, pinned(turned, pltpu.VMEM)]
     return pl.pallas_call(
         functools.partial(direct_kernel, waves, few, trim),
         out_shape=jax.ShapeDtypeStruct(spectra.shape, jnp.bfloat16),

time: 17.2 us -> 17.2 us (level)
  no operation moved by 1% of the time
where the time goes in v6:
time: 17.2 us; the launch traced here: 17 us
  starting transfers between devices  5.68 us (33%)
  blocking collectives  5.22 us (30%)
  Pallas kernels  4.76 us (28%)
  matrix products  1.07 us (6%)
    ppermute x3, starting transfers between devices, gather_slots(): lax.ppermute(sent, 'band', [(i, i ^ k) for i in range(waves)])  5.68 us
    all_gather x1, blocking collectives, on_device(): totals = lax.all_gather(total, ('fld', 'sub'))  5.22 us
    pallas_call x1, Pallas kernels, on_device(): pl.pallas_call(functools.partial(inverse_kernel, spacing, chunk, trim), o...  2.17 us
    pallas_call x1, Pallas kernels, on_device(): pl.pallas_call(functools.partial(direct_kernel, waves, few, trim), out_sh...  1.76 us
    dot_general x1, matrix products, on_device(): jnp.einsum('kbh,ba->kha', table.reshape(chunks, chunk, lats), same, prefe...  1.07 us
    pallas_call x1, Pallas kernels, on_device(): pl.pallas_call(functools.partial(aux_kernel, waves, few, spacing), out_sh...  0.82 us
  transfers between devices with their start and end apart: 3, of which 1 were waited for; matrix products, arithmetic and copies ran while one was open for 6% of the time, Pallas kernels for 5%

profile of v6, /device:TPU:0, one launch (start us, length us, event | category | flops | bytes accessed | tf_op | source)
XLA Modules:
  0.0 17.0 jit_solution(13571529806002138847)
XLA Ops:
  0.0 2.2 %inverse.1 = (bf16[48,128]{1,0:T(8,128)(2,1)S(1)}, bf16[48,1152]{1,0:T(8,128)(2,1)S(1)}, bf16[1280,1280]{1,0:T(8,128)(2,1)S(1)}) custom-call(s32[4]{0:T(128)} %assign_ref.3, bf16[1,4,3,2,1280]{4,3,2,1,0:T(2,128)(2,1)} %spectra_ref.3, bf16[1,1280,1280]{2,1,0:T(8,128)(2,1)} %legendre_ref.1), custom_call_target="tpu_custom_call" | custom-call | tf_op jit(solution)/shard_map/inverse/pallas_call | solution.py:393
  2.2 4.1 %collective-permute-start.2 = (bf16[48,1152]{1,0:T(8,128)(2,1)S(1)}, bf16[48,1152]{1,0:T(8,128)(2,1)S(1)}, u32[]{:S(2)}, u32[]{:S(2)}) collective-permute-start(bf16[48,1152]{1,0:T(8,128)(2,1)S(1)} %get-tuple-element.11.after_ref.own_ref), channel_id=1, source_target_pairs={{0,8},{4,12},{8,0},{12,4},{1,9},{5,13},{9,1},{13,5},{2,10},{6,14},... | collective-permute-start | bytes 331784 | tf_op jit(solution)/shard_map/ppermute | solution.py:371
  6.3 1.6 %collective-permute-start.1 = (bf16[48,1152]{1,0:T(8,128)(2,1)S(1)}, bf16[48,1152]{1,0:T(8,128)(2,1)S(1)}, u32[]{:S(2)}, u32[]{:S(2)}) collective-permute-start(bf16[48,1152]{1,0:T(8,128)(2,1)S(1)} %get-tuple-element.11.after_ref.own_ref), channel_id=1, source_target_pairs={{0,4},{4,0},{8,12},{12,8},{1,5},{5,1},{9,13},{13,9},{2,6},{6,2},{1... | collective-permute-start | bytes 331784 | tf_op jit(solution)/shard_map/ppermute | solution.py:371
  7.9 0.0 collective-permute-start
  7.9 0.0 copy-start.5
  7.9 0.0 copy-start
  7.9 0.0 copy-start.1
  7.9 0.0 copy-start.2
  7.9 0.0 copy-start.3
  7.9 0.0 copy-start.4
  7.9 1.1 %convolution_convert_fusion.refs_5_ = bf16[5,1280,256]{2,1,0:T(8,128)(2,1)S(1)} fusion(bf16[5,256,1280]{2,1,0:T(8,128)(2,1)S(1)} %bitcast.6), kind=kOutput, calls=%fused_computation | convolution fusion | flops 840564736 | bytes 6553600 | tf_op jit(solution)/shard_map/kbh,ba->kha/dot_general | solution.py:414
  9.0 0.0 copy-done.5
  9.0 0.0 copy-done
  9.0 0.0 copy-done.1
  9.0 0.0 copy-done.2
  9.0 0.0 copy-done.3
  9.1 0.0 copy-done.4
  9.1 0.8 %tables.1 = (f32[120,1280]{1,0:T(8,128)S(1)}, f32[2,1280]{1,0:T(2,128)S(1)}) custom-call(s32[4]{0:T(128)S(1)} %copy-done.3, f32[4]{0:T(128)S(1)} %copy-done.4, s32[1,1280]{1,0:T(1,128)S(1)} %reshape.6.counts_ref, f32[2,1280]{1,0:T(2,128)S(1)} %copy-done.1, f32[2,1280]{1,0:T(2,128)S(1)} %copy-done.2, bf16[1,4,3,2,1280]{4,3,2,1,0:T(2,128)(2,1)S(1)} %copy-done, ...), custom_call_target="tpu_custom_call" | custom-call | tf_op jit(solution)/shard_map/tables/pallas_call | solution.py:418
  9.9 5.2 %all-gather.1.refs_3_ = f32[4,2,1280]{2,1,0:T(2,128)S(1)} all-gather(f32[1,2,1280]{2,1,0:T(2,128)S(1)} %bitcast.7), channel_id=2, replica_groups=mesh['member'=2,'band'=4,'fld'=2,'sub'=2] {'fld','sub'}, dimensions={0}, use_global_device_ids=true | all-gather | bytes 51200 | tf_op jit(solution)/shard_map/all_gather | solution.py:430
  15.1 0.0 collective-permute-done.2.refs_2_
  15.1 0.0 collective-permute-done.1.refs_1_
  15.1 0.1 collective-permute-done.refs_0_
  15.2 1.8 %direct.1 = bf16[1,4,3,2,1280]{4,3,2,1,0:T(2,128)(2,1)} custom-call(bf16[48,128]{1,0:T(8,128)(2,1)S(1)} %get-tuple-element.10.head_ref, bf16[48,1152]{1,0:T(8,128)(2,1)S(1)} %get-tuple-element.11.after_ref.own_ref, bf16[48,1152]{1,0:T(8,128)(2,1)S(1)} %collective-permute-done.refs_0_, bf16[48,1152]{1,0:T(8,128)(2,1)S(1)} %collective-permute-done.1.refs_1_, ...), custom_call_target="tpu_custom_call" | custom-call | tf_op jit(solution)/shard_map/direct/pallas_call | solution.py:433
  (1 shorter events, 0.0 us)
Async XLA Ops:
  2.2 12.9 %collective-permute-start.2 = (bf16[48,1152]{1,0:T(8,128)(2,1)S(1)}, bf16[48,1152]{1,0:T(8,128)(2,1)S(1)}, u32[]{:S(2)}, u32[]{:S(2)}) collective-permute-start(bf16[48,1152]{1,0:T(8,128)(2,1)S(1)} %get-tuple-element.11.after_ref.own_ref), channel_id=1, source_target_pairs={{0,8},{4,12},{8,0},{12,4},{1,9},{5,13},{9,1},{13,5},{2,10},{6,14},... | collective-permute-start | bytes 331784 | tf_op jit(solution)/shard_map/ppermute | solution.py:371
  6.3 8.8 %collective-permute-start.1 = (bf16[48,1152]{1,0:T(8,128)(2,1)S(1)}, bf16[48,1152]{1,0:T(8,128)(2,1)S(1)}, u32[]{:S(2)}, u32[]{:S(2)}) collective-permute-start(bf16[48,1152]{1,0:T(8,128)(2,1)S(1)} %get-tuple-element.11.after_ref.own_ref), channel_id=1, source_target_pairs={{0,4},{4,0},{8,12},{12,8},{1,5},{5,1},{9,13},{13,9},{2,6},{6,2},{1... | collective-permute-start | bytes 331784 | tf_op jit(solution)/shard_map/ppermute | solution.py:371
  7.9 7.4 %collective-permute-start = (bf16[48,1152]{1,0:T(8,128)(2,1)S(1)}, bf16[48,1152]{1,0:T(8,128)(2,1)S(1)}, u32[]{:S(2)}, u32[]{:S(2)}) collective-permute-start(bf16[48,1152]{1,0:T(8,128)(2,1)S(1)} %get-tuple-element.11.after_ref.own_ref), channel_id=1, source_target_pairs={{0,12},{4,8},{8,4},{12,0},{1,13},{5,9},{9,5},{13,1},{2,14},{6,10},... | collective-permute-start | bytes 331784 | tf_op jit(solution)/shard_map/ppermute | solution.py:371
  7.9 1.1 %copy-start.5 = (s32[1280]{0:T(1024)S(1)}, s32[1280]{0:T(1024)}, u32[]{:S(2)}) copy-start(s32[1280]{0:T(1024)} %param.10) | copy-start | bytes 15364
  7.9 1.1 %copy-start = (bf16[1,4,3,2,1280]{4,3,2,1,0:T(2,128)(2,1)S(1)}, bf16[1,4,3,2,1280]{4,3,2,1,0:T(2,128)(2,1)}, u32[]{:S(2)}) copy-start(bf16[1,4,3,2,1280]{4,3,2,1,0:T(2,128)(2,1)} %spectra_ref.3) | copy-start | bytes 184324
  7.9 1.2 %copy-start.1 = (f32[2,1280]{1,0:T(2,128)S(1)}, f32[2,1280]{1,0:T(2,128)}, u32[]{:S(2)}) copy-start(f32[2,1280]{1,0:T(2,128)} %planet_ref.1) | copy-start | bytes 30724
  7.9 1.2 %copy-start.2 = (f32[2,1280]{1,0:T(2,128)S(1)}, f32[2,1280]{1,0:T(2,128)}, u32[]{:S(2)}) copy-start(f32[2,1280]{1,0:T(2,128)} %quad_ref.1) | copy-start | bytes 30724
  7.9 1.2 %copy-start.3 = (s32[4]{0:T(128)S(1)}, s32[4]{0:T(128)}, u32[]{:S(2)}) copy-start(s32[4]{0:T(128)} %assign_ref.3) | copy-start | bytes 52
  7.9 1.2 %copy-start.4 = (f32[4]{0:T(128)S(1)}, f32[4]{0:T(128)}, u32[]{:S(2)}) copy-start(f32[4]{0:T(128)} %thick_ref.1) | copy-start | bytes 52

commit v7 on v6

--- a/solution.py
+++ b/solution.py
@@ -313,7 +313,9 @@
         for first in range(0, lats, step):
             for lane in range(first, first + step, LANES):
                 products(lane, waves if lane >= trim else 1)
-            share(first, step)
+                if first > 0 and lane == first:
+                    share(first - step, step)
+        share(lats - step, step)
     else:
         def lat_block(block, carry):
             products(pl.multiple_of(block * LANES, LANES), waves)

time: 17.2 us -> 17.2 us (level)
  no operation moved by 1% of the time
where the time goes in v7:
time: 17.2 us; the launch traced here: 17 us
  starting transfers between devices  5.68 us (33%)
  blocking collectives  5.22 us (30%)
  Pallas kernels  4.76 us (28%)
  matrix products  1.07 us (6%)
    ppermute x3, starting transfers between devices, gather_slots(): lax.ppermute(sent, 'band', [(i, i ^ k) for i in range(waves)])  5.68 us
    all_gather x1, blocking collectives, on_device(): totals = lax.all_gather(total, ('fld', 'sub'))  5.22 us
    pallas_call x1, Pallas kernels, on_device(): pl.pallas_call(functools.partial(inverse_kernel, spacing, chunk, trim), o...  2.17 us
    pallas_call x1, Pallas kernels, on_device(): pl.pallas_call(functools.partial(direct_kernel, waves, few, trim), out_sh...  1.76 us
    dot_general x1, matrix products, on_device(): jnp.einsum('kbh,ba->kha', table.reshape(chunks, chunk, lats), same, prefe...  1.07 us
    pallas_call x1, Pallas kernels, on_device(): pl.pallas_call(functools.partial(aux_kernel, waves, few, spacing), out_sh...  0.82 us
  transfers between devices with their start and end apart: 3, of which 1 were waited for; matrix products, arithmetic and copies ran while one was open for 6% of the time, Pallas kernels for 5%

profile of v7, /device:TPU:0, one launch (start us, length us, event | category | flops | bytes accessed | tf_op | source)
XLA Modules:
  0.0 17.0 jit_solution(13571529806002138847)
XLA Ops:
  0.0 2.2 %inverse.1 = (bf16[48,128]{1,0:T(8,128)(2,1)S(1)}, bf16[48,1152]{1,0:T(8,128)(2,1)S(1)}, bf16[1280,1280]{1,0:T(8,128)(2,1)S(1)}) custom-call(s32[4]{0:T(128)} %assign_ref.3, bf16[1,4,3,2,1280]{4,3,2,1,0:T(2,128)(2,1)} %spectra_ref.3, bf16[1,1280,1280]{2,1,0:T(8,128)(2,1)} %legendre_ref.1), custom_call_target="tpu_custom_call" | custom-call | tf_op jit(solution)/shard_map/inverse/pallas_call | solution.py:395
  2.2 4.1 %collective-permute-start.2 = (bf16[48,1152]{1,0:T(8,128)(2,1)S(1)}, bf16[48,1152]{1,0:T(8,128)(2,1)S(1)}, u32[]{:S(2)}, u32[]{:S(2)}) collective-permute-start(bf16[48,1152]{1,0:T(8,128)(2,1)S(1)} %get-tuple-element.11.after_ref.own_ref), channel_id=1, source_target_pairs={{0,8},{4,12},{8,0},{12,4},{1,9},{5,13},{9,1},{13,5},{2,10},{6,14},... | collective-permute-start | bytes 331784 | tf_op jit(solution)/shard_map/ppermute | solution.py:373
  6.3 1.6 %collective-permute-start.1 = (bf16[48,1152]{1,0:T(8,128)(2,1)S(1)}, bf16[48,1152]{1,0:T(8,128)(2,1)S(1)}, u32[]{:S(2)}, u32[]{:S(2)}) collective-permute-start(bf16[48,1152]{1,0:T(8,128)(2,1)S(1)} %get-tuple-element.11.after_ref.own_ref), channel_id=1, source_target_pairs={{0,4},{4,0},{8,12},{12,8},{1,5},{5,1},{9,13},{13,9},{2,6},{6,2},{1... | collective-permute-start | bytes 331784 | tf_op jit(solution)/shard_map/ppermute | solution.py:373
  7.9 0.0 collective-permute-start
  7.9 0.0 copy-start.5
  7.9 0.0 copy-start
  7.9 0.0 copy-start.1
  7.9 0.0 copy-start.2
  7.9 0.0 copy-start.3
  7.9 0.0 copy-start.4
  7.9 1.1 %convolution_convert_fusion.refs_5_ = bf16[5,1280,256]{2,1,0:T(8,128)(2,1)S(1)} fusion(bf16[5,256,1280]{2,1,0:T(8,128)(2,1)S(1)} %bitcast.6), kind=kOutput, calls=%fused_computation | convolution fusion | flops 840564736 | bytes 6553600 | tf_op jit(solution)/shard_map/kbh,ba->kha/dot_general | solution.py:416
  9.0 0.0 copy-done.5
  9.0 0.0 copy-done
  9.0 0.0 copy-done.1
  9.0 0.0 copy-done.2
  9.0 0.0 copy-done.3
  9.1 0.0 copy-done.4
  9.1 0.8 %tables.1 = (f32[120,1280]{1,0:T(8,128)S(1)}, f32[2,1280]{1,0:T(2,128)S(1)}) custom-call(s32[4]{0:T(128)S(1)} %copy-done.3, f32[4]{0:T(128)S(1)} %copy-done.4, s32[1,1280]{1,0:T(1,128)S(1)} %reshape.6.counts_ref, f32[2,1280]{1,0:T(2,128)S(1)} %copy-done.1, f32[2,1280]{1,0:T(2,128)S(1)} %copy-done.2, bf16[1,4,3,2,1280]{4,3,2,1,0:T(2,128)(2,1)S(1)} %copy-done, ...), custom_call_target="tpu_custom_call" | custom-call | tf_op jit(solution)/shard_map/tables/pallas_call | solution.py:420
  9.9 5.2 %all-gather.1.refs_3_ = f32[4,2,1280]{2,1,0:T(2,128)S(1)} all-gather(f32[1,2,1280]{2,1,0:T(2,128)S(1)} %bitcast.7), channel_id=2, replica_groups=mesh['member'=2,'band'=4,'fld'=2,'sub'=2] {'fld','sub'}, dimensions={0}, use_global_device_ids=true | all-gather | bytes 51200 | tf_op jit(solution)/shard_map/all_gather | solution.py:432
  15.1 0.0 collective-permute-done.2.refs_2_
  15.1 0.0 collective-permute-done.1.refs_1_
  15.1 0.1 collective-permute-done.refs_0_
  15.2 1.8 %direct.1 = bf16[1,4,3,2,1280]{4,3,2,1,0:T(2,128)(2,1)} custom-call(bf16[48,128]{1,0:T(8,128)(2,1)S(1)} %get-tuple-element.10.head_ref, bf16[48,1152]{1,0:T(8,128)(2,1)S(1)} %get-tuple-element.11.after_ref.own_ref, bf16[48,1152]{1,0:T(8,128)(2,1)S(1)} %collective-permute-done.refs_0_, bf16[48,1152]{1,0:T(8,128)(2,1)S(1)} %collective-permute-done.1.refs_1_, ...), custom_call_target="tpu_custom_call" | custom-call | tf_op jit(solution)/shard_map/direct/pallas_call | solution.py:435
  (1 shorter events, 0.0 us)
Async XLA Ops:
  2.2 12.9 %collective-permute-start.2 = (bf16[48,1152]{1,0:T(8,128)(2,1)S(1)}, bf16[48,1152]{1,0:T(8,128)(2,1)S(1)}, u32[]{:S(2)}, u32[]{:S(2)}) collective-permute-start(bf16[48,1152]{1,0:T(8,128)(2,1)S(1)} %get-tuple-element.11.after_ref.own_ref), channel_id=1, source_target_pairs={{0,8},{4,12},{8,0},{12,4},{1,9},{5,13},{9,1},{13,5},{2,10},{6,14},... | collective-permute-start | bytes 331784 | tf_op jit(solution)/shard_map/ppermute | solution.py:373
  6.3 8.8 %collective-permute-start.1 = (bf16[48,1152]{1,0:T(8,128)(2,1)S(1)}, bf16[48,1152]{1,0:T(8,128)(2,1)S(1)}, u32[]{:S(2)}, u32[]{:S(2)}) collective-permute-start(bf16[48,1152]{1,0:T(8,128)(2,1)S(1)} %get-tuple-element.11.after_ref.own_ref), channel_id=1, source_target_pairs={{0,4},{4,0},{8,12},{12,8},{1,5},{5,1},{9,13},{13,9},{2,6},{6,2},{1... | collective-permute-start | bytes 331784 | tf_op jit(solution)/shard_map/ppermute | solution.py:373
  7.9 7.4 %collective-permute-start = (bf16[48,1152]{1,0:T(8,128)(2,1)S(1)}, bf16[48,1152]{1,0:T(8,128)(2,1)S(1)}, u32[]{:S(2)}, u32[]{:S(2)}) collective-permute-start(bf16[48,1152]{1,0:T(8,128)(2,1)S(1)} %get-tuple-element.11.after_ref.own_ref), channel_id=1, source_target_pairs={{0,12},{4,8},{8,4},{12,0},{1,13},{5,9},{9,5},{13,1},{2,14},{6,10},... | collective-permute-start | bytes 331784 | tf_op jit(solution)/shard_map/ppermute | solution.py:373
  7.9 1.1 %copy-start.5 = (s32[1280]{0:T(1024)S(1)}, s32[1280]{0:T(1024)}, u32[]{:S(2)}) copy-start(s32[1280]{0:T(1024)} %param.10) | copy-start | bytes 15364
  7.9 1.1 %copy-start = (bf16[1,4,3,2,1280]{4,3,2,1,0:T(2,128)(2,1)S(1)}, bf16[1,4,3,2,1280]{4,3,2,1,0:T(2,128)(2,1)}, u32[]{:S(2)}) copy-start(bf16[1,4,3,2,1280]{4,3,2,1,0:T(2,128)(2,1)} %spectra_ref.3) | copy-start | bytes 184324
  7.9 1.2 %copy-start.1 = (f32[2,1280]{1,0:T(2,128)S(1)}, f32[2,1280]{1,0:T(2,128)}, u32[]{:S(2)}) copy-start(f32[2,1280]{1,0:T(2,128)} %planet_ref.1) | copy-start | bytes 30724
  7.9 1.2 %copy-start.2 = (f32[2,1280]{1,0:T(2,128)S(1)}, f32[2,1280]{1,0:T(2,128)}, u32[]{:S(2)}) copy-start(f32[2,1280]{1,0:T(2,128)} %quad_ref.1) | copy-start | bytes 30724
  7.9 1.2 %copy-start.3 = (s32[4]{0:T(128)S(1)}, s32[4]{0:T(128)}, u32[]{:S(2)}) copy-start(s32[4]{0:T(128)} %assign_ref.3) | copy-start | bytes 52
  7.9 1.2 %copy-start.4 = (f32[4]{0:T(128)S(1)}, f32[4]{0:T(128)}, u32[]{:S(2)}) copy-start(f32[4]{0:T(128)} %thick_ref.1) | copy-start | bytes 52

commit v8 on v6

--- a/solution.py
+++ b/solution.py
@@ -406,7 +406,7 @@
             pltpu.VMEM((2 * rows, lats), jnp.float32),
             pltpu.SemaphoreType.DMA((chunks + 3,)),
         ],
-        compiler_params=pltpu.CompilerParams(vmem_limit_bytes=16 << 20),
+        compiler_params=pltpu.CompilerParams(vmem_limit_bytes=8 << 20),
         name="inverse",
     )(*(pinned(x, pltpu.HBM) for x in (assignment, spectra, legendre)))
     gathered = gather_slots(waves, few, fourier, fourier)
@@ -423,7 +423,7 @@
         ),
         in_specs=[smem, smem, vmem, vmem, vmem, vmem, anywhere],
         out_specs=(vmem, vmem),
-        compiler_params=pltpu.CompilerParams(vmem_limit_bytes=(16 if few else 48) << 20),
+        compiler_params=pltpu.CompilerParams(vmem_limit_bytes=(8 if few else 48) << 20),
         name="tables",
     )(assignment, thickness, circle_longitudes.reshape(1, lats), coriolis, weights, spectra, fourier)
 
@@ -442,7 +442,7 @@
             pltpu.VMEM(total.shape, jnp.float32),
             pltpu.SemaphoreType.DMA((chunks,)),
         ],
-        compiler_params=pltpu.CompilerParams(vmem_limit_bytes=(24 if few else 56) << 20),
+        compiler_params=pltpu.CompilerParams(vmem_limit_bytes=(8 if few else 56) << 20),
         name="direct",
     )(*operands)
 

time: 17.2 us -> 17.2 us (level)
  no operation moved by 1% of the time
where the time goes in v8:
time: 17.2 us; the launch traced here: 17 us
  starting transfers between devices  5.68 us (33%)
  blocking collectives  5.22 us (30%)
  Pallas kernels  4.79 us (28%)
  matrix products  1.07 us (6%)
    ppermute x3, starting transfers between devices, gather_slots(): lax.ppermute(sent, 'band', [(i, i ^ k) for i in range(waves)])  5.68 us
    all_gather x1, blocking collectives, on_device(): totals = lax.all_gather(total, ('fld', 'sub'))  5.22 us
    pallas_call x1, Pallas kernels, on_device(): pl.pallas_call(functools.partial(inverse_kernel, spacing, chunk, trim), o...  2.17 us
    pallas_call x1, Pallas kernels, on_device(): pl.pallas_call(functools.partial(direct_kernel, waves, few, trim), out_sh...  1.8 us
    dot_general x1, matrix products, on_device(): jnp.einsum('kbh,ba->kha', table.reshape(chunks, chunk, lats), same, prefe...  1.07 us
    pallas_call x1, Pallas kernels, on_device(): pl.pallas_call(functools.partial(aux_kernel, waves, few, spacing), out_sh...  0.82 us
  transfers between devices with their start and end apart: 3, of which 1 were waited for; matrix products, arithmetic and copies ran while one was open for 6% of the time, Pallas kernels for 5%

profile of v8, /device:TPU:0, one launch (start us, length us, event | category | flops | bytes accessed | tf_op | source)
XLA Modules:
  0.0 17.0 jit_solution(11259417510535383577)
XLA Ops:
  0.0 2.2 %inverse.1 = (bf16[48,128]{1,0:T(8,128)(2,1)S(1)}, bf16[48,1152]{1,0:T(8,128)(2,1)S(1)}, bf16[1280,1280]{1,0:T(8,128)(2,1)S(1)}) custom-call(s32[4]{0:T(128)} %assign_ref.3, bf16[1,4,3,2,1280]{4,3,2,1,0:T(2,128)(2,1)} %spectra_ref.3, bf16[1,1280,1280]{2,1,0:T(8,128)(2,1)} %legendre_ref.1), custom_call_target="tpu_custom_call" | custom-call | tf_op jit(solution)/shard_map/inverse/pallas_call | solution.py:393
  2.2 4.1 %collective-permute-start.2 = (bf16[48,1152]{1,0:T(8,128)(2,1)S(1)}, bf16[48,1152]{1,0:T(8,128)(2,1)S(1)}, u32[]{:S(2)}, u32[]{:S(2)}) collective-permute-start(bf16[48,1152]{1,0:T(8,128)(2,1)S(1)} %get-tuple-element.11.after_ref.own_ref), channel_id=1, source_target_pairs={{0,8},{4,12},{8,0},{12,4},{1,9},{5,13},{9,1},{13,5},{2,10},{6,14},... | collective-permute-start | bytes 331784 | tf_op jit(solution)/shard_map/ppermute | solution.py:371
  6.3 1.6 %collective-permute-start.1 = (bf16[48,1152]{1,0:T(8,128)(2,1)S(1)}, bf16[48,1152]{1,0:T(8,128)(2,1)S(1)}, u32[]{:S(2)}, u32[]{:S(2)}) collective-permute-start(bf16[48,1152]{1,0:T(8,128)(2,1)S(1)} %get-tuple-element.11.after_ref.own_ref), channel_id=1, source_target_pairs={{0,4},{4,0},{8,12},{12,8},{1,5},{5,1},{9,13},{13,9},{2,6},{6,2},{1... | collective-permute-start | bytes 331784 | tf_op jit(solution)/shard_map/ppermute | solution.py:371
  7.9 0.0 collective-permute-start
  7.9 0.0 copy-start.5
  7.9 0.0 copy-start
  7.9 0.0 copy-start.1
  7.9 0.0 copy-start.2
  7.9 0.0 copy-start.3
  7.9 0.0 copy-start.4
  7.9 1.1 %convolution_convert_fusion.refs_5_ = bf16[5,1280,256]{2,1,0:T(8,128)(2,1)S(1)} fusion(bf16[5,256,1280]{2,1,0:T(8,128)(2,1)S(1)} %bitcast.6), kind=kOutput, calls=%fused_computation | convolution fusion | flops 840564736 | bytes 6553600 | tf_op jit(solution)/shard_map/kbh,ba->kha/dot_general | solution.py:414
  9.0 0.0 copy-done.5
  9.0 0.0 copy-done
  9.0 0.0 copy-done.1
  9.0 0.0 copy-done.2
  9.0 0.0 copy-done.3
  9.1 0.0 copy-done.4
  9.1 0.8 %tables.1 = (f32[120,1280]{1,0:T(8,128)S(1)}, f32[2,1280]{1,0:T(2,128)S(1)}) custom-call(s32[4]{0:T(128)S(1)} %copy-done.3, f32[4]{0:T(128)S(1)} %copy-done.4, s32[1,1280]{1,0:T(1,128)S(1)} %reshape.6.counts_ref, f32[2,1280]{1,0:T(2,128)S(1)} %copy-done.1, f32[2,1280]{1,0:T(2,128)S(1)} %copy-done.2, bf16[1,4,3,2,1280]{4,3,2,1,0:T(2,128)(2,1)S(1)} %copy-done, ...), custom_call_target="tpu_custom_call" | custom-call | tf_op jit(solution)/shard_map/tables/pallas_call | solution.py:418
  9.9 5.2 %all-gather.1.refs_3_ = f32[4,2,1280]{2,1,0:T(2,128)S(1)} all-gather(f32[1,2,1280]{2,1,0:T(2,128)S(1)} %bitcast.7), channel_id=2, replica_groups=mesh['member'=2,'band'=4,'fld'=2,'sub'=2] {'fld','sub'}, dimensions={0}, use_global_device_ids=true | all-gather | bytes 51200 | tf_op jit(solution)/shard_map/all_gather | solution.py:430
  15.1 0.0 collective-permute-done.2.refs_2_
  15.1 0.0 collective-permute-done.1.refs_1_
  15.1 0.1 collective-permute-done.refs_0_
  15.2 1.8 %direct.1 = bf16[1,4,3,2,1280]{4,3,2,1,0:T(2,128)(2,1)} custom-call(bf16[48,128]{1,0:T(8,128)(2,1)S(1)} %get-tuple-element.10.head_ref, bf16[48,1152]{1,0:T(8,128)(2,1)S(1)} %get-tuple-element.11.after_ref.own_ref, bf16[48,1152]{1,0:T(8,128)(2,1)S(1)} %collective-permute-done.refs_0_, bf16[48,1152]{1,0:T(8,128)(2,1)S(1)} %collective-permute-done.1.refs_1_, ...), custom_call_target="tpu_custom_call" | custom-call | tf_op jit(solution)/shard_map/direct/pallas_call | solution.py:433
  (1 shorter events, 0.0 us)
Async XLA Ops:
  2.2 12.9 %collective-permute-start.2 = (bf16[48,1152]{1,0:T(8,128)(2,1)S(1)}, bf16[48,1152]{1,0:T(8,128)(2,1)S(1)}, u32[]{:S(2)}, u32[]{:S(2)}) collective-permute-start(bf16[48,1152]{1,0:T(8,128)(2,1)S(1)} %get-tuple-element.11.after_ref.own_ref), channel_id=1, source_target_pairs={{0,8},{4,12},{8,0},{12,4},{1,9},{5,13},{9,1},{13,5},{2,10},{6,14},... | collective-permute-start | bytes 331784 | tf_op jit(solution)/shard_map/ppermute | solution.py:371
  6.3 8.8 %collective-permute-start.1 = (bf16[48,1152]{1,0:T(8,128)(2,1)S(1)}, bf16[48,1152]{1,0:T(8,128)(2,1)S(1)}, u32[]{:S(2)}, u32[]{:S(2)}) collective-permute-start(bf16[48,1152]{1,0:T(8,128)(2,1)S(1)} %get-tuple-element.11.after_ref.own_ref), channel_id=1, source_target_pairs={{0,4},{4,0},{8,12},{12,8},{1,5},{5,1},{9,13},{13,9},{2,6},{6,2},{1... | collective-permute-start | bytes 331784 | tf_op jit(solution)/shard_map/ppermute | solution.py:371
  7.9 7.4 %collective-permute-start = (bf16[48,1152]{1,0:T(8,128)(2,1)S(1)}, bf16[48,1152]{1,0:T(8,128)(2,1)S(1)}, u32[]{:S(2)}, u32[]{:S(2)}) collective-permute-start(bf16[48,1152]{1,0:T(8,128)(2,1)S(1)} %get-tuple-element.11.after_ref.own_ref), channel_id=1, source_target_pairs={{0,12},{4,8},{8,4},{12,0},{1,13},{5,9},{9,5},{13,1},{2,14},{6,10},... | collective-permute-start | bytes 331784 | tf_op jit(solution)/shard_map/ppermute | solution.py:371
  7.9 1.1 %copy-start.5 = (s32[1280]{0:T(1024)S(1)}, s32[1280]{0:T(1024)}, u32[]{:S(2)}) copy-start(s32[1280]{0:T(1024)} %param.10) | copy-start | bytes 15364
  7.9 1.1 %copy-start = (bf16[1,4,3,2,1280]{4,3,2,1,0:T(2,128)(2,1)S(1)}, bf16[1,4,3,2,1280]{4,3,2,1,0:T(2,128)(2,1)}, u32[]{:S(2)}) copy-start(bf16[1,4,3,2,1280]{4,3,2,1,0:T(2,128)(2,1)} %spectra_ref.3) | copy-start | bytes 184324
  7.9 1.2 %copy-start.1 = (f32[2,1280]{1,0:T(2,128)S(1)}, f32[2,1280]{1,0:T(2,128)}, u32[]{:S(2)}) copy-start(f32[2,1280]{1,0:T(2,128)} %planet_ref.1) | copy-start | bytes 30724
  7.9 1.2 %copy-start.2 = (f32[2,1280]{1,0:T(2,128)S(1)}, f32[2,1280]{1,0:T(2,128)}, u32[]{:S(2)}) copy-start(f32[2,1280]{1,0:T(2,128)} %quad_ref.1) | copy-start | bytes 30724
  7.9 1.2 %copy-start.3 = (s32[4]{0:T(128)S(1)}, s32[4]{0:T(128)}, u32[]{:S(2)}) copy-start(s32[4]{0:T(128)} %assign_ref.3) | copy-start | bytes 52
  7.9 1.2 %copy-start.4 = (f32[4]{0:T(128)S(1)}, f32[4]{0:T(128)}, u32[]{:S(2)}) copy-start(f32[4]{0:T(128)} %thick_ref.1) | copy-start | bytes 52
